TPU v7x, 32 devices: a whole 2x2x4 slice. The times are simulated.
32 devices in a mesh: ctx: 8 (over z, x), fsdp: 4 (over y, core).
Axes of the slice: x: 2, y: 2, z: 4, core: 2. Of those that a mesh axis runs over, the one named last changes fastest.
Arguments:
- inputs: bfloat16 [1024, 8192], P('ctx', 'fsdp'), may hold values from -6 to 6
- upstream: bfloat16 [1024, 8192], P('ctx', 'fsdp'), may hold values from -6 to 6
- medium_filter: bfloat16 [512, 128], P('fsdp'), may hold values from -0.5 to 0.5
- short_filter: bfloat16 [512, 7], P('fsdp'), may hold values from -2 to 2
Outputs:
- input_gradient: bfloat16 [1024, 8192], P('ctx', 'fsdp')
- medium_gradient: float32 [512, 128], P('fsdp')
- short_gradient: float32 [512, 7], P('fsdp')
All inputs are finite; a program needn't handle non-finite values.
Results may differ from a plain program's by a relative error of at most 0.005.
Values may be sent and summed in bfloat16 or wider, within the bound.
No kernel may reach another device: no remote copies, remote signals or barrier semaphores. Data moves between devices by JAX's collectives and lax.ppermute only.
A program may use at most 128 MiB of HBM per device.

v0:
```python
import math

import jax
import jax.numpy as jnp
import numpy as np
from jax import lax
from jax.sharding import PartitionSpec as P

GROUP = 16


def shifted(block, axis, distance):
    devices = range(lax.axis_size(axis))
    route = [(i - distance, i) for i in devices if i - distance in devices]
    return lax.ppermute(block, axis, route)


def band_tables(medium_filter, block_rows, band_count):
    tap_count = medium_filter.shape[1]
    offsets = (
        np.arange(band_count)[:, None, None] * block_rows
        + np.arange(block_rows)[None, :, None]
        - np.arange(block_rows)[None, None, :]
    )
    inside = (offsets >= 0) & (offsets < tap_count)
    indices = np.clip(offsets, 0, tap_count - 1).reshape(-1)
    picked = jnp.take(medium_filter, jnp.asarray(indices, dtype=jnp.int32), axis=1)
    picked = picked.reshape(medium_filter.shape[0], band_count, block_rows, block_rows)
    return jnp.where(jnp.asarray(inside)[None], picked, jnp.zeros((), medium_filter.dtype))


def blocked(source_t, block_rows):
    return source_t.reshape(
        source_t.shape[0] // GROUP, GROUP, source_t.shape[1] // block_rows, block_rows
    )


def causal_conv(source_t, bands, block_rows, band_count, number):
    pieces = blocked(source_t, block_rows)
    top = band_count - 1
    total = None
    for band_index in range(band_count):
        part = pieces[:, :, top - band_index : top - band_index + number]
        term = jnp.einsum(
            "gcks,gts->gckt", part, bands[:, band_index], preferred_element_type=jnp.float32
        )
        total = term if total is None else total + term
    return total.reshape(source_t.shape[0], number * block_rows)


def later_conv(source_t, bands, block_rows, band_count, number):
    pieces = blocked(source_t, block_rows)
    total = None
    for band_index in range(band_count):
        part = pieces[:, :, band_index : band_index + number]
        term = jnp.einsum(
            "gcks,gst->gckt", part, bands[:, band_index], preferred_element_type=jnp.float32
        )
        total = term if total is None else total + term
    return total.reshape(source_t.shape[0], number * block_rows)


def short_apply(source_t, short_channel, lead_rows, number):
    total = jnp.zeros((source_t.shape[0], number), jnp.float32)
    for tap_index in range(short_channel.shape[1]):
        window = source_t[:, lead_rows - tap_index : lead_rows - tap_index + number]
        total = total + short_channel[:, tap_index][:, None] * window.astype(jnp.float32)
    return total


def diagonal_sums(pair_sums, tap_count):
    group_count, band_count, block_rows = (
        pair_sums.shape[0],
        pair_sums.shape[1],
        pair_sums.shape[2],
    )
    widened = jnp.pad(pair_sums, ((0, 0), (0, 0), (0, 0), (block_rows, 0)))
    flattened = widened.reshape(group_count, band_count, 2 * block_rows * block_rows)
    flattened = jnp.pad(flattened, ((0, 0), (0, 0), (0, block_rows)))
    skewed = flattened.reshape(group_count, band_count, block_rows, 2 * block_rows + 1)
    flipped = jnp.sum(skewed, axis=2)[:, :, ::-1]
    extent = (band_count + 1) * block_rows + 1
    accum = jnp.zeros((group_count, extent), jnp.float32)
    for band_index in range(band_count):
        offset = band_index * block_rows
        accum = accum + jnp.pad(
            flipped[:, band_index], ((0, 0), (offset, extent - offset - 2 * block_rows - 1))
        )
    return accum[:, block_rows : block_rows + tap_count]


def local(inputs, upstream, medium_filter, short_filter):
    length_dev = inputs.shape[0]
    width = inputs.shape[1]
    groups = width // GROUP
    tap_count = medium_filter.shape[1]
    short_taps = short_filter.shape[1]
    halo_rows = tap_count - 1
    block_rows = math.gcd(length_dev, 128)
    lead_blocks = -(-halo_rows // block_rows)
    band_count = lead_blocks + 1
    lead_rows = lead_blocks * block_rows
    own_blocks = length_dev // block_rows
    top = band_count - 1
    bands = band_tables(medium_filter, block_rows, band_count)
    short_channel = jnp.repeat(short_filter, GROUP, axis=0).astype(jnp.float32)
    previous = shifted(inputs[length_dev - halo_rows :], "ctx", 1)
    front_pad = jnp.zeros((lead_rows - halo_rows, width), inputs.dtype)
    extended_t = jnp.concatenate([front_pad, previous, inputs], axis=0).T
    conv_out = causal_conv(extended_t, bands, block_rows, band_count, own_blocks)
    gate = short_apply(extended_t, short_channel, lead_rows, length_dev)
    cot_values = upstream.T.astype(jnp.float32)
    gate_cot = (cot_values * conv_out).astype(jnp.bfloat16)
    conv_cot = (cot_values * gate).astype(jnp.bfloat16)
    next_conv, next_gate = shifted(
        (conv_cot[:, :halo_rows].T, gate_cot[:, : short_taps - 1].T), "ctx", -1
    )
    tail_pad = jnp.zeros((width, lead_rows - halo_rows), conv_cot.dtype)
    conv_tail = jnp.concatenate([conv_cot, next_conv.T, tail_pad], axis=1)
    gate_tail = jnp.concatenate([gate_cot, next_gate.T], axis=1)
    medium_back = later_conv(conv_tail, bands, block_rows, band_count, own_blocks)
    short_back = jnp.zeros((width, length_dev), jnp.float32)
    short_rows = []
    gate_values = gate_cot.astype(jnp.float32)
    for tap_index in range(short_taps):
        ahead = gate_tail[:, tap_index : tap_index + length_dev].astype(jnp.float32)
        short_back = short_back + short_channel[:, tap_index][:, None] * ahead
        window = extended_t[:, lead_rows - tap_index : lead_rows - tap_index + length_dev].astype(
            jnp.float32
        )
        channel_sums = jnp.sum(gate_values * window, axis=1)
        short_rows.append(jnp.sum(channel_sums.reshape(groups, GROUP), axis=1))
    input_gradient = (medium_back + short_back).astype(jnp.bfloat16).T
    cot_blocks = blocked(conv_cot, block_rows)
    token_blocks = blocked(extended_t, block_rows)
    pair_list = []
    for band_index in range(band_count):
        part = token_blocks[:, :, top - band_index : top - band_index + own_blocks]
        pair_list.append(
            jnp.einsum("gckt,gcks->gts", cot_blocks, part, preferred_element_type=jnp.float32)
        )
    pair_sums = jnp.stack(pair_list, axis=1)
    medium_part = diagonal_sums(pair_sums, tap_count)
    short_part = jnp.stack(short_rows, axis=1)
    factor = float(GROUP * length_dev * lax.axis_size("ctx")) ** (-0.5)
    total_medium, total_short = lax.psum((medium_part, short_part), "ctx")
    return (input_gradient, total_medium * factor, total_short * factor)


def solution(mesh):
    return jax.shard_map(
        local,
        mesh=mesh,
        in_specs=(P("ctx", "fsdp"), P("ctx", "fsdp"), P("fsdp", None), P("fsdp", None)),
        out_specs=(P("ctx", "fsdp"), P("fsdp", None), P("fsdp", None)),
        check_vma=False,
    )
```

profile of v0, /device:TPU:0, one launch (start us, length us, event | category | flops | bytes accessed | tf_op | source)
XLA Modules:
  0.0 373.8 jit_solution(8095847646933808629)
XLA Ops:
  7.2 1.3 copy.38
  8.5 0.2 slice.157
  8.7 4.9 %collective-permute-start = (bf16[127,2048]{0,1:T(8,128)(2,1)S(1)}, bf16[127,2048]{0,1:T(8,128)(2,1)S(1)}, u32[]{:S(2)}, u32[]{:S(2)}) collective-permute-start(bf16[127,2048]{0,1:T(8,128)(2,1)S(1)} %slice.157), channel_id=1, source_target_pairs={{0,4},{4,8},{8,12},{12,16},{16,20},{20,24},{24,28},{1,5},{5,9},{9,... | collective-permute-start | bytes 1560584 | tf_op jit(solution)/shard_map/ppermute | solution.py:15
  13.6 0.9 copy.41
  14.5 0.9 broadcast_clamp_fusion
  15.4 114.2 %gather_fusion = bf16[32768,128]{1,0:T(8,128)(2,1)} fusion(bf16[128,128]{0,1:T(8,128)(2,1)S(1)} %copy.41, s32[32768]{0:T(1024)S(1)} %broadcast_clamp_fusion), kind=kCustom, calls=%fused_computation | custom fusion | bytes 16908288 | tf_op jit(solution)/shard_map/jit(_take)/gather | solution.py:27
  129.6 12.5 %copy.42 = bf16[128,2,128,128]{3,2,0,1:T(8,128)(2,1)} copy(bf16[128,2,128,128]{0,3,2,1:T(8,128)(2,1)} %bitcast.81) | data formatting | bytes 16777216 | tf_op jit(solution)/shard_map/jit(_take)/gather | solution.py:27
  142.1 7.3 %broadcast_select_fusion = bf16[128,2,128,128]{3,2,0,1:T(8,128)(2,1)} fusion(bf16[128,2,128,128]{3,2,0,1:T(8,128)(2,1)} %copy.42, pred[2,128,128]{2,1,0:T(8,128)(4,1)S(1)} %bitcast.101), kind=kLoop, calls=%fused_computation.2 | loop fusion | flops 4194304 | bytes 16809984 | tf_op jit(solution)/shard_map/jit(_where)/select_n | solution.py:29
  149.5 0.2 broadcast_in_dim.36
  149.7 0.3 convert_element_type.83
  149.9 0.3 copy.37
  150.3 0.5 maximum_bitcast_fusion
  150.7 0.3 reshape.94
  151.0 3.1 fusion.13
  154.1 0.8 slice_bitcast_fusion.11
  154.9 1.5 collective-permute-start.1
  156.4 1.5 fusion.37
  157.9 2.3 fusion
  160.2 4.5 %convolution_bitcast_fusion.1 = f32[128,1,128,128]{3,2,0,1:T(8,128)} fusion(bf16[128,16,128]{2,1,0:T(8,128)(2,1)S(1)} %bitcast.82, bf16[128,16,1,128]{3,2,1,0:T(2,128)(2,1)S(1)} %get-tuple-element.23), kind=kOutput, calls=%fused_computation.10 | convolution fusion | flops 67108864 | bytes 9437184 | tf_op jit(solution)/shard_map/gckt,gcks->gts/dot_general | solution.py:140
  164.7 4.5 %convolution_bitcast_fusion = f32[128,1,128,128]{3,2,0,1:T(8,128)} fusion(bf16[128,16,128]{2,1,0:T(8,128)(2,1)S(1)} %bitcast.83, bf16[128,16,1,128]{3,2,1,0:T(2,128)(2,1)S(1)} %get-tuple-element.22), kind=kOutput, calls=%fused_computation.9 | convolution fusion | flops 67108864 | bytes 9437184 | tf_op jit(solution)/shard_map/gckt,gcks->gts/dot_general | solution.py:140
  169.2 2.3 fusion.5
  171.5 2.9 fusion.28
  174.7 0.1 reduce_sum.141
  174.9 0.1 reduce_sum.143
  175.1 0.1 reduce_sum.145
  175.8 0.8 slice_bitcast_fusion.10
  176.7 11.7 %pad_maximum_fusion = f32[128,2,128,128]{3,2,0,1:T(8,128)} fusion(f32[128,1,128,128]{3,2,0,1:T(8,128)} %convolution_bitcast_fusion, f32[128,1,128,128]{3,2,0,1:T(8,128)} %convolution_bitcast_fusion.1), kind=kLoop, calls=%fused_computation.1 | loop fusion | flops 4194304 | bytes 33554432 | tf_op jit(solution)/shard_map/stack | solution.py:142
  188.3 18.1 %copy.54 = f32[128,2,128,128]{0,3,2,1:T(8,128)} copy(f32[128,2,128,128]{3,2,0,1:T(8,128)} %pad_maximum_fusion) | data formatting | bytes 33554432
  206.4 9.4 %pad.16.clone = f32[128,2,128,256]{0,3,2,1:T(8,128)S(1)} pad(f32[128,2,128,128]{0,3,2,1:T(8,128)} %copy.54, f32[]{:T(128)} %constant.14.clone.1), padding=0_0x0_0x0_0x128_0 | pad | bytes 50331652 | tf_op jit(solution)/shard_map/jit(_pad)/pad | solution.py:77
  215.8 11.4 %pad.17 = f32[128,2,32896]{0,2,1:T(8,128)} pad(f32[128,2,32768]{0,2,1:T(8,128)S(1)} %bitcast.80, f32[]{:T(128)} %constant.14.clone.1), padding=0_0x0_0x0_128 | pad | bytes 67239936 | tf_op jit(solution)/shard_map/jit(_pad)/pad | solution.py:79
  227.2 34.4 %reshape.100 = f32[128,2,128,257]{0,3,2,1:T(8,128)} reshape(f32[128,2,32896]{0,2,1:T(8,128)} %pad.17) | data formatting | bytes 67371008 | tf_op jit(solution)/shard_map/reshape | solution.py:80
  261.7 11.8 %reduce_sum.135 = f32[128,2,257]{0,2,1:T(8,128)S(1)} reduce(f32[128,2,128,257]{0,3,2,1:T(8,128)} %reshape.100, f32[]{:T(128)} %constant.14.clone.1), dimensions={2}, to_apply=%region_0.1 | reduce | flops 8355584 | bytes 33948676 | tf_op jit(solution)/shard_map/reduce_sum | solution.py:81
  273.5 0.2 slice.150
  273.8 0.2 slice.152
  274.0 0.6 pad_add_fusion
  274.7 23.4 %psum.15 = f32[128,7]{0,1:T(8,128)S(1)} all-reduce(f32[128,7]{0,1:T(8,128)S(1)} %stack.43), channel_id=1, replica_groups=mesh['ctx'=8,'fsdp'=4] {'ctx'}, use_global_device_ids=true, to_apply=%region_16.17 | all-reduce | flops 896 | bytes 7168 | tf_op jit(solution)/shard_map/psum | solution.py:146
  298.1 0.6 broadcast_multiply_fusion.1
  298.7 1.5 collective-permute-start.2
  300.2 47.5 %all-reduce.6.cloned.1.call-done = f32[128,128]{0,1:T(8,128)} async-done(((f32[128,128]{0,1:T(8,128)}), f32[128,128]{0,1:T(8,128)}) %all-reduce.6.cloned.1.call-update) | async-done | bytes 65552 | tf_op jit(solution)/shard_map/psum | solution.py:146
  347.7 0.8 broadcast_multiply_fusion
  348.6 0.7 copy.48
  349.3 1.3 maximum_maximum_fusion
  350.6 0.3 reshape.90
  350.9 1.5 fusion.36
  352.4 3.4 fusion.1
  355.7 3.4 fusion.4
  359.2 6.8 %fusion.21 = bf16[2048,128]{1,0:T(8,128)(2,1)S(1)} fusion(bf16[2048,128]{1,0:T(8,128)(2,1)S(1)} %get-tuple-element.19, f32[128,16,128]{2,1,0:T(8,128)S(1)} %fusion.4, bf16[2048,6]{1,0:T(8,128)(2,1)} %bitcast.22, f32[2048]{0:T(1024)S(1)} %bitcast.90, f32[2048]{0:T(1024)S(1)} %bitcast.92, f32[2048]{0:T(1024)S(1)} %bitcast.94, f32[2048]{0:T(1024)S(1)} %bitcast.96, ...), kind=kLoop, calls=%fused_computation.53 | loop fusion | flops 10485760 | bytes 2179072 | tf_op jit(solution)/shard_map/convert_element_type | solution.py:133
  366.0 1.0 copy.47
  (29 shorter events, 1.2 us)
Async XLA Ops:
  7.2 340.5 %all-reduce.6.cloned.1.call-start = ((), (), s32[]{:S(2)}) async-start(), calls=%async_computation | async-start | bytes 131072 | tf_op jit(solution)/shard_map/psum | solution.py:146
  8.7 141.5 %collective-permute-start = (bf16[127,2048]{0,1:T(8,128)(2,1)S(1)}, bf16[127,2048]{0,1:T(8,128)(2,1)S(1)}, u32[]{:S(2)}, u32[]{:S(2)}) collective-permute-start(bf16[127,2048]{0,1:T(8,128)(2,1)S(1)} %slice.157), channel_id=1, source_target_pairs={{0,4},{4,8},{8,12},{12,16},{16,20},{20,24},{24,28},{1,5},{5,9},{9,... | collective-permute-start | bytes 1560584 | tf_op jit(solution)/shard_map/ppermute | solution.py:15
  129.6 12.5 %copy-start.2 = (pred[2,128,128]{2,1,0:T(32,128)(4,1)S(1)}, pred[2,128,128]{2,1,0:T(32,128)(4,1)}, u32[]{:S(2)}) copy-start(pred[2,128,128]{2,1,0:T(32,128)(4,1)} %constant.32.clone) | copy-start | bytes 98308
  142.1 7.4 %copy-start.3 = (bf16[128,7]{0,1:T(8,128)(2,1)S(1)}, bf16[128,7]{0,1:T(8,128)(2,1)}, u32[]{:S(2)}) copy-start(bf16[128,7]{0,1:T(8,128)(2,1)} %param.9) | copy-start | bytes 5380
  142.1 7.8 %copy-start.1 = (bf16[128,2048]{1,0:T(8,128)(2,1)S(1)}, bf16[128,2048]{1,0:T(8,128)(2,1)}, u32[]{:S(2)}) copy-start(bf16[128,2048]{1,0:T(8,128)(2,1)} %param.7) | copy-start | bytes 1572868
  151.0 6.9 %copy-start = (bf16[128,2,128,128]{3,2,0,1:T(8,128)(2,1)S(1)}, bf16[128,2,128,128]{3,2,0,1:T(8,128)(2,1)}, u32[]{:S(2)}) copy-start(bf16[128,2,128,128]{3,2,0,1:T(8,128)(2,1)} %broadcast_select_fusion) | copy-start | bytes 25165828
  154.9 194.3 %collective-permute-start.1 = (bf16[127,2048]{0,1:T(8,128)(2,1)}, bf16[127,2048]{0,1:T(8,128)(2,1)}, u32[]{:S(2)}, u32[]{:S(2)}) collective-permute-start(bf16[127,2048]{0,1:T(8,128)(2,1)} %slice_bitcast_fusion.11), channel_id=1, source_target_pairs={{4,0},{8,4},{12,8},{16,12},{20,16},{24,20},{28,24},{5,1},{9,5},{13... | collective-permute-start | bytes 1560584 | tf_op jit(solution)/shard_map/ppermute | solution.py:15
  298.7 60.5 %collective-permute-start.2 = (bf16[6,2048]{0,1:T(8,128)(2,1)}, bf16[6,2048]{0,1:T(8,128)(2,1)}, u32[]{:S(2)}, u32[]{:S(2)}) collective-permute-start(bf16[6,2048]{0,1:T(8,128)(2,1)} %slice_bitcast_fusion.10), channel_id=1, source_target_pairs={{4,0},{8,4},{12,8},{16,12},{20,16},{24,20},{28,24},{5,1},{9,5},{13... | collective-permute-start | bytes 73736 | tf_op jit(solution)/shard_map/ppermute | solution.py:15
Sparse Core Ops, SparseCore 0:
  274.8 72.8 all-reduce.5
where the time goes:
time: 376 us; the launch traced here: 374 us
  local copies, waits for them, and re-layouts  211 us (56%)
  other arithmetic  49.1 us (13%)
  waiting for transfers between devices  47.5 us (13%)
  blocking collectives  23.4 us (6%)
  matrix products  20.4 us (5%)
  between operations  14.3 us (4%)
  starting transfers between devices  7.87 us (2%)
    gather x2, local copies, waits for them, and re-layouts, band_tables(): jnp.take(medium_filter, jnp.asarray(indices, dtype=jnp.int32), axis=1)  127 us
    psum x1, waiting for transfers between devices, local(): total_medium, total_short = lax.psum((medium_part, short_part), 'ctx')  47.5 us
    reshape x1, local copies, waits for them, and re-layouts, diagonal_sums(): flattened.reshape(group_count, band_count, block_rows, 2 * block_rows + 1)  34.4 us
    psum x1, blocking collectives, local(): total_medium, total_short = lax.psum((medium_part, short_part), 'ctx')  23.4 us
    unnamed x14, local copies, waits for them, and re-layouts  22.3 us
    reduce_sum x1, other arithmetic, diagonal_sums(): flipped = jnp.sum(skewed, axis=2)[:, :, ::-1]  11.8 us
    another operation x1, other arithmetic, local(): pair_sums = jnp.stack(pair_list, axis=1)  11.7 us
    pad x1, local copies, waits for them, and re-layouts, diagonal_sums(): flattened = jnp.pad(flattened, ((0, 0), (0, 0), (0, block_rows)))  11.4 us
  transfers between devices with their start and end apart: 4, of which 1 were waited for; matrix products, arithmetic and copies ran while one was open for 71% of the time, Pallas kernels for 0%

commit v1 on v0

v1 whole, which is shorter than its diff:
```python
import functools

import jax
import jax.numpy as jnp
from jax import lax
from jax.experimental import pallas as pl
from jax.experimental.pallas import tpu as pltpu
from jax.sharding import PartitionSpec as P

GROUP = 16
ROWS = 16
F32 = jnp.float32
BF16 = jnp.bfloat16


def iota(shape, dim):
    return lax.broadcasted_iota(jnp.int32, shape, dim)


def split3(values):
    high = values.astype(BF16)
    rest = values - high.astype(F32)
    middle = rest.astype(BF16)
    low = (rest - middle.astype(F32)).astype(BF16)
    return jnp.concatenate([high, middle, low], axis=0)


def exact_dot(values, table):
    rows = values.shape[0]
    out = jnp.dot(split3(values), table, preferred_element_type=F32)
    return out[:rows] + out[rows : 2 * rows] + out[2 * rows :]


def delayed(values, distance):
    return values if distance == 0 else pltpu.roll(values, distance, 0)


def toeplitz(base, table_ref):
    groups, lanes = base.shape
    for g in range(groups):
        row = jnp.broadcast_to(base[g : g + 1], (ROWS, lanes))
        table_ref[g * ROWS : (g + 1) * ROWS, :] = pltpu.roll(
            row, 0, 1, stride=1, stride_axis=0
        ).astype(BF16)


def own_group(product, lane_group):
    total = product[:ROWS]
    for g in range(1, product.shape[0] // ROWS):
        total = jnp.where(lane_group == g, product[g * ROWS : (g + 1) * ROWS], total)
    return total


def cot_kernel(taps, x_ref, u_ref, st_ref, *outs):
    cot_refs, wide_ref = outs[:-1], outs[-1]
    rows, cols = x_ref.shape
    groups = st_ref.shape[1]
    first = pl.program_id(0) * (cols // GROUP)
    spread = iota((groups, cols), 0) == first + iota((groups, cols), 1) // GROUP
    wide = jnp.dot(st_ref[...], spread.astype(BF16), preferred_element_type=F32)
    wide_ref[...] = wide
    x = x_ref[...].astype(F32)
    gate = wide[0:1] * x
    for j in range(1, taps):
        gate = gate + wide[j : j + 1] * delayed(x, j)
    cot = (u_ref[...].astype(F32) * gate).astype(BF16)[ROWS:]
    if len(cot_refs) == 1:
        cot_refs[0][...] = cot
    else:
        steps = pl.num_programs(0) // len(cot_refs)
        for i, ref in enumerate(cot_refs):

            @pl.when(pl.program_id(0) // steps == i)
            def _():
                ref[...] = cot


def sum_kernel(taps, factor, first_step, m_ref, prev_ref, x_ref, u_ref, cot_ref, wide_ref,
               *rest):
    sums_in, rest = (rest[0], rest[1:]) if len(rest) == 6 else (None, rest)
    gate_cot_ref, edge_ref, sums_ref, x_ext, table = rest
    rows, cols = x_ref.shape
    halo = prev_ref.shape[0]
    med = m_ref.shape[1]
    groups = m_ref.shape[0]
    window = med + ROWS
    lanes = table.shape[1]
    step = pl.program_id(0)
    total_groups = sums_ref.shape[0] - 8

    if sums_in is None:

        @pl.when(step == 0)
        def _():
            sums_ref[...] = jnp.zeros_like(sums_ref)

    else:

        @pl.when(step == 0)
        def _():
            sums_ref[...] = sums_in[...]

    x_ext[:halo, :] = prev_ref[...]
    x_ext[halo:, :] = x_ref[...]
    flip = iota((med, lanes), 0) == med - iota((med, lanes), 1)
    toeplitz(jnp.dot(m_ref[...], flip.astype(BF16), preferred_element_type=F32), table)
    lane_group = iota((ROWS, cols), 1) // GROUP

    x_near = x_ext[halo - ROWS :, :].astype(F32)
    wide = wide_ref[...]
    head = x_near[: 2 * ROWS]
    gate = wide[0:1] * head
    for j in range(1, taps):
        gate = gate + wide[j : j + 1] * delayed(head, j)
    head_cot = (u_ref[:ROWS, :].astype(F32) * gate[ROWS:]).astype(BF16)
    edge_ref[:ROWS, :] = head_cot

    upturn = iota((rows, rows), 0) ^ (ROWS - 1) == iota((rows, rows), 1)
    cots = jnp.concatenate([head_cot, cot_ref[...]], 0)
    cots = jnp.dot(upturn.astype(BF16), cots, preferred_element_type=F32).astype(BF16)

    pairs = jnp.zeros((groups * ROWS, window), F32)
    for a in range(rows // ROWS):
        here = slice(a * ROWS, (a + 1) * ROWS)
        part = x_ext[a * ROWS : a * ROWS + window, :]
        conv = own_group(
            jnp.dot(table[:, :window], part, preferred_element_type=F32), lane_group
        )
        gate_cot_ref[here, :] = (u_ref[here, :].astype(F32) * conv).astype(BF16)
        cot = cots[here]
        alone = jnp.concatenate(
            [jnp.where(lane_group == g, cot, jnp.zeros_like(cot)) for g in range(groups)], 0
        )
        pairs = pairs + lax.dot_general(
            alone, part, (((1,), (1,)), ((), ())), preferred_element_type=F32
        )
    edge_ref[ROWS:, :] = gate_cot_ref[:ROWS, :]

    pairs = jnp.concatenate([pairs, jnp.zeros((groups * ROWS, lanes - window), F32)], 1)
    diagonals = []
    for g in range(groups):
        block = pltpu.roll(
            pairs[g * ROWS : (g + 1) * ROWS], 0, 1, stride=1, stride_axis=0
        )
        diagonals.append(jnp.sum(block, 0, keepdims=True))
    flip_back = iota((lanes, med), 0) == med + ROWS - 1 - iota((lanes, med), 1)
    medium = exact_dot(jnp.concatenate(diagonals, 0), flip_back.astype(BF16))
    at = pl.multiple_of((first_step + step) * groups, groups)
    sums_ref[pl.ds(at, groups), :] = medium * factor

    gate_cot = gate_cot_ref[...].astype(F32)
    short = [
        jnp.sum(gate_cot * delayed(x_near, j)[ROWS:], 0, keepdims=True) for j in range(taps)
    ]
    short.append(jnp.zeros((8 - taps, cols), F32))
    gather = (
        iota((cols, med), 1) == (first_step + step) * groups + iota((cols, med), 0) // GROUP
    )
    sums_ref[total_groups:, :] += (
        exact_dot(jnp.concatenate(short, 0), gather.astype(BF16)) * factor
    )


def back_kernel(ms_ref, cot_ref, gate_cot_ref, edge_ref, next_ref, next_edge_ref, out_ref,
                c_ext, g_ext, table):
    rows, cols = gate_cot_ref.shape
    med = next_ref.shape[0] + ROWS
    window = med + ROWS
    toeplitz(ms_ref[...].astype(F32), table)
    lane_group = iota((ROWS, cols), 1) // GROUP
    c_ext[:ROWS, :] = edge_ref[:ROWS, :]
    c_ext[ROWS:rows, :] = cot_ref[...]
    c_ext[rows : rows + ROWS, :] = next_edge_ref[:ROWS, :]
    c_ext[rows + ROWS :, :] = next_ref[...]
    g_ext[:rows, :] = gate_cot_ref[...]
    g_ext[rows:, :] = next_edge_ref[ROWS:, :]
    for a in range(rows // ROWS):
        part = jnp.concatenate(
            [
                c_ext[a * ROWS : a * ROWS + window, :],
                g_ext[a * ROWS : (a + 2) * ROWS, :],
            ],
            0,
        )
        product = jnp.dot(
            table[:, : window + 2 * ROWS], part, preferred_element_type=F32
        )
        out_ref[a * ROWS : (a + 1) * ROWS, :] = own_group(product, lane_group).astype(BF16)


def permuted(block, pairs):
    return lax.ppermute(block, "ctx", pairs)


def local(inputs, upstream, medium_filter, short_filter):
    rows, width = inputs.shape
    groups, med = medium_filter.shape
    taps = short_filter.shape[1]
    devices = lax.axis_size("ctx")
    assert rows % ROWS == 0 and rows >= med and med % 128 == 0 and groups <= med
    assert taps <= 8
    cols = 256 if width % 256 == 0 else width
    chunks = 2 if width % (2 * cols) == 0 else 1
    steps = width // cols // chunks
    part = steps * cols
    tile = cols // GROUP
    lanes = med + 128
    factor = float(GROUP * rows * devices) ** -0.5
    forward = [(i, i + 1) for i in range(devices - 1)]
    backward = [(i + 1, i) for i in range(devices - 1)]
    limit = 48 << 20

    def params():
        return pltpu.CompilerParams(vmem_limit_bytes=limit)

    tail = inputs[rows - med :]
    previous = [permuted(tail[:, i * part : (i + 1) * part], forward) for i in range(chunks)]

    short_rows = jnp.pad(short_filter.T, ((0, 8 - taps), (0, 0)))
    whole = lambda i: (0, 0)
    along = lambda i: (0, i)

    def held(k):
        return lambda i: (0, jnp.clip(i - k * steps, 0, steps - 1))

    *cots, wide = pl.pallas_call(
        functools.partial(cot_kernel, taps),
        grid=(chunks * steps,),
        in_specs=[
            pl.BlockSpec((rows, cols), along),
            pl.BlockSpec((rows, cols), along),
            pl.BlockSpec((8, groups), whole),
        ],
        out_specs=[pl.BlockSpec((rows - ROWS, cols), held(k)) for k in range(chunks)]
        + [pl.BlockSpec((8, cols), along)],
        out_shape=[jax.ShapeDtypeStruct((rows - ROWS, part), BF16)] * chunks
        + [jax.ShapeDtypeStruct((8, width), F32)],
        compiler_params=params(),
        name="conv_cot",
    )(inputs, upstream, short_rows)

    following = [permuted(c[: med - ROWS], backward) for c in cots]

    gate_cots, edges, sums = [], [], None
    for k in range(chunks):
        base = k * steps
        shift = lambda i, base=base: (0, base + i)
        in_specs = [
            pl.BlockSpec((tile, med), lambda i, base=base: (base + i, 0)),
            pl.BlockSpec((med, cols), along),
            pl.BlockSpec((rows, cols), shift),
            pl.BlockSpec((rows, cols), shift),
            pl.BlockSpec((rows - ROWS, cols), along),
            pl.BlockSpec((8, cols), shift),
        ]
        operands = [medium_filter, previous[k], inputs, upstream, cots[k], wide]
        if k:
            in_specs.append(pl.BlockSpec((groups + 8, med), whole))
            operands.append(sums)
        gate_cot, edge, sums = pl.pallas_call(
            functools.partial(sum_kernel, taps, factor, base),
            grid=(steps,),
            in_specs=in_specs,
            out_specs=[
                pl.BlockSpec((rows, cols), along),
                pl.BlockSpec((2 * ROWS, cols), along),
                pl.BlockSpec((groups + 8, med), whole),
            ],
            out_shape=[
                jax.ShapeDtypeStruct((rows, part), BF16),
                jax.ShapeDtypeStruct((2 * ROWS, part), BF16),
                jax.ShapeDtypeStruct((groups + 8, med), F32),
            ],
            scratch_shapes=[
                pltpu.VMEM((med + rows, cols), BF16),
                pltpu.VMEM((tile * ROWS, lanes), BF16),
            ],
            compiler_params=params(),
            name="filter_sums",
        )(*operands)
        gate_cots.append(gate_cot)
        edges.append(edge)

    next_edges = [permuted(e, backward) for e in edges]

    if devices & (devices - 1):
        sums = lax.psum(sums, "ctx")
    else:
        reach = 1
        while reach < devices:
            sums = sums + permuted(sums, [(i, i ^ reach) for i in range(devices)])
            reach *= 2

    both = jnp.pad(medium_filter, ((0, 0), (0, lanes - med))) + jnp.pad(
        short_filter, ((0, 0), (med + ROWS, lanes - med - ROWS - taps))
    )
    pieces = []
    for k in range(chunks):
        base = k * steps
        pieces.append(
            pl.pallas_call(
                back_kernel,
                grid=(steps,),
                in_specs=[
                    pl.BlockSpec((tile, lanes), lambda i, base=base: (base + i, 0)),
                    pl.BlockSpec((rows - ROWS, cols), along),
                    pl.BlockSpec((rows, cols), along),
                    pl.BlockSpec((2 * ROWS, cols), along),
                    pl.BlockSpec((med - ROWS, cols), along),
                    pl.BlockSpec((2 * ROWS, cols), along),
                ],
                out_specs=pl.BlockSpec((rows, cols), along),
                out_shape=jax.ShapeDtypeStruct((rows, part), BF16),
                scratch_shapes=[
                    pltpu.VMEM((rows + med, cols), BF16),
                    pltpu.VMEM((rows + ROWS, cols), BF16),
                    pltpu.VMEM((tile * ROWS, lanes), BF16),
                ],
                compiler_params=params(),
                name="input_grad",
            )(both, cots[k], gate_cots[k], edges[k], following[k], next_edges[k])
        )
    input_gradient = jnp.concatenate(pieces, axis=1)
    return input_gradient, sums[:groups], sums[groups : groups + taps, :groups].T


def solution(mesh):
    return jax.shard_map(
        local,
        mesh=mesh,
        in_specs=(P("ctx", "fsdp"), P("ctx", "fsdp"), P("fsdp", None), P("fsdp", None)),
        out_specs=(P("ctx", "fsdp"), P("fsdp", None), P("fsdp", None)),
        check_vma=False,
    )
```

time: 376 us -> 54.7 us (0.15)
  local copies, waits for them, and re-layouts: 211 us -> 2.54 us
  other arithmetic: 49.1 us -> 0.94 us
  waiting for transfers between devices: 47.5 us -> 10.3 us
  blocking collectives: 23.4 us -> 0 us
  matrix products: 20.4 us -> 0 us
  Pallas kernels: 0 us -> 16.3 us
  starting transfers between devices: 7.87 us -> 23.5 us
  between operations: 14.3 us -> 0.86 us
    gather x2 -> x0, local copies, waits for them, and re-layouts: 127 us -> none  [band_tables(): jnp.take(medium_filter, jnp.asarray(indices, dtype=jnp.int32), axis=1)]
    psum x1 -> x0, waiting for transfers between devices: 47.5 us -> none  [local(): total_medium, total_short = lax.psum((medium_part, short_part), 'ctx')]
    reshape x10 -> x0, local copies, waits for them, and re-layouts: 35.6 us -> none  [the longest x1 34.4 us: diagonal_sums(): flattened.reshape(group_count, band_count, block_rows, 2 * block_rows + 1)]
    psum x1 -> x0, blocking collectives: 23.4 us -> none  [local(): total_medium, total_short = lax.psum((medium_part, short_part), 'ctx')]
    unnamed x14 -> x9, local copies, waits for them, and re-layouts: 22.3 us -> 0.16 us
    pad x2 -> x1, local copies, waits for them, and re-layouts: 20.8 us -> 0.01 us  [local(): short_rows = jnp.pad(short_filter.T, ((0, 8 - taps), (0, 0)))]
    dot_general x6 -> x0, matrix products: 20.4 us -> none  [the longest x2 9.04 us: local(): jnp.einsum('gckt,gcks->gts', cot_blocks, part, preferred_element_type=jnp...]
    pallas_call x0 -> x5, Pallas kernels: none -> 16.3 us  [the longest x2 9.94 us: local(): pl.pallas_call(functools.partial(sum_kernel, taps, factor, base), grid=(s...]
  transfers between devices with their start and end apart: 4 -> 9, of which waited for: 1 -> 2; matrix products, arithmetic and copies ran while one was open for 71% -> 2% of each run, Pallas kernels for 0% -> 30%
where the time goes in v1:
time: 54.7 us; the launch traced here: 54.4 us
  starting transfers between devices  23.5 us (43%)
  Pallas kernels  16.3 us (30%)
  waiting for transfers between devices  10.3 us (19%)
  local copies, waits for them, and re-layouts  2.54 us (5%)
  other arithmetic  0.94 us (2%)
  between operations  0.86 us (2%)
    ppermute x9, starting transfers between devices, permuted(): return lax.ppermute(block, 'ctx', pairs)  23.5 us
    ppermute x9, waiting for transfers between devices, permuted(): return lax.ppermute(block, 'ctx', pairs)  10.3 us
    pallas_call x2, Pallas kernels, local(): pl.pallas_call(functools.partial(sum_kernel, taps, factor, base), grid=(s...  9.94 us
    pallas_call x2, Pallas kernels, local(): pl.pallas_call(back_kernel, grid=(steps,), in_specs=[pl.BlockSpec((tile,...  4.27 us
    pallas_call x1, Pallas kernels, local(): pl.pallas_call(functools.partial(cot_kernel, taps), grid=(chunks * steps,...  2.08 us
    slice x1, local copies, waits for them, and re-layouts, local(): tail[:, i * part:(i + 1) * part]  1.15 us
  transfers between devices with their start and end apart: 9, of which 2 were waited for; matrix products, arithmetic and copies ran while one was open for 2% of the time, Pallas kernels for 30%

profile of v1, /device:TPU:0, one launch (start us, length us, event | category | flops | bytes accessed | tf_op | source)
XLA Modules:
  0.0 54.4 jit_solution(9958575482889079932)
XLA Ops:
  0.6 0.0 copy-start
  0.6 0.0 copy-start.1
  0.6 1.2 %fusion = (bf16[128,1024]{1,0:T(8,128)(2,1)S(1)}, bf16[128,1024]{1,0:T(8,128)(2,1)S(1)}) fusion(bf16[128,2048]{1,0:T(8,128)(2,1)} %x_ref.5), kind=kLoop, calls=%fused_computation.3 | loop fusion | bytes 1048576 | tf_op jit(solution)/shard_map/slice | solution.py:217
  1.8 0.0 copy-start.3
  1.8 4.9 %collective-permute-start = (bf16[128,1024]{1,0:T(8,128)(2,1)S(1)}, bf16[128,1024]{1,0:T(8,128)(2,1)S(1)}, u32[]{:S(2)}, u32[]{:S(2)}) collective-permute-start(bf16[128,1024]{1,0:T(8,128)(2,1)S(1)} %get-tuple-element.21), channel_id=1, source_target_pairs={{0,4},{4,8},{8,12},{12,16},{16,20},{20,24},{24,28},{1,5},{5,9},{9,... | collective-permute-start | bytes 786440 | tf_op jit(solution)/shard_map/ppermute | solution.py:192
  6.7 3.5 %collective-permute-start.3 = (bf16[128,1024]{1,0:T(8,128)(2,1)S(1)}, bf16[128,1024]{1,0:T(8,128)(2,1)S(1)}, u32[]{:S(2)}, u32[]{:S(2)}) collective-permute-start(bf16[128,1024]{1,0:T(8,128)(2,1)S(1)} %get-tuple-element.22), channel_id=1, source_target_pairs={{0,4},{4,8},{8,12},{12,16},{16,20},{20,24},{24,28},{1,5},{5,9},{9,... | collective-permute-start | bytes 786440 | tf_op jit(solution)/shard_map/ppermute | solution.py:192
  10.1 0.0 copy-done.3
  10.2 0.0 copy-done
  10.2 0.0 copy-done.1
  10.2 0.0 copy-start.2
  10.2 2.1 %conv_cot.1 = (bf16[112,1024]{1,0:T(8,128)(2,1)S(1)}, bf16[112,1024]{1,0:T(8,128)(2,1)S(1)}, f32[8,2048]{1,0:T(8,128)S(1)}) custom-call(bf16[128,2048]{1,0:T(8,128)(2,1)S(1)} %copy-done, bf16[128,2048]{1,0:T(8,128)(2,1)S(1)} %copy-done.1, bf16[8,128]{1,0:T(8,128)(2,1)S(1)} %pad.14.st_ref), custom_call_target="tpu_custom_call" | custom-call | tf_op jit(solution)/shard_map/conv_cot/pallas_call | solution.py:226
  12.3 1.3 %collective-permute-start.4 = (bf16[112,1024]{1,0:T(8,128)(2,1)S(1)}, bf16[112,1024]{1,0:T(8,128)(2,1)S(1)}, u32[]{:S(2)}, u32[]{:S(2)}) collective-permute-start(bf16[112,1024]{1,0:T(8,128)(2,1)S(1)} %get-tuple-element.16.cot_ref), channel_id=1, source_target_pairs={{4,0},{8,4},{12,8},{16,12},{20,16},{24,20},{28,24},{5,1},{9,5},{13... | collective-permute-start | bytes 688136 | tf_op jit(solution)/shard_map/ppermute | solution.py:192
  13.6 1.3 %collective-permute-start.1 = (bf16[112,1024]{1,0:T(8,128)(2,1)S(1)}, bf16[112,1024]{1,0:T(8,128)(2,1)S(1)}, u32[]{:S(2)}, u32[]{:S(2)}) collective-permute-start(bf16[112,1024]{1,0:T(8,128)(2,1)S(1)} %get-tuple-element.12.cot_ref), channel_id=1, source_target_pairs={{4,0},{8,4},{12,8},{16,12},{20,16},{24,20},{28,24},{5,1},{9,5},{13... | collective-permute-start | bytes 688136 | tf_op jit(solution)/shard_map/ppermute | solution.py:192
  14.9 0.0 collective-permute-done.prev_ref
  14.9 0.0 copy-done.2
  14.9 5.0 %filter_sums.2 = (bf16[128,1024]{1,0:T(8,128)(2,1)S(1)}, bf16[32,1024]{1,0:T(8,128)(2,1)S(1)}, f32[136,128]{1,0:T(8,128)S(1)}) custom-call(bf16[128,128]{1,0:T(8,128)(2,1)S(1)} %copy-done.2, bf16[128,1024]{1,0:T(8,128)(2,1)S(1)} %collective-permute-done.prev_ref, bf16[128,2048]{1,0:T(8,128)(2,1)S(1)} %copy-done, bf16[128,2048]{1,0:T(8,128)(2,1)S(1)} %copy-done.1, ...), custom_call_target="tpu_custom_call" | custom-call | tf_op jit(solution)/shard_map/filter_sums/pallas_call | solution.py:260
  19.9 7.8 %collective-permute-done.3.prev_ref = bf16[128,1024]{1,0:T(8,128)(2,1)S(1)} collective-permute-done((bf16[128,1024]{1,0:T(8,128)(2,1)S(1)}, bf16[128,1024]{1,0:T(8,128)(2,1)S(1)}, u32[]{:S(2)}, u32[]{:S(2)}) %collective-permute-start.3) | collective-permute-done | bytes 262176 | tf_op jit(solution)/shard_map/ppermute | solution.py:192
  27.7 5.0 %filter_sums.3 = (bf16[128,1024]{1,0:T(8,128)(2,1)S(1)}, bf16[32,1024]{1,0:T(8,128)(2,1)S(1)}, f32[136,128]{1,0:T(8,128)S(1)}) custom-call(bf16[128,128]{1,0:T(8,128)(2,1)S(1)} %copy-done.2, bf16[128,1024]{1,0:T(8,128)(2,1)S(1)} %collective-permute-done.3.prev_ref, bf16[128,2048]{1,0:T(8,128)(2,1)S(1)} %copy-done, bf16[128,2048]{1,0:T(8,128)(2,1)S(1)} %copy-done.1, ...), custom_call_target="tpu_custom_call" | custom-call | tf_op jit(solution)/shard_map/filter_sums/pallas_call | solution.py:260
  32.6 2.5 %collective-permute-start.6 = (f32[136,128]{1,0:T(8,128)S(1)}, f32[136,128]{1,0:T(8,128)S(1)}, u32[]{:S(2)}, u32[]{:S(2)}) collective-permute-start(f32[136,128]{1,0:T(8,128)S(1)} %get-tuple-element.20), channel_id=1, source_target_pairs={{0,4},{4,0},{8,12},{12,8},{16,20},{20,16},{24,28},{28,24},{1,5},{5... | collective-permute-start | bytes 208904 | tf_op jit(solution)/shard_map/ppermute | solution.py:192
  35.2 0.1 copy.7
  35.3 1.3 %collective-permute-start.5 = (bf16[32,1024]{1,0:T(8,128)(2,1)S(1)}, bf16[32,1024]{1,0:T(8,128)(2,1)S(1)}, u32[]{:S(2)}, u32[]{:S(2)}) collective-permute-start(bf16[32,1024]{1,0:T(8,128)(2,1)S(1)} %get-tuple-element.19.edge_ref), channel_id=1, source_target_pairs={{4,0},{8,4},{12,8},{16,12},{20,16},{24,20},{28,24},{5,1},{9,5},{13... | collective-permute-start | bytes 196616 | tf_op jit(solution)/shard_map/ppermute | solution.py:192
  36.6 1.3 %collective-permute-start.2 = (bf16[32,1024]{1,0:T(8,128)(2,1)S(1)}, bf16[32,1024]{1,0:T(8,128)(2,1)S(1)}, u32[]{:S(2)}, u32[]{:S(2)}) collective-permute-start(bf16[32,1024]{1,0:T(8,128)(2,1)S(1)} %get-tuple-element.15.edge_ref), channel_id=1, source_target_pairs={{4,0},{8,4},{12,8},{16,12},{20,16},{24,20},{28,24},{5,1},{9,5},{13... | collective-permute-start | bytes 196616 | tf_op jit(solution)/shard_map/ppermute | solution.py:192
  37.9 0.0 collective-permute-done.6
  38.0 4.8 %collective-permute-start.7 = (f32[136,128]{1,0:T(8,128)S(1)}, f32[136,128]{1,0:T(8,128)S(1)}, u32[]{:S(2)}, u32[]{:S(2)}) collective-permute-start(f32[136,128]{1,0:T(8,128)S(1)} %add.19), channel_id=1, source_target_pairs={{0,8},{4,12},{8,0},{12,4},{16,24},{20,28},{24,16},{28,20},{1,9},{5... | collective-permute-start | bytes 208904 | tf_op jit(solution)/shard_map/ppermute | solution.py:192
  42.7 0.1 pad_add_fusion.ms_ref
  42.8 0.0 collective-permute-done.4.next_ref
  42.8 0.0 collective-permute-done.5.next_edge_ref
  42.8 2.1 %input_grad.3 = bf16[128,1024]{1,0:T(8,128)(2,1)S(1)} custom-call(bf16[128,256]{1,0:T(8,128)(2,1)S(1)} %pad_add_fusion.ms_ref, bf16[112,1024]{1,0:T(8,128)(2,1)S(1)} %get-tuple-element.16.cot_ref, bf16[128,1024]{1,0:T(8,128)(2,1)S(1)} %get-tuple-element.18.gate_cot_ref, bf16[32,1024]{1,0:T(8,128)(2,1)S(1)} %get-tuple-element.19.edge_ref, ...), custom_call_target="tpu_custom_call" | custom-call | tf_op jit(solution)/shard_map/input_grad/pallas_call | solution.py:301
  45.0 0.0 collective-permute-done.1.next_ref
  45.0 0.0 collective-permute-done.2.next_edge_ref
  45.0 2.1 %input_grad.2 = bf16[128,1024]{1,0:T(8,128)(2,1)S(1)} custom-call(bf16[128,256]{1,0:T(8,128)(2,1)S(1)} %pad_add_fusion.ms_ref, bf16[112,1024]{1,0:T(8,128)(2,1)S(1)} %get-tuple-element.12.cot_ref, bf16[128,1024]{1,0:T(8,128)(2,1)S(1)} %get-tuple-element.14.gate_cot_ref, bf16[32,1024]{1,0:T(8,128)(2,1)S(1)} %get-tuple-element.15.edge_ref, ...), custom_call_target="tpu_custom_call" | custom-call | tf_op jit(solution)/shard_map/input_grad/pallas_call | solution.py:301
  47.1 0.0 collective-permute-done.7
  47.2 2.6 %collective-permute-start.8 = (f32[136,128]{1,0:T(8,128)S(1)}, f32[136,128]{1,0:T(8,128)S(1)}, u32[]{:S(2)}, u32[]{:S(2)}) collective-permute-start(f32[136,128]{1,0:T(8,128)S(1)} %add.20), channel_id=1, source_target_pairs={{0,16},{4,20},{8,24},{12,28},{16,0},{20,4},{24,8},{28,12},{1,17},{... | collective-permute-start | bytes 208904 | tf_op jit(solution)/shard_map/ppermute | solution.py:192
  49.8 0.8 %pad_maximum_fusion = bf16[128,2048]{1,0:T(8,128)(2,1)} fusion(bf16[128,1024]{1,0:T(8,128)(2,1)S(1)} %input_grad.3, bf16[128,1024]{1,0:T(8,128)(2,1)S(1)} %input_grad.2), kind=kLoop, calls=%fused_computation | loop fusion | flops 1048576 | bytes 1048576 | tf_op jit(solution)/shard_map/concatenate | solution.py:323
  50.7 2.5 %collective-permute-done.8 = f32[136,128]{1,0:T(8,128)S(1)} collective-permute-done((f32[136,128]{1,0:T(8,128)S(1)}, f32[136,128]{1,0:T(8,128)S(1)}, u32[]{:S(2)}, u32[]{:S(2)}) %collective-permute-start.8) | collective-permute-done | bytes 69664 | tf_op jit(solution)/shard_map/ppermute | solution.py:192
  53.2 0.6 %slice.16 = f32[128,128]{1,0:T(8,128)} slice(f32[136,128]{1,0:T(8,128)S(1)} %add.21), slice={[0:128], [0:128]} | slice | bytes 131072 | tf_op jit(solution)/shard_map/slice | solution.py:324
  53.8 0.6 %slice_bitcast_fusion = f32[128,7]{0,1:T(8,128)} fusion(f32[136,128]{1,0:T(8,128)S(1)} %add.21), kind=kLoop, calls=%fused_computation.2 | loop fusion | bytes 7168 | tf_op jit(solution)/shard_map/transpose | solution.py:324
  (4 shorter events, 0.0 us)
Async XLA Ops:
  0.6 9.5 %copy-start = (bf16[128,2048]{1,0:T(8,128)(2,1)S(1)}, bf16[128,2048]{1,0:T(8,128)(2,1)}, u32[]{:S(2)}) copy-start(bf16[128,2048]{1,0:T(8,128)(2,1)} %x_ref.5) | copy-start | bytes 1572868
  0.6 9.5 %copy-start.1 = (bf16[128,2048]{1,0:T(8,128)(2,1)S(1)}, bf16[128,2048]{1,0:T(8,128)(2,1)}, u32[]{:S(2)}) copy-start(bf16[128,2048]{1,0:T(8,128)(2,1)} %u_ref.5) | copy-start | bytes 1572868
  1.8 8.3 %copy-start.3 = (bf16[128,7]{0,1:T(8,128)(2,1)S(1)}, bf16[128,7]{0,1:T(8,128)(2,1)}, u32[]{:S(2)}) copy-start(bf16[128,7]{0,1:T(8,128)(2,1)} %param.7) | copy-start | bytes 5380
  1.8 13.1 %collective-permute-start = (bf16[128,1024]{1,0:T(8,128)(2,1)S(1)}, bf16[128,1024]{1,0:T(8,128)(2,1)S(1)}, u32[]{:S(2)}, u32[]{:S(2)}) collective-permute-start(bf16[128,1024]{1,0:T(8,128)(2,1)S(1)} %get-tuple-element.21), channel_id=1, source_target_pairs={{0,4},{4,8},{8,12},{12,16},{16,20},{20,24},{24,28},{1,5},{5,9},{9,... | collective-permute-start | bytes 786440 | tf_op jit(solution)/shard_map/ppermute | solution.py:192
  6.7 21.0 %collective-permute-start.3 = (bf16[128,1024]{1,0:T(8,128)(2,1)S(1)}, bf16[128,1024]{1,0:T(8,128)(2,1)S(1)}, u32[]{:S(2)}, u32[]{:S(2)}) collective-permute-start(bf16[128,1024]{1,0:T(8,128)(2,1)S(1)} %get-tuple-element.22), channel_id=1, source_target_pairs={{0,4},{4,8},{8,12},{12,16},{16,20},{20,24},{24,28},{1,5},{5,9},{9,... | collective-permute-start | bytes 786440 | tf_op jit(solution)/shard_map/ppermute | solution.py:192
  10.2 4.7 %copy-start.2 = (bf16[128,128]{1,0:T(8,128)(2,1)S(1)}, bf16[128,128]{1,0:T(8,128)(2,1)}, u32[]{:S(2)}) copy-start(bf16[128,128]{1,0:T(8,128)(2,1)} %m_ref.3) | copy-start | bytes 98308
  12.3 30.5 %collective-permute-start.4 = (bf16[112,1024]{1,0:T(8,128)(2,1)S(1)}, bf16[112,1024]{1,0:T(8,128)(2,1)S(1)}, u32[]{:S(2)}, u32[]{:S(2)}) collective-permute-start(bf16[112,1024]{1,0:T(8,128)(2,1)S(1)} %get-tuple-element.16.cot_ref), channel_id=1, source_target_pairs={{4,0},{8,4},{12,8},{16,12},{20,16},{24,20},{28,24},{5,1},{9,5},{13... | collective-permute-start | bytes 688136 | tf_op jit(solution)/shard_map/ppermute | solution.py:192
  13.6 31.4 %collective-permute-start.1 = (bf16[112,1024]{1,0:T(8,128)(2,1)S(1)}, bf16[112,1024]{1,0:T(8,128)(2,1)S(1)}, u32[]{:S(2)}, u32[]{:S(2)}) collective-permute-start(bf16[112,1024]{1,0:T(8,128)(2,1)S(1)} %get-tuple-element.12.cot_ref), channel_id=1, source_target_pairs={{4,0},{8,4},{12,8},{16,12},{20,16},{24,20},{28,24},{5,1},{9,5},{13... | collective-permute-start | bytes 688136 | tf_op jit(solution)/shard_map/ppermute | solution.py:192
  32.6 5.3 %collective-permute-start.6 = (f32[136,128]{1,0:T(8,128)S(1)}, f32[136,128]{1,0:T(8,128)S(1)}, u32[]{:S(2)}, u32[]{:S(2)}) collective-permute-start(f32[136,128]{1,0:T(8,128)S(1)} %get-tuple-element.20), channel_id=1, source_target_pairs={{0,4},{4,0},{8,12},{12,8},{16,20},{20,16},{24,28},{28,24},{1,5},{5... | collective-permute-start | bytes 208904 | tf_op jit(solution)/shard_map/ppermute | solution.py:192
  35.3 7.5 %collective-permute-start.5 = (bf16[32,1024]{1,0:T(8,128)(2,1)S(1)}, bf16[32,1024]{1,0:T(8,128)(2,1)S(1)}, u32[]{:S(2)}, u32[]{:S(2)}) collective-permute-start(bf16[32,1024]{1,0:T(8,128)(2,1)S(1)} %get-tuple-element.19.edge_ref), channel_id=1, source_target_pairs={{4,0},{8,4},{12,8},{16,12},{20,16},{24,20},{28,24},{5,1},{9,5},{13... | collective-permute-start | bytes 196616 | tf_op jit(solution)/shard_map/ppermute | solution.py:192
  36.6 8.4 %collective-permute-start.2 = (bf16[32,1024]{1,0:T(8,128)(2,1)S(1)}, bf16[32,1024]{1,0:T(8,128)(2,1)S(1)}, u32[]{:S(2)}, u32[]{:S(2)}) collective-permute-start(bf16[32,1024]{1,0:T(8,128)(2,1)S(1)} %get-tuple-element.15.edge_ref), channel_id=1, source_target_pairs={{4,0},{8,4},{12,8},{16,12},{20,16},{24,20},{28,24},{5,1},{9,5},{13... | collective-permute-start | bytes 196616 | tf_op jit(solution)/shard_map/ppermute | solution.py:192
  38.0 9.2 %collective-permute-start.7 = (f32[136,128]{1,0:T(8,128)S(1)}, f32[136,128]{1,0:T(8,128)S(1)}, u32[]{:S(2)}, u32[]{:S(2)}) collective-permute-start(f32[136,128]{1,0:T(8,128)S(1)} %add.19), channel_id=1, source_target_pairs={{0,8},{4,12},{8,0},{12,4},{16,24},{20,28},{24,16},{28,20},{1,9},{5... | collective-permute-start | bytes 208904 | tf_op jit(solution)/shard_map/ppermute | solution.py:192
  47.2 6.0 %collective-permute-start.8 = (f32[136,128]{1,0:T(8,128)S(1)}, f32[136,128]{1,0:T(8,128)S(1)}, u32[]{:S(2)}, u32[]{:S(2)}) collective-permute-start(f32[136,128]{1,0:T(8,128)S(1)} %add.20), channel_id=1, source_target_pairs={{0,16},{4,20},{8,24},{12,28},{16,0},{20,4},{24,8},{28,12},{1,17},{... | collective-permute-start | bytes 208904 | tf_op jit(solution)/shard_map/ppermute | solution.py:192

commit v2 on v1

v2 whole, which is shorter than its diff:
```python
import functools

import jax
import jax.numpy as jnp
from jax import lax
from jax.experimental import pallas as pl
from jax.experimental.pallas import tpu as pltpu
from jax.sharding import PartitionSpec as P

GROUP = 16
ROWS = 16
LANES = 128
F32 = jnp.float32
BF16 = jnp.bfloat16


def iota(shape, dim):
    return lax.broadcasted_iota(jnp.int32, shape, dim)


def split3(values):
    high = values.astype(BF16)
    rest = values - high.astype(F32)
    middle = rest.astype(BF16)
    low = (rest - middle.astype(F32)).astype(BF16)
    return jnp.concatenate([high, middle, low], axis=0)


def exact_dot(values, table):
    rows = values.shape[0]
    out = jnp.dot(split3(values), table, preferred_element_type=F32)
    return out[:rows] + out[rows : 2 * rows] + out[2 * rows :]


def delayed(values, distance):
    return values if distance == 0 else pltpu.roll(values, distance, 0)


def toeplitz(base):
    lanes = base.shape[1]
    blocks = [
        pltpu.roll(
            jnp.broadcast_to(base[g : g + 1], (ROWS, lanes)), 0, 1, stride=1, stride_axis=0
        )
        for g in range(base.shape[0])
    ]
    return jnp.concatenate(blocks, 0).astype(BF16)


def own_group(product, lane_group):
    total = product[:ROWS]
    for g in range(1, product.shape[0] // ROWS):
        total = jnp.where(lane_group == g, product[g * ROWS : (g + 1) * ROWS], total)
    return total


def stacked(first, second, start, stop):
    extent = first.shape[0]
    if stop <= extent:
        return first[start:stop]
    if start >= extent:
        return second[start - extent : stop - extent]
    return jnp.concatenate([first[start:], second[: stop - extent]], 0)


def sum_kernel(taps, factor, first_step, m_ref, st_ref, prev_ref, x_ref, u_ref, *rest):
    sums_in, rest = (rest[0], rest[1:]) if len(rest) == 4 else (None, rest)
    gate_cot_ref, cot_ref, sums_ref = rest
    rows, cols = x_ref.shape
    groups, med = m_ref.shape
    window = med + ROWS
    lanes = med + 128
    tile = LANES // GROUP
    step = pl.program_id(0)
    here = (first_step + step) * groups
    total_groups = sums_ref.shape[0] - 8

    @pl.when(step == 0)
    def _():
        sums_ref[...] = jnp.zeros_like(sums_ref) if sums_in is None else sums_in[...]

    flip = iota((med, lanes), 0) == med - iota((med, lanes), 1)
    base = jnp.dot(m_ref[...], flip.astype(BF16), preferred_element_type=F32)
    spread = iota((st_ref.shape[1], cols), 0) == here + iota((st_ref.shape[1], cols), 1) // GROUP
    wide = jnp.dot(st_ref[...], spread.astype(BF16), preferred_element_type=F32)
    upturn = (iota((rows, rows), 0) ^ (ROWS - 1) == iota((rows, rows), 1)).astype(BF16)
    lane_group = iota((ROWS, 2 * LANES), 1) % LANES // GROUP

    diagonals, short = [], []
    for block in range(cols // LANES):
        at = slice(block * LANES, (block + 1) * LANES)
        prev, x = prev_ref[:, at], x_ref[:, at]
        u = u_ref[:, at].astype(F32)
        near = jnp.concatenate([prev[med - ROWS :], x], 0).astype(F32)
        late = [delayed(near, j)[ROWS:] for j in range(taps)]
        gate = wide[0:1, at] * late[0]
        for j in range(1, taps):
            gate = gate + wide[j : j + 1, at] * late[j]
        cot = (u * gate).astype(BF16)
        cot_ref[ROWS:, at] = cot
        upturned = jnp.dot(upturn, cot, preferred_element_type=F32).astype(BF16)
        table = toeplitz(base[block * tile : (block + 1) * tile])[:, :window]

        pairs = jnp.zeros((tile * ROWS, window), F32)
        gate_cots = []
        for a in range(0, rows // ROWS, 2):
            lo, mid, hi = (ROWS * k for k in (a, a + 1, a + 2))
            part = jnp.concatenate(
                [stacked(prev, x, k, k + window) for k in (lo, mid)], 1
            )
            conv = own_group(jnp.dot(table, part, preferred_element_type=F32), lane_group)
            for k in range(2):
                gate_cots.append(
                    (u[lo + k * ROWS : mid + k * ROWS] * conv[:, k * LANES : (k + 1) * LANES])
                    .astype(BF16)
                )
            both = jnp.concatenate([upturned[lo:mid], upturned[mid:hi]], 1)
            alone = jnp.concatenate(
                [jnp.where(lane_group == g, both, jnp.zeros_like(both)) for g in range(tile)], 0
            )
            pairs = pairs + lax.dot_general(
                alone, part, (((1,), (1,)), ((), ())), preferred_element_type=F32
            )
        gate_cot = jnp.concatenate(gate_cots, 0)
        gate_cot_ref[:, at] = gate_cot
        cot_ref[:ROWS, at] = gate_cot[:ROWS]

        pairs = jnp.concatenate([pairs, jnp.zeros((tile * ROWS, lanes - window), F32)], 1)
        for g in range(tile):
            diagonals.append(
                jnp.sum(
                    pltpu.roll(
                        pairs[g * ROWS : (g + 1) * ROWS], 0, 1, stride=1, stride_axis=0
                    ),
                    0,
                    keepdims=True,
                )
            )
        gate_cot = gate_cot.astype(F32)
        sums = [jnp.sum(gate_cot * late[j], 0, keepdims=True) for j in range(taps)]
        short.append(jnp.concatenate(sums + [jnp.zeros((8 - taps, LANES), F32)], 0))

    flip_back = iota((lanes, med), 0) == med + ROWS - 1 - iota((lanes, med), 1)
    medium = exact_dot(jnp.concatenate(diagonals, 0), flip_back.astype(BF16))
    sums_ref[pl.ds(pl.multiple_of(here, groups), groups), :] = medium * factor
    gather = iota((cols, med), 1) == here + iota((cols, med), 0) // GROUP
    sums_ref[total_groups:, :] += (
        exact_dot(jnp.concatenate(short, 1), gather.astype(BF16)) * factor
    )


def back_kernel(ms_ref, gate_cot_ref, cot_ref, next_ref, *rest):
    out_ref = rest[-1]
    rows, cols = gate_cot_ref.shape
    window = next_ref.shape[0]
    tile = LANES // GROUP
    base = ms_ref[...].astype(F32)
    lane_group = iota((ROWS, 2 * LANES), 1) % LANES // GROUP
    for block in range(cols // LANES):
        at = slice(block * LANES, (block + 1) * LANES)
        table = toeplitz(base[block * tile : (block + 1) * tile])[:, : window + 2 * ROWS]
        cot, after = cot_ref[ROWS:, at], next_ref[ROWS:, at]
        gate_cot, gate_after = gate_cot_ref[:, at], next_ref[:ROWS, at]
        for a in range(0, rows // ROWS, 2):
            sides = []
            for k in (a * ROWS, (a + 1) * ROWS):
                sides.append(
                    jnp.concatenate(
                        [
                            stacked(cot, after, k, k + window),
                            stacked(gate_cot, gate_after, k, k + 2 * ROWS),
                        ],
                        0,
                    )
                )
            product = jnp.dot(
                table, jnp.concatenate(sides, 1), preferred_element_type=F32
            )
            out = own_group(product, lane_group).astype(BF16)
            out_ref[a * ROWS : (a + 1) * ROWS, at] = out[:, :LANES]
            out_ref[(a + 1) * ROWS : (a + 2) * ROWS, at] = out[:, LANES:]


def permuted(block, pairs):
    return lax.ppermute(block, "ctx", pairs)


def local(inputs, upstream, medium_filter, short_filter):
    rows, width = inputs.shape
    groups, med = medium_filter.shape
    taps = short_filter.shape[1]
    devices = lax.axis_size("ctx")
    assert rows % (2 * ROWS) == 0 and rows >= med and med % 128 == 0 and groups <= med
    assert taps <= 8 and width % LANES == 0
    chunks = 2 if width % (4 * LANES) == 0 else 1
    part = width // chunks
    cols = max(c for c in (4 * LANES, 2 * LANES, LANES) if part % c == 0)
    steps = part // cols
    tile = cols // GROUP
    lanes = med + 128
    factor = float(GROUP * rows * devices) ** -0.5
    forward = [(i, i + 1) for i in range(devices - 1)]
    backward = [(i + 1, i) for i in range(devices - 1)]

    def params():
        return pltpu.CompilerParams(vmem_limit_bytes=48 << 20)

    whole = lambda i: (0, 0)
    along = lambda i: (0, i)

    tail = inputs[rows - med :]
    previous = [permuted(tail[:, i * part : (i + 1) * part], forward) for i in range(chunks)]
    short_rows = jnp.pad(short_filter.T, ((0, 8 - taps), (0, 0)))

    gate_cots, cots, following, sums = [], [], [], None
    for k in range(chunks):
        base = k * steps
        shift = lambda i, base=base: (0, base + i)
        in_specs = [
            pl.BlockSpec((tile, med), lambda i, base=base: (base + i, 0)),
            pl.BlockSpec((8, groups), whole),
            pl.BlockSpec((med, cols), along),
            pl.BlockSpec((rows, cols), shift),
            pl.BlockSpec((rows, cols), shift),
        ]
        operands = [medium_filter, short_rows, previous[k], inputs, upstream]
        if k:
            in_specs.append(pl.BlockSpec((groups + 8, med), whole))
            operands.append(sums)
        gate_cot, cot, sums = pl.pallas_call(
            functools.partial(sum_kernel, taps, factor, base),
            grid=(steps,),
            in_specs=in_specs,
            out_specs=[
                pl.BlockSpec((rows, cols), along),
                pl.BlockSpec((rows + ROWS, cols), along),
                pl.BlockSpec((groups + 8, med), whole),
            ],
            out_shape=[
                jax.ShapeDtypeStruct((rows, part), BF16),
                jax.ShapeDtypeStruct((rows + ROWS, part), BF16),
                jax.ShapeDtypeStruct((groups + 8, med), F32),
            ],
            compiler_params=params(),
            name="filter_sums",
        )(*operands)
        gate_cots.append(gate_cot)
        cots.append(cot)
        following.append(permuted(cot[: med + ROWS], backward))

    if devices & (devices - 1):
        sums = lax.psum(sums, "ctx")
    else:
        reach = 1
        while reach < devices:
            sums = sums + permuted(sums, [(i, i ^ reach) for i in range(devices)])
            reach *= 2

    both = jnp.pad(medium_filter, ((0, 0), (0, lanes - med))) + jnp.pad(
        short_filter, ((0, 0), (med + ROWS, lanes - med - ROWS - taps))
    )
    gradient = None
    for k in range(chunks):
        base = k * steps
        in_specs = [
            pl.BlockSpec((tile, lanes), lambda i, base=base: (base + i, 0)),
            pl.BlockSpec((rows, cols), along),
            pl.BlockSpec((rows + ROWS, cols), along),
            pl.BlockSpec((med + ROWS, cols), along),
        ]
        operands = [both, gate_cots[k], cots[k], following[k]]
        if k:
            in_specs.append(pl.BlockSpec(memory_space=pl.ANY))
            operands.append(gradient)
        gradient = pl.pallas_call(
            back_kernel,
            grid=(steps,),
            in_specs=in_specs,
            out_specs=pl.BlockSpec((rows, cols), lambda i, base=base: (0, base + i)),
            out_shape=jax.ShapeDtypeStruct((rows, width), BF16),
            input_output_aliases={4: 0} if k else {},
            compiler_params=params(),
            name="input_grad",
        )(*operands)
    return gradient, sums[:groups], sums[groups : groups + taps, :groups].T


def solution(mesh):
    return jax.shard_map(
        local,
        mesh=mesh,
        in_specs=(P("ctx", "fsdp"), P("ctx", "fsdp"), P("fsdp", None), P("fsdp", None)),
        out_specs=(P("ctx", "fsdp"), P("fsdp", None), P("fsdp", None)),
        check_vma=False,
    )
```

time: 54.7 us -> 51.6 us (0.943)
  Pallas kernels: 16.3 us -> 9.26 us
  waiting for transfers between devices: 10.3 us -> 17.1 us
  starting transfers between devices: 23.5 us -> 20.7 us
  other arithmetic: 0.94 us -> 0.11 us
  local copies, waits for them, and re-layouts: 2.54 us -> 3.3 us
    ppermute x9 -> x7, waiting for transfers between devices: 10.3 us -> 17.1 us  [permuted(): return lax.ppermute(block, 'ctx', pairs)]
    pallas_call x2, Pallas kernels: 9.94 us -> 5.8 us  [local(): pl.pallas_call(functools.partial(sum_kernel, taps, factor, base), grid=(s...]
    pallas_call x3 -> x2, Pallas kernels: 6.35 us -> 3.46 us  [local(): pl.pallas_call(back_kernel, grid=(steps,), in_specs=in_specs, out_specs=p...]
    ppermute x9 -> x7, starting transfers between devices: 23.5 us -> 20.7 us  [permuted(): return lax.ppermute(block, 'ctx', pairs)]
    concatenate x1 -> x0, other arithmetic: 0.83 us -> none  [local(): input_gradient = jnp.concatenate(pieces, axis=1)]
    unnamed x9 -> x11, local copies, waits for them, and re-layouts: 0.16 us -> 0.91 us
  transfers between devices with their start and end apart: 9 -> 7, of which waited for: 2 -> 4; matrix products, arithmetic and copies ran while one was open for 2% -> 3% of each run, Pallas kernels for 30% -> 9%
where the time goes in v2:
time: 51.6 us; the launch traced here: 51.3 us
  starting transfers between devices  20.7 us (40%)
  waiting for transfers between devices  17.1 us (33%)
  Pallas kernels  9.26 us (18%)
  local copies, waits for them, and re-layouts  3.3 us (6%)
  between operations  0.76 us (1%)
    ppermute x7, starting transfers between devices, permuted(): return lax.ppermute(block, 'ctx', pairs)  20.7 us
    ppermute x7, waiting for transfers between devices, permuted(): return lax.ppermute(block, 'ctx', pairs)  17.1 us
    pallas_call x2, Pallas kernels, local(): pl.pallas_call(functools.partial(sum_kernel, taps, factor, base), grid=(s...  5.8 us
    pallas_call x2, Pallas kernels, local(): pl.pallas_call(back_kernel, grid=(steps,), in_specs=in_specs, out_specs=p...  3.46 us
    slice x1, local copies, waits for them, and re-layouts, local(): tail[:, i * part:(i + 1) * part]  1.15 us
  transfers between devices with their start and end apart: 7, of which 4 were waited for; matrix products, arithmetic and copies ran while one was open for 3% of the time, Pallas kernels for 9%

profile of v2, /device:TPU:0, one launch (start us, length us, event | category | flops | bytes accessed | tf_op | source)
XLA Modules:
  0.0 51.3 jit_solution(2071027287237966741)
XLA Ops:
  0.6 0.0 copy-start
  0.6 0.0 copy-start.1
  0.6 1.2 %fusion = (bf16[128,1024]{1,0:T(8,128)(2,1)S(1)}, bf16[128,1024]{1,0:T(8,128)(2,1)S(1)}) fusion(bf16[128,2048]{1,0:T(8,128)(2,1)} %x_ref.3), kind=kLoop, calls=%fused_computation.2 | loop fusion | bytes 1048576 | tf_op jit(solution)/shard_map/slice | solution.py:212
  1.8 0.0 copy-start.4
  1.8 4.9 %collective-permute-start.1 = (bf16[128,1024]{1,0:T(8,128)(2,1)S(1)}, bf16[128,1024]{1,0:T(8,128)(2,1)S(1)}, u32[]{:S(2)}, u32[]{:S(2)}) collective-permute-start(bf16[128,1024]{1,0:T(8,128)(2,1)S(1)} %get-tuple-element.15), channel_id=1, source_target_pairs={{0,4},{4,8},{8,12},{12,16},{16,20},{20,24},{24,28},{1,5},{5,9},{9,... | collective-permute-start | bytes 786440 | tf_op jit(solution)/shard_map/ppermute | solution.py:185
  6.7 3.5 %collective-permute-start = (bf16[128,1024]{1,0:T(8,128)(2,1)S(1)}, bf16[128,1024]{1,0:T(8,128)(2,1)S(1)}, u32[]{:S(2)}, u32[]{:S(2)}) collective-permute-start(bf16[128,1024]{1,0:T(8,128)(2,1)S(1)} %get-tuple-element.16), channel_id=1, source_target_pairs={{0,4},{4,8},{8,12},{12,16},{16,20},{20,24},{24,28},{1,5},{5,9},{9,... | collective-permute-start | bytes 786440 | tf_op jit(solution)/shard_map/ppermute | solution.py:185
  10.1 0.0 copy-done.4
  10.2 3.2 %collective-permute-done.1.prev_ref = bf16[128,1024]{1,0:T(8,128)(2,1)S(1)} collective-permute-done((bf16[128,1024]{1,0:T(8,128)(2,1)S(1)}, bf16[128,1024]{1,0:T(8,128)(2,1)S(1)}, u32[]{:S(2)}, u32[]{:S(2)}) %collective-permute-start.1) | collective-permute-done | bytes 262176 | tf_op jit(solution)/shard_map/ppermute | solution.py:185
  13.4 0.0 copy-done
  13.4 0.0 copy-done.1
  13.4 0.0 copy-start.2
  13.4 0.8 %copy-done.2 = bf16[128,128]{1,0:T(8,128)(2,1)S(1)} copy-done((bf16[128,128]{1,0:T(8,128)(2,1)S(1)}, bf16[128,128]{1,0:T(8,128)(2,1)}, u32[]{:S(2)}) %copy-start.2) | copy-done | bytes 32792
  14.1 2.9 %filter_sums.2 = (bf16[128,1024]{1,0:T(8,128)(2,1)S(1)}, bf16[144,1024]{1,0:T(8,128)(2,1)S(1)}, f32[136,128]{1,0:T(8,128)S(1)}) custom-call(bf16[128,128]{1,0:T(8,128)(2,1)S(1)} %copy-done.2, bf16[8,128]{1,0:T(8,128)(2,1)S(1)} %pad.14.st_ref, bf16[128,1024]{1,0:T(8,128)(2,1)S(1)} %collective-permute-done.1.prev_ref, bf16[128,2048]{1,0:T(8,128)(2,1)S(1)} %copy-done, ...), custom_call_target="tpu_custom_call" | custom-call | tf_op jit(solution)/shard_map/filter_sums/pallas_call | solution.py:230
  17.0 0.8 %collective-permute-done.prev_ref = bf16[128,1024]{1,0:T(8,128)(2,1)S(1)} collective-permute-done((bf16[128,1024]{1,0:T(8,128)(2,1)S(1)}, bf16[128,1024]{1,0:T(8,128)(2,1)S(1)}, u32[]{:S(2)}, u32[]{:S(2)}) %collective-permute-start) | collective-permute-done | bytes 262176 | tf_op jit(solution)/shard_map/ppermute | solution.py:185
  17.8 2.9 %filter_sums.3 = (bf16[128,1024]{1,0:T(8,128)(2,1)S(1)}, bf16[144,1024]{1,0:T(8,128)(2,1)S(1)}, f32[136,128]{1,0:T(8,128)S(1)}) custom-call(bf16[128,128]{1,0:T(8,128)(2,1)S(1)} %copy-done.2, bf16[8,128]{1,0:T(8,128)(2,1)S(1)} %pad.14.st_ref, bf16[128,1024]{1,0:T(8,128)(2,1)S(1)} %collective-permute-done.prev_ref, bf16[128,2048]{1,0:T(8,128)(2,1)S(1)} %copy-done, ...), custom_call_target="tpu_custom_call" | custom-call | tf_op jit(solution)/shard_map/filter_sums/pallas_call | solution.py:230
  20.8 2.5 %collective-permute-start.4 = (f32[136,128]{1,0:T(8,128)S(1)}, f32[136,128]{1,0:T(8,128)S(1)}, u32[]{:S(2)}, u32[]{:S(2)}) collective-permute-start(f32[136,128]{1,0:T(8,128)S(1)} %get-tuple-element.14), channel_id=1, source_target_pairs={{0,4},{4,0},{8,12},{12,8},{16,20},{20,16},{24,28},{28,24},{1,5},{5... | collective-permute-start | bytes 208904 | tf_op jit(solution)/shard_map/ppermute | solution.py:185
  23.3 2.3 %collective-permute-done.4 = f32[136,128]{1,0:T(8,128)S(1)} collective-permute-done((f32[136,128]{1,0:T(8,128)S(1)}, f32[136,128]{1,0:T(8,128)S(1)}, u32[]{:S(2)}, u32[]{:S(2)}) %collective-permute-start.4) | collective-permute-done | bytes 69664 | tf_op jit(solution)/shard_map/ppermute | solution.py:185
  25.6 3.1 %collective-permute-start.5 = (f32[136,128]{1,0:T(8,128)S(1)}, f32[136,128]{1,0:T(8,128)S(1)}, u32[]{:S(2)}, u32[]{:S(2)}) collective-permute-start(f32[136,128]{1,0:T(8,128)S(1)} %add.19), channel_id=1, source_target_pairs={{0,8},{4,12},{8,0},{12,4},{16,24},{20,28},{24,16},{28,20},{1,9},{5... | collective-permute-start | bytes 208904 | tf_op jit(solution)/shard_map/ppermute | solution.py:185
  28.7 0.1 copy.8
  28.8 1.3 %collective-permute-start.3 = (bf16[144,1024]{1,0:T(8,128)(2,1)S(1)}, bf16[144,1024]{1,0:T(8,128)(2,1)S(1)}, u32[]{:S(2)}, u32[]{:S(2)}) collective-permute-start(bf16[144,1024]{1,0:T(8,128)(2,1)S(1)} %get-tuple-element.13.cot_ref), channel_id=1, source_target_pairs={{4,0},{8,4},{12,8},{16,12},{20,16},{24,20},{28,24},{5,1},{9,5},{13... | collective-permute-start | bytes 884744 | tf_op jit(solution)/shard_map/ppermute | solution.py:185
  30.1 0.0 copy-start.3
  30.1 1.3 %collective-permute-start.2 = (bf16[144,1024]{1,0:T(8,128)(2,1)S(1)}, bf16[144,1024]{1,0:T(8,128)(2,1)S(1)}, u32[]{:S(2)}, u32[]{:S(2)}) collective-permute-start(bf16[144,1024]{1,0:T(8,128)(2,1)S(1)} %get-tuple-element.11.cot_ref), channel_id=1, source_target_pairs={{4,0},{8,4},{12,8},{16,12},{20,16},{24,20},{28,24},{5,1},{9,5},{13... | collective-permute-start | bytes 884744 | tf_op jit(solution)/shard_map/ppermute | solution.py:185
  31.4 0.0 collective-permute-done.5
  31.4 4.2 %collective-permute-start.6 = (f32[136,128]{1,0:T(8,128)S(1)}, f32[136,128]{1,0:T(8,128)S(1)}, u32[]{:S(2)}, u32[]{:S(2)}) collective-permute-start(f32[136,128]{1,0:T(8,128)S(1)} %add.20), channel_id=1, source_target_pairs={{0,16},{4,20},{8,24},{12,28},{16,0},{20,4},{24,8},{28,12},{1,17},{... | collective-permute-start | bytes 208904 | tf_op jit(solution)/shard_map/ppermute | solution.py:185
  35.7 0.0 copy-done.3
  35.7 0.1 pad_add_fusion.ms_ref
  35.8 10.8 %collective-permute-done.6 = f32[136,128]{1,0:T(8,128)S(1)} collective-permute-done((f32[136,128]{1,0:T(8,128)S(1)}, f32[136,128]{1,0:T(8,128)S(1)}, u32[]{:S(2)}, u32[]{:S(2)}) %collective-permute-start.6) | collective-permute-done | bytes 69664 | tf_op jit(solution)/shard_map/ppermute | solution.py:185
  46.6 0.6 %slice.16 = f32[128,128]{1,0:T(8,128)} slice(f32[136,128]{1,0:T(8,128)S(1)} %add.21), slice={[0:128], [0:128]} | slice | bytes 131072 | tf_op jit(solution)/shard_map/slice | solution.py:285
  47.2 0.6 %slice_bitcast_fusion = f32[128,7]{0,1:T(8,128)} fusion(f32[136,128]{1,0:T(8,128)S(1)} %add.21), kind=kLoop, calls=%fused_computation.1 | loop fusion | bytes 7168 | tf_op jit(solution)/shard_map/transpose | solution.py:285
  47.8 0.0 collective-permute-done.3.next_ref
  47.8 1.7 %input_grad.2.rest_0_ = bf16[128,2048]{1,0:T(8,128)(2,1)} custom-call(bf16[128,256]{1,0:T(8,128)(2,1)S(1)} %pad_add_fusion.ms_ref, bf16[128,1024]{1,0:T(8,128)(2,1)S(1)} %get-tuple-element.12.gate_cot_ref, bf16[144,1024]{1,0:T(8,128)(2,1)S(1)} %get-tuple-element.13.cot_ref, bf16[144,1024]{1,0:T(8,128)(2,1)S(1)} %collective-permute-done.3.next_ref), custom_call_target="tpu_custom_call" | custom-call | tf_op jit(solution)/shard_map/input_grad/pallas_call | solution.py:275
  49.5 0.0 collective-permute-done.2.next_ref
  49.5 1.7 %input_grad.3 = bf16[128,2048]{1,0:T(8,128)(2,1)} custom-call(bf16[128,256]{1,0:T(8,128)(2,1)S(1)} %pad_add_fusion.ms_ref, bf16[128,1024]{1,0:T(8,128)(2,1)S(1)} %get-tuple-element.10.gate_cot_ref, bf16[144,1024]{1,0:T(8,128)(2,1)S(1)} %get-tuple-element.11.cot_ref, ...), custom_call_target="tpu_custom_call", output_to_operand_aliasing={{}: (4, {})} | custom-call | tf_op jit(solution)/shard_map/input_grad/pallas_call | solution.py:275
  (4 shorter events, 0.0 us)
Async XLA Ops:
  0.6 12.7 %copy-start = (bf16[128,2048]{1,0:T(8,128)(2,1)S(1)}, bf16[128,2048]{1,0:T(8,128)(2,1)}, u32[]{:S(2)}) copy-start(bf16[128,2048]{1,0:T(8,128)(2,1)} %x_ref.3) | copy-start | bytes 1572868
  0.6 12.7 %copy-start.1 = (bf16[128,2048]{1,0:T(8,128)(2,1)S(1)}, bf16[128,2048]{1,0:T(8,128)(2,1)}, u32[]{:S(2)}) copy-start(bf16[128,2048]{1,0:T(8,128)(2,1)} %u_ref.3) | copy-start | bytes 1572868
  1.8 8.3 %copy-start.4 = (bf16[128,7]{0,1:T(8,128)(2,1)S(1)}, bf16[128,7]{0,1:T(8,128)(2,1)}, u32[]{:S(2)}) copy-start(bf16[128,7]{0,1:T(8,128)(2,1)} %param.7) | copy-start | bytes 5380
  1.8 11.5 %collective-permute-start.1 = (bf16[128,1024]{1,0:T(8,128)(2,1)S(1)}, bf16[128,1024]{1,0:T(8,128)(2,1)S(1)}, u32[]{:S(2)}, u32[]{:S(2)}) collective-permute-start(bf16[128,1024]{1,0:T(8,128)(2,1)S(1)} %get-tuple-element.15), channel_id=1, source_target_pairs={{0,4},{4,8},{8,12},{12,16},{16,20},{20,24},{24,28},{1,5},{5,9},{9,... | collective-permute-start | bytes 786440 | tf_op jit(solution)/shard_map/ppermute | solution.py:185
  6.7 11.1 %collective-permute-start = (bf16[128,1024]{1,0:T(8,128)(2,1)S(1)}, bf16[128,1024]{1,0:T(8,128)(2,1)S(1)}, u32[]{:S(2)}, u32[]{:S(2)}) collective-permute-start(bf16[128,1024]{1,0:T(8,128)(2,1)S(1)} %get-tuple-element.16), channel_id=1, source_target_pairs={{0,4},{4,8},{8,12},{12,16},{16,20},{20,24},{24,28},{1,5},{5,9},{9,... | collective-permute-start | bytes 786440 | tf_op jit(solution)/shard_map/ppermute | solution.py:185
  13.4 0.8 %copy-start.2 = (bf16[128,128]{1,0:T(8,128)(2,1)S(1)}, bf16[128,128]{1,0:T(8,128)(2,1)}, u32[]{:S(2)}) copy-start(bf16[128,128]{1,0:T(8,128)(2,1)} %m_ref.3) | copy-start | bytes 98308
  20.8 4.8 %collective-permute-start.4 = (f32[136,128]{1,0:T(8,128)S(1)}, f32[136,128]{1,0:T(8,128)S(1)}, u32[]{:S(2)}, u32[]{:S(2)}) collective-permute-start(f32[136,128]{1,0:T(8,128)S(1)} %get-tuple-element.14), channel_id=1, source_target_pairs={{0,4},{4,0},{8,12},{12,8},{16,20},{20,16},{24,28},{28,24},{1,5},{5... | collective-permute-start | bytes 208904 | tf_op jit(solution)/shard_map/ppermute | solution.py:185
  25.6 5.8 %collective-permute-start.5 = (f32[136,128]{1,0:T(8,128)S(1)}, f32[136,128]{1,0:T(8,128)S(1)}, u32[]{:S(2)}, u32[]{:S(2)}) collective-permute-start(f32[136,128]{1,0:T(8,128)S(1)} %add.19), channel_id=1, source_target_pairs={{0,8},{4,12},{8,0},{12,4},{16,24},{20,28},{24,16},{28,20},{1,9},{5... | collective-permute-start | bytes 208904 | tf_op jit(solution)/shard_map/ppermute | solution.py:185
  28.8 19.0 %collective-permute-start.3 = (bf16[144,1024]{1,0:T(8,128)(2,1)S(1)}, bf16[144,1024]{1,0:T(8,128)(2,1)S(1)}, u32[]{:S(2)}, u32[]{:S(2)}) collective-permute-start(bf16[144,1024]{1,0:T(8,128)(2,1)S(1)} %get-tuple-element.13.cot_ref), channel_id=1, source_target_pairs={{4,0},{8,4},{12,8},{16,12},{20,16},{24,20},{28,24},{5,1},{9,5},{13... | collective-permute-start | bytes 884744 | tf_op jit(solution)/shard_map/ppermute | solution.py:185
  30.1 5.6 %copy-start.3 = (bf16[128,128]{1,0:T(8,128)(2,1)S(1)}, bf16[128,128]{1,0:T(8,128)(2,1)}, u32[]{:S(2)}) copy-start(bf16[128,128]{1,0:T(8,128)(2,1)} %m_ref.3) | copy-start | bytes 98308
  30.1 19.4 %collective-permute-start.2 = (bf16[144,1024]{1,0:T(8,128)(2,1)S(1)}, bf16[144,1024]{1,0:T(8,128)(2,1)S(1)}, u32[]{:S(2)}, u32[]{:S(2)}) collective-permute-start(bf16[144,1024]{1,0:T(8,128)(2,1)S(1)} %get-tuple-element.11.cot_ref), channel_id=1, source_target_pairs={{4,0},{8,4},{12,8},{16,12},{20,16},{24,20},{28,24},{5,1},{9,5},{13... | collective-permute-start | bytes 884744 | tf_op jit(solution)/shard_map/ppermute | solution.py:185
  31.4 15.1 %collective-permute-start.6 = (f32[136,128]{1,0:T(8,128)S(1)}, f32[136,128]{1,0:T(8,128)S(1)}, u32[]{:S(2)}, u32[]{:S(2)}) collective-permute-start(f32[136,128]{1,0:T(8,128)S(1)} %add.20), channel_id=1, source_target_pairs={{0,16},{4,20},{8,24},{12,28},{16,0},{20,4},{24,8},{28,12},{1,17},{... | collective-permute-start | bytes 208904 | tf_op jit(solution)/shard_map/ppermute | solution.py:185

commit v3 on v2

v3 whole, which is shorter than its diff:
```python
import functools

import jax
import jax.numpy as jnp
from jax import lax
from jax.experimental import pallas as pl
from jax.experimental.pallas import tpu as pltpu
from jax.sharding import PartitionSpec as P

GROUP = 16
ROWS = 16
LANES = 128
F32 = jnp.float32
BF16 = jnp.bfloat16
SMALL = pl.CostEstimate(flops=1, bytes_accessed=1, transcendentals=0)


def iota(shape, dim):
    return lax.broadcasted_iota(jnp.int32, shape, dim)


def split3(values):
    high = values.astype(BF16)
    rest = values - high.astype(F32)
    middle = rest.astype(BF16)
    low = (rest - middle.astype(F32)).astype(BF16)
    return jnp.concatenate([high, middle, low], axis=0)


def exact_dot(values, table):
    rows = values.shape[0]
    out = jnp.dot(split3(values), table, preferred_element_type=F32)
    return out[:rows] + out[rows : 2 * rows] + out[2 * rows :]


def delayed(values, distance):
    return values if distance == 0 else pltpu.roll(values, distance, 0)


def toeplitz(base):
    lanes = base.shape[1]
    blocks = [
        pltpu.roll(
            jnp.broadcast_to(base[g : g + 1], (ROWS, lanes)), 0, 1, stride=1, stride_axis=0
        )
        for g in range(base.shape[0])
    ]
    return jnp.concatenate(blocks, 0).astype(BF16)


def own_group(product, lane_group):
    total = product[:ROWS]
    for g in range(1, product.shape[0] // ROWS):
        total = jnp.where(lane_group == g, product[g * ROWS : (g + 1) * ROWS], total)
    return total


def stacked(first, second, start, stop):
    extent = first.shape[0]
    if stop <= extent:
        return first[start:stop]
    if start >= extent:
        return second[start - extent : stop - extent]
    return jnp.concatenate([first[start:], second[: stop - extent]], 0)


def masked(cots, lane_group):
    return jnp.concatenate(
        [
            jnp.where(lane_group == g, cots, jnp.zeros_like(cots))
            for g in range(LANES // GROUP)
        ],
        0,
    )


def contracted(alone, part):
    return lax.dot_general(
        alone, part, (((1,), (1,)), ((), ())), preferred_element_type=F32
    )


def diagonal_sums(pairs, lanes):
    if pairs.shape[1] < lanes:
        pad = jnp.zeros((pairs.shape[0], lanes - pairs.shape[1]), F32)
        pairs = jnp.concatenate([pairs, pad], 1)
    return [
        jnp.sum(
            pltpu.roll(pairs[g * ROWS : (g + 1) * ROWS], 0, 1, stride=1, stride_axis=0),
            0,
            keepdims=True,
        )
        for g in range(LANES // GROUP)
    ]


def medium_sums(diagonals, med, lanes):
    flip_back = iota((lanes, med), 0) == med + ROWS - 1 - iota((lanes, med), 1)
    return exact_dot(jnp.concatenate(diagonals, 0), flip_back.astype(BF16))


def turning(extent):
    return (iota((extent, extent), 0) ^ (ROWS - 1) == iota((extent, extent), 1)).astype(BF16)


def gated(wide, near, taps):
    gate = wide[0:1] * near[ROWS:]
    for j in range(1, taps):
        gate = gate + wide[j : j + 1] * delayed(near, j)[ROWS:]
    return gate


def lane_groups():
    return iota((ROWS, 2 * LANES), 1) % LANES // GROUP


def own_kernel(taps, pieces, m_ref, st_ref, x_ref, u_ref, *outs):
    *send_refs, turned_ref, conv_ref, medium_ref, table_ref, wide_ref, made = outs
    rows, cols = x_ref.shape
    groups, med = m_ref.shape
    window = med + ROWS
    lanes = med + 128
    tile = LANES // GROUP
    first = pl.program_id(0) * groups

    flip = iota((med, lanes), 0) == med - iota((med, lanes), 1)
    base = jnp.dot(m_ref[...], flip.astype(BF16), preferred_element_type=F32)
    spread = iota((st_ref.shape[1], cols), 0) == first + iota((st_ref.shape[1], cols), 1) // GROUP
    wide_ref[...] = jnp.dot(st_ref[...], spread.astype(BF16), preferred_element_type=F32)
    made[rows - ROWS : rows, :] = x_ref[:ROWS, :]
    made[rows:, :] = u_ref[:ROWS, :]
    upturn = turning(rows)
    lane_group = lane_groups()

    diagonals = []
    for block in range(cols // LANES):
        at = slice(block * LANES, (block + 1) * LANES)
        x = x_ref[:, at]
        near = jnp.concatenate([jnp.zeros((ROWS, LANES), F32), x.astype(F32)], 0)
        cot = (u_ref[:, at].astype(F32) * gated(wide_ref[:, at], near, taps)).astype(BF16)
        made[: rows - ROWS, at] = cot[ROWS:]
        turned = jnp.dot(upturn, cot, preferred_element_type=F32).astype(BF16)
        turned_ref[:, at] = turned
        table = toeplitz(base[block * tile : (block + 1) * tile])
        table_ref[block * LANES : (block + 1) * LANES, :] = table

        pairs = jnp.zeros((LANES, window), F32)
        for a in range(0, rows // ROWS, 2):
            lo, mid, hi = (ROWS * k for k in (a, a + 1, a + 2))
            empty = jnp.zeros((med - lo, LANES), BF16)
            part = jnp.concatenate(
                [
                    jnp.concatenate([empty, x[:mid]], 0),
                    jnp.concatenate([empty, x[ROWS:hi]], 0),
                ],
                1,
            )
            conv = own_group(
                jnp.dot(table[:, :window], part, preferred_element_type=F32), lane_group
            )
            conv_ref[lo:mid, at] = conv[:, :LANES]
            conv_ref[mid:hi, at] = conv[:, LANES:]
            if a:
                both = jnp.concatenate([turned[lo:mid], turned[mid:hi]], 1)
                pairs = pairs + contracted(masked(both, lane_group), part)
        diagonals += diagonal_sums(pairs, lanes)
    medium_ref[...] = medium_sums(diagonals, med, lanes)

    step = pl.program_id(0)
    for send_ref, (start, count) in zip(send_refs, pieces):

        @pl.when(jnp.logical_and(step >= start, step < start + count))
        def _(send_ref=send_ref):
            send_ref[...] = made[...]


def halo_kernel(taps, factor, table_ref, wide_ref, prev_ref, x_ref, u_ref, turned_ref,
                conv_ref, medium_ref, *rest):
    gate_cot_ref, sums_ref = rest[:2] if len(rest) == 2 else rest[1:3]
    rows, cols = x_ref.shape
    med = prev_ref.shape[0]
    groups = medium_ref.shape[0]
    window = med + ROWS
    lanes = med + 128
    step = pl.program_id(0)
    first = step * groups
    total_groups = sums_ref.shape[0] - 8

    @pl.when(step == 0)
    def _():
        sums_ref[total_groups:, :] = jnp.zeros((8, med), F32)

    upturn = turning(ROWS)
    lane_group = lane_groups()
    diagonals, short = [], []
    for block in range(cols // LANES):
        at = slice(block * LANES, (block + 1) * LANES)
        prev, x, u = prev_ref[:, at], x_ref[:, at], u_ref[:, at]
        near = jnp.concatenate([prev[med - ROWS :], x], 0).astype(F32)
        table = table_ref[block * LANES : (block + 1) * LANES, :]
        head = gated(wide_ref[:, at], near[: 2 * ROWS], taps) * u[:ROWS].astype(F32)
        head = head.astype(BF16)
        gate_cot_ref[:ROWS, at] = head
        head = jnp.dot(upturn, head, preferred_element_type=F32).astype(BF16)

        pairs = None
        gate_cots = []
        for a in range(0, rows // ROWS, 2):
            lo, mid, hi = (ROWS * k for k in (a, a + 1, a + 2))
            if a and med <= lo:
                conv = jnp.zeros((ROWS, 2 * LANES), F32)
            else:
                part = jnp.concatenate(
                    [stacked(prev, x, lo, med), stacked(prev, x, mid, med + ROWS)], 1
                )
                conv = own_group(
                    jnp.dot(table[:, : med - lo], part, preferred_element_type=F32),
                    lane_group,
                )
                if a == 0:
                    part = jnp.concatenate([part, jnp.concatenate([x[:ROWS], x[ROWS:hi]], 1)], 0)
                    both = jnp.concatenate([head, turned_ref[mid:hi, at]], 1)
                else:
                    both = jnp.concatenate([turned_ref[lo:mid, at], turned_ref[mid:hi, at]], 1)
                more = contracted(masked(both, lane_group), part)
                if more.shape[1] < window:
                    more = jnp.concatenate(
                        [more, jnp.zeros((LANES, window - more.shape[1]), F32)], 1
                    )
                pairs = more if pairs is None else pairs + more
            for k in range(2):
                here = slice(lo + k * ROWS, mid + k * ROWS)
                whole = conv_ref[here, at] + conv[:, k * LANES : (k + 1) * LANES]
                gate_cots.append((u[here].astype(F32) * whole).astype(BF16))
        gate_cot = jnp.concatenate(gate_cots, 0)
        gate_cot_ref[ROWS:, at] = gate_cot
        diagonals += diagonal_sums(pairs, lanes)
        gate_cot = gate_cot.astype(F32)
        sums = [
            jnp.sum(gate_cot * delayed(near, j)[ROWS:], 0, keepdims=True) for j in range(taps)
        ]
        short.append(jnp.concatenate(sums + [jnp.zeros((8 - taps, LANES), F32)], 0))

    medium = medium_ref[...] + medium_sums(diagonals, med, lanes)
    sums_ref[pl.ds(pl.multiple_of(first, groups), groups), :] = medium * factor
    gather = iota((cols, med), 1) == first + iota((cols, med), 0) // GROUP
    sums_ref[total_groups:, :] += (
        exact_dot(jnp.concatenate(short, 1), gather.astype(BF16)) * factor
    )


def back_kernel(taps, ms_ref, table_ref, wide_ref, x_ref, gate_cot_ref, cot_ref, next_ref, *rest):
    out_ref = rest[-1]
    rows, cols = x_ref.shape
    window = table_ref.shape[1] - 128 + ROWS
    tile = LANES // GROUP
    base = ms_ref[...].astype(F32)
    lane_group = lane_groups()
    for block in range(cols // LANES):
        at = slice(block * LANES, (block + 1) * LANES)
        forward = table_ref[block * LANES : (block + 1) * LANES, :window]
        table = toeplitz(base[block * tile : (block + 1) * tile])[:, : window + 2 * ROWS]
        x, x_next = x_ref[:, at], next_ref[rows - ROWS : rows, at]
        u_next = next_ref[rows:, at].astype(F32)
        near = jnp.concatenate([x[rows - ROWS :], x_next], 0).astype(F32)
        head = (u_next * gated(wide_ref[:, at], near, taps)).astype(BF16)
        part = jnp.concatenate([x[rows + ROWS - window :], x_next], 0)
        conv = jnp.dot(forward, part, preferred_element_type=F32)
        gate_after = (u_next * own_group(conv, lane_group[:, :LANES])).astype(BF16)
        cot = jnp.concatenate([gate_cot_ref[:ROWS, at], cot_ref[: rows - ROWS, at]], 0)
        after = jnp.concatenate([head, next_ref[: rows - ROWS, at]], 0)
        gate_cot = gate_cot_ref[ROWS:, at]
        for a in range(0, rows // ROWS, 2):
            sides = [
                jnp.concatenate(
                    [
                        stacked(cot, after, k, k + window),
                        stacked(gate_cot, gate_after, k, k + 2 * ROWS),
                    ],
                    0,
                )
                for k in (a * ROWS, (a + 1) * ROWS)
            ]
            product = jnp.dot(
                table, jnp.concatenate(sides, 1), preferred_element_type=F32
            )
            out = own_group(product, lane_group).astype(BF16)
            out_ref[a * ROWS : (a + 1) * ROWS, at] = out[:, :LANES]
            out_ref[(a + 1) * ROWS : (a + 2) * ROWS, at] = out[:, LANES:]


def add_kernel(own_ref, other_ref, held_ref, out_ref, held_out_ref):
    out_ref[...] = own_ref[...] + other_ref[...]


def add_after(own, other, held):
    return pl.pallas_call(
        add_kernel,
        in_specs=[pl.BlockSpec(own.shape, lambda: (0, 0))] * 2
        + [pl.BlockSpec(memory_space=pl.ANY)],
        out_specs=[
            pl.BlockSpec(own.shape, lambda: (0, 0)),
            pl.BlockSpec(memory_space=pl.ANY),
        ],
        out_shape=[
            jax.ShapeDtypeStruct(own.shape, own.dtype),
            jax.ShapeDtypeStruct(held.shape, held.dtype),
        ],
        input_output_aliases={2: 1},
        compiler_params=pltpu.CompilerParams(vmem_limit_bytes=16 << 20),
        cost_estimate=SMALL,
        name="add_sums",
    )(own, other, held)


def finish_kernel(groups, taps, own_ref, other_ref, held_ref, medium_ref, short_ref, held_out_ref):
    total = own_ref[...] + other_ref[...]
    medium_ref[...] = total[:groups]
    short_ref[...] = total[groups : groups + taps, :groups]


def finish(own, other, held, groups, taps):
    lanes = own.shape[1]
    return pl.pallas_call(
        functools.partial(finish_kernel, groups, taps),
        in_specs=[pl.BlockSpec(own.shape, lambda: (0, 0))] * 2
        + [pl.BlockSpec(memory_space=pl.ANY)],
        out_specs=[
            pl.BlockSpec((groups, lanes), lambda: (0, 0)),
            pl.BlockSpec((taps, groups), lambda: (0, 0)),
            pl.BlockSpec(memory_space=pl.ANY),
        ],
        out_shape=[
            jax.ShapeDtypeStruct((groups, lanes), own.dtype),
            jax.ShapeDtypeStruct((taps, groups), own.dtype),
            jax.ShapeDtypeStruct(held.shape, held.dtype),
        ],
        input_output_aliases={2: 2},
        compiler_params=pltpu.CompilerParams(vmem_limit_bytes=16 << 20),
        cost_estimate=SMALL,
        name="finish_sums",
    )(own, other, held)


def permuted(block, pairs):
    return lax.ppermute(block, "ctx", pairs)


def local(inputs, upstream, medium_filter, short_filter):
    rows, width = inputs.shape
    groups, med = medium_filter.shape
    taps = short_filter.shape[1]
    devices = lax.axis_size("ctx")
    assert rows == med and med % 128 == 0 and groups <= med
    assert taps <= 8 and width % LANES == 0
    steps = 4 if width % (4 * LANES) == 0 else 1
    cols = width // steps
    tile = cols // GROUP
    lanes = med + 128
    factor = float(GROUP * rows * devices) ** -0.5
    forward = [(i, i + 1) for i in range(devices - 1)]
    backward = [(i + 1, i) for i in range(devices - 1)]

    def params(mebibytes=40):
        return pltpu.CompilerParams(vmem_limit_bytes=mebibytes << 20)

    def block(extent, base=0):
        return pl.BlockSpec((extent, cols), lambda i: (0, base + i))

    def filters(extent, base=0):
        return pl.BlockSpec((tile, extent), lambda i: (base + i, 0))

    def tables(extent, base=0):
        return pl.BlockSpec((tile * ROWS, extent), lambda i: (base + i, 0))

    short_rows = jnp.pad(short_filter.T, ((0, 8 - taps), (0, 0)))
    previous = permuted(inputs, forward)
    pieces = [(0, 2), (2, 1), (3, 1)] if steps == 4 else [(0, 1)]
    *sends, turned, conv, medium, table, wide = pl.pallas_call(
        functools.partial(own_kernel, taps, pieces),
        grid=(steps,),
        in_specs=[
            filters(med),
            pl.BlockSpec((8, groups), lambda i: (0, 0)),
            block(rows),
            block(rows),
        ],
        out_specs=[
            pl.BlockSpec(
                (rows + ROWS, cols),
                lambda i, start=start, count=count: (0, jnp.clip(i - start, 0, count - 1)),
            )
            for start, count in pieces
        ]
        + [
            block(rows),
            block(rows),
            filters(med),
            tables(lanes),
            block(8),
        ],
        out_shape=[
            jax.ShapeDtypeStruct((rows + ROWS, count * cols), BF16) for _, count in pieces
        ]
        + [
            jax.ShapeDtypeStruct((rows, width), BF16),
            jax.ShapeDtypeStruct((rows, width), F32),
            jax.ShapeDtypeStruct((groups, med), F32),
            jax.ShapeDtypeStruct((groups * ROWS, lanes), BF16),
            jax.ShapeDtypeStruct((8, width), F32),
        ],
        scratch_shapes=[pltpu.VMEM((rows + ROWS, cols), BF16)],
        compiler_params=params(),
        cost_estimate=SMALL,
        name="own_block",
    )(medium_filter, short_rows, inputs, upstream)
    following = [permuted(sends[0], backward)]

    halo_in = [table, wide, previous, inputs, upstream, turned, conv, medium]
    halo_specs = [
        tables(med),
        block(8),
        block(med),
        block(rows),
        block(rows),
        block(rows),
        block(rows),
        filters(med),
    ]
    halo_out = [
        jax.ShapeDtypeStruct((rows + ROWS, width), BF16),
        jax.ShapeDtypeStruct((groups + 8, med), F32),
    ]
    halo_out_specs = [block(rows + ROWS), pl.BlockSpec((groups + 8, med), lambda i: (0, 0))]
    held = sends[1:2]
    gate_cot, sums, *held = pl.pallas_call(
        functools.partial(halo_kernel, taps, factor),
        grid=(steps,),
        in_specs=halo_specs + [pl.BlockSpec(memory_space=pl.ANY)] * len(held),
        out_specs=halo_out_specs + [pl.BlockSpec(memory_space=pl.ANY)] * len(held),
        out_shape=halo_out + [jax.ShapeDtypeStruct(h.shape, h.dtype) for h in held],
        input_output_aliases={8: 2} if held else {},
        compiler_params=params(),
        cost_estimate=SMALL,
        name="halo_sums",
    )(*halo_in, *held)
    sends[1:2] = held

    both = jnp.pad(medium_filter, ((0, 0), (0, lanes - med))) + jnp.pad(
        short_filter, ((0, 0), (med + ROWS, lanes - med - ROWS - taps))
    )

    def input_grad(which, gradient):
        first, count = pieces[which]
        in_specs = [
            filters(lanes, first),
            tables(lanes, first),
            block(8, first),
            block(rows, first),
            block(rows + ROWS, first),
            block(rows + ROWS),
            block(rows + ROWS),
        ]
        operands = [both, table, wide, inputs, gate_cot, sends[which], following[which]]
        if gradient is not None:
            in_specs.append(pl.BlockSpec(memory_space=pl.ANY))
            operands.append(gradient)
        return pl.pallas_call(
            functools.partial(back_kernel, taps),
            grid=(count,),
            in_specs=in_specs,
            out_specs=block(rows, first),
            out_shape=jax.ShapeDtypeStruct((rows, width), BF16),
            input_output_aliases={} if gradient is None else {7: 0},
            compiler_params=params(),
            cost_estimate=SMALL,
            name="input_grad",
        )(*operands)

    gradient, made = None, 0
    if devices & (devices - 1):
        stages = 1
        sums = lax.psum(sums, "ctx")
    else:
        stages = max(1, (devices - 1).bit_length())
    others = jnp.zeros_like(sums)
    for stage in range(stages):
        if devices & (devices - 1) == 0:
            others = permuted(sums, [(i, i ^ (1 << stage)) for i in range(devices)])
        if stage + 1 < len(pieces):
            following.append(permuted(sends[stage + 1], backward))
        last = stage == stages - 1
        while made < len(following) and (last or stage == stages - 2 and made == 0):
            gradient = input_grad(made, gradient)
            made += 1
        if last:
            break
        if stage + 2 < len(pieces):
            sums, sends[stage + 2] = add_after(sums, others, sends[stage + 2])
        elif gradient is None:
            sums = sums + others
        else:
            sums, gradient = add_after(sums, others, gradient)
    for piece in range(made, len(pieces)):
        if piece == len(following):
            following.append(permuted(sends[piece], backward))
        gradient = input_grad(piece, gradient)
    medium, short, gradient = finish(sums, others, gradient, groups, taps)
    return gradient, medium, short.T


def solution(mesh):
    return jax.shard_map(
        local,
        mesh=mesh,
        in_specs=(P("ctx", "fsdp"), P("ctx", "fsdp"), P("fsdp", None), P("fsdp", None)),
        out_specs=(P("ctx", "fsdp"), P("fsdp", None), P("fsdp", None)),
        check_vma=False,
    )
```

time: 51.6 us -> 41.1 us (0.80)
  waiting for transfers between devices: 17.1 us -> 2.04 us
  Pallas kernels: 9.26 us -> 16.1 us
  starting transfers between devices: 20.7 us -> 18 us
    ppermute x7, waiting for transfers between devices: 17.1 us -> 2.04 us  [permuted(): return lax.ppermute(block, 'ctx', pairs)]
    pallas_call x4 -> x8, Pallas kernels: 9.26 us -> 16.1 us  [the longest x1 5.44 us: local(): pl.pallas_call(functools.partial(own_kernel, taps, pieces), grid=(steps,)...]
    ppermute x7, starting transfers between devices: 20.7 us -> 18 us  [permuted(): return lax.ppermute(block, 'ctx', pairs)]
    unnamed x11 -> x15, local copies, waits for them, and re-layouts: 0.91 us -> 2.99 us
    slice x2 -> x0, local copies, waits for them, and re-layouts: 1.79 us -> none  [the longest x1 1.15 us: local(): tail[:, i * part:(i + 1) * part]]
    pad x1, local copies, waits for them, and re-layouts: 0.01 us -> 0.69 us  [local(): short_rows = jnp.pad(short_filter.T, ((0, 8 - taps), (0, 0)))]
    transpose x1 -> x0, local copies, waits for them, and re-layouts: 0.59 us -> none  [local(): return (gradient, sums[:groups], sums[groups:groups + taps, :groups].T)]
  transfers between devices with their start and end apart: 7 -> 7, of which waited for: 4 -> 2; matrix products, arithmetic and copies ran while one was open for 3% -> 2% of each run, Pallas kernels for 9% -> 38%
where the time goes in v3:
time: 41.1 us; the launch traced here: 40.6 us
  starting transfers between devices  18 us (44%)
  Pallas kernels  16.1 us (39%)
  local copies, waits for them, and re-layouts  3.68 us (9%)
  waiting for transfers between devices  2.04 us (5%)
  between operations  0.71 us (2%)
    ppermute x7, starting transfers between devices, permuted(): return lax.ppermute(block, 'ctx', pairs)  18 us
    pallas_call x1, Pallas kernels, local(): pl.pallas_call(functools.partial(own_kernel, taps, pieces), grid=(steps,)...  5.44 us
    pallas_call x1, Pallas kernels, local(): pl.pallas_call(functools.partial(halo_kernel, taps, factor), grid=(steps,...  5.07 us
    pallas_call x3, Pallas kernels, input_grad(): pl.pallas_call(functools.partial(back_kernel, taps), grid=(count,), in_sp...  4.97 us
    unnamed x15, local copies, waits for them, and re-layouts  2.99 us
    ppermute x7, waiting for transfers between devices, permuted(): return lax.ppermute(block, 'ctx', pairs)  2.04 us
  transfers between devices with their start and end apart: 7, of which 2 were waited for; matrix products, arithmetic and copies ran while one was open for 2% of the time, Pallas kernels for 38%

profile of v3, /device:TPU:0, one launch (start us, length us, event | category | flops | bytes accessed | tf_op | source)
XLA Modules:
  0.0 40.6 jit_solution(14048327366617220566)
XLA Ops:
  0.6 4.9 %collective-permute-start = (bf16[128,2048]{1,0:T(8,128)(2,1)}, bf16[128,2048]{1,0:T(8,128)(2,1)S(1)}, u32[]{:S(2)}, u32[]{:S(2)}) collective-permute-start(bf16[128,2048]{1,0:T(8,128)(2,1)} %x_ref.9), channel_id=1, source_target_pairs={{0,4},{4,8},{8,12},{12,16},{16,20},{20,24},{24,28},{1,5},{5,9},{9,... | collective-permute-start | bytes 1572872 | tf_op jit(solution)/shard_map/ppermute | solution.py:346
  5.5 0.7 %pad.12.st_ref = bf16[8,128]{1,0:T(8,128)(2,1)S(1)} pad(bf16[7,128]{1,0:T(8,128)(2,1)} %bitcast.2, bf16[]{:T(256)} %constant.2.clone.1), padding=0_1x0_0 | pad | bytes 3842 | tf_op jit(solution)/shard_map/jit(_pad)/pad | solution.py:376
  6.2 0.0 copy-start
  6.2 1.0 %copy-done = bf16[128,2048]{1,0:T(8,128)(2,1)S(1)} copy-done((bf16[128,2048]{1,0:T(8,128)(2,1)S(1)}, bf16[128,2048]{1,0:T(8,128)(2,1)}, u32[]{:S(2)}) %copy-start) | copy-done | bytes 524312
  7.2 0.0 copy-start.2
  7.2 1.0 %copy-done.2 = bf16[128,2048]{1,0:T(8,128)(2,1)S(1)} copy-done((bf16[128,2048]{1,0:T(8,128)(2,1)S(1)}, bf16[128,2048]{1,0:T(8,128)(2,1)}, u32[]{:S(2)}) %copy-start.2) | copy-done | bytes 524312
  8.3 0.0 copy-start.4
  8.3 0.8 %copy-done.4 = bf16[128,128]{1,0:T(8,128)(2,1)S(1)} copy-done((bf16[128,128]{1,0:T(8,128)(2,1)S(1)}, bf16[128,128]{1,0:T(8,128)(2,1)}, u32[]{:S(2)}) %copy-start.4) | copy-done | bytes 32792
  9.0 0.0 copy-start.1
  9.0 0.0 copy-start.3
  9.1 5.4 %own_block.1 = (bf16[144,1024]{1,0:T(8,128)(2,1)S(1)}, bf16[144,512]{1,0:T(8,128)(2,1)S(1)}, bf16[144,512]{1,0:T(8,128)(2,1)S(1)}, bf16[128,2048]{1,0:T(8,128)(2...) custom-call(bf16[128,128]{1,0:T(8,128)(2,1)S(1)} %copy-done.4, ...), custom_call_target="tpu_custom_call" | custom-call | flops 1 | bytes 1 | tf_op jit(solution)/shard_map/own_block/pallas_call | solution.py:379
  14.5 1.3 %collective-permute-start.3 = (bf16[144,1024]{1,0:T(8,128)(2,1)S(1)}, bf16[144,1024]{1,0:T(8,128)(2,1)S(1)}, u32[]{:S(2)}, u32[]{:S(2)}) collective-permute-start(bf16[144,1024]{1,0:T(8,128)(2,1)S(1)} %get-tuple-element.31.cot_ref), channel_id=1, source_target_pairs={{4,0},{8,4},{12,8},{16,12},{20,16},{24,20},{28,24},{5,1},{9,5},{13... | collective-permute-start | bytes 884744 | tf_op jit(solution)/shard_map/ppermute | solution.py:346
  15.8 1.2 %collective-permute-done.prev_ref = bf16[128,2048]{1,0:T(8,128)(2,1)S(1)} collective-permute-done((bf16[128,2048]{1,0:T(8,128)(2,1)}, bf16[128,2048]{1,0:T(8,128)(2,1)S(1)}, u32[]{:S(2)}, u32[]{:S(2)}) %collective-permute-start) | collective-permute-done | bytes 524320 | tf_op jit(solution)/shard_map/ppermute | solution.py:346
  17.0 0.0 copy-done.1
  17.0 0.0 copy-done.3
  17.0 0.0 copy-start.6
  17.0 5.1 %halo_sums.1 = (bf16[144,2048]{1,0:T(8,128)(2,1)S(1)}, f32[136,128]{1,0:T(8,128)S(1)}, bf16[144,512]{1,0:T(8,128)(2,1)S(1)}) custom-call(bf16[2048,256]{1,0:T(8,128)(2,1)S(1)} %get-tuple-element.21.table_ref, f32[8,2048]{1,0:T(8,128)S(1)} %get-tuple-element.22.wide_ref, ...), custom_call_target="tpu_custom_call", output_to_operand_aliasing={{2}: (8, {})} | custom-call | flops 1 | bytes 1 | tf_op jit(solution)/shard_map/halo_sums/pallas_call | solution.py:436
  22.1 2.5 %collective-permute-start.1 = (f32[136,128]{1,0:T(8,128)S(1)}, f32[136,128]{1,0:T(8,128)S(1)}, u32[]{:S(2)}, u32[]{:S(2)}) collective-permute-start(f32[136,128]{1,0:T(8,128)S(1)} %get-tuple-element.27.own_ref), channel_id=1, source_target_pairs={{0,4},{4,0},{8,12},{12,8},{16,20},{20,16},{24,28},{28,24},{1,5},{5... | collective-permute-start | bytes 208904 | tf_op jit(solution)/shard_map/ppermute | solution.py:346
  24.5 0.0 copy-done.6
  24.5 0.1 copy.13
  24.6 1.3 %collective-permute-start.6 = (bf16[144,512]{1,0:T(8,128)(2,1)S(1)}, bf16[144,512]{1,0:T(8,128)(2,1)S(1)}, u32[]{:S(2)}, u32[]{:S(2)}) collective-permute-start(bf16[144,512]{1,0:T(8,128)(2,1)S(1)} %get-tuple-element.34.cot_ref), channel_id=1, source_target_pairs={{4,0},{8,4},{12,8},{16,12},{20,16},{24,20},{28,24},{5,1},{9,5},{13... | collective-permute-start | bytes 442376 | tf_op jit(solution)/shard_map/ppermute | solution.py:346
  25.9 0.9 %collective-permute-done.1.other_ref = f32[136,128]{1,0:T(8,128)S(1)} collective-permute-done((f32[136,128]{1,0:T(8,128)S(1)}, f32[136,128]{1,0:T(8,128)S(1)}, u32[]{:S(2)}, u32[]{:S(2)}) %collective-permute-start.1) | collective-permute-done | bytes 69664 | tf_op jit(solution)/shard_map/ppermute | solution.py:346
  26.8 0.0 copy-start.5
  26.8 3.5 %collective-permute-start.2 = (f32[136,128]{1,0:T(8,128)S(1)}, f32[136,128]{1,0:T(8,128)S(1)}, u32[]{:S(2)}, u32[]{:S(2)}) collective-permute-start(f32[136,128]{1,0:T(8,128)S(1)} %get-tuple-element.29.own_ref), channel_id=1, source_target_pairs={{0,8},{4,12},{8,0},{12,4},{16,24},{20,28},{24,16},{28,20},{1,9},{5... | collective-permute-start | bytes 208904 | tf_op jit(solution)/shard_map/ppermute | solution.py:346
  30.3 1.3 %collective-permute-start.5 = (bf16[144,512]{1,0:T(8,128)(2,1)S(1)}, bf16[144,512]{1,0:T(8,128)(2,1)S(1)}, u32[]{:S(2)}, u32[]{:S(2)}) collective-permute-start(bf16[144,512]{1,0:T(8,128)(2,1)S(1)} %get-tuple-element.33.cot_ref), channel_id=1, source_target_pairs={{4,0},{8,4},{12,8},{16,12},{20,16},{24,20},{28,24},{5,1},{9,5},{13... | collective-permute-start | bytes 442376 | tf_op jit(solution)/shard_map/ppermute | solution.py:346
  31.6 0.0 copy-done.5
  31.6 0.1 pad_add_fusion.ms_ref
  31.7 0.0 collective-permute-done.3.next_ref
  31.7 2.2 %input_grad.3.held_ref = bf16[128,2048]{1,0:T(8,128)(2,1)} custom-call(bf16[128,256]{1,0:T(8,128)(2,1)S(1)} %pad_add_fusion.ms_ref, bf16[2048,256]{1,0:T(8,128)(2,1)S(1)} %get-tuple-element.21.table_ref, f32[8,2048]{1,0:T(8,128)S(1)} %get-tuple-element.22.wide_ref, bf16[128,2048]{1,0:T(8,128)(2,1)S(1)} %copy-done.1, ...), custom_call_target="tpu_custom_call" | custom-call | flops 1 | bytes 1 | tf_op jit(solution)/shard_map/input_grad/pallas_call | solution.py:468
  34.0 0.0 collective-permute-done.2.other_ref
  34.0 3.3 %collective-permute-start.4 = (f32[136,128]{1,0:T(8,128)S(1)}, f32[136,128]{1,0:T(8,128)S(1)}, u32[]{:S(2)}, u32[]{:S(2)}) collective-permute-start(f32[136,128]{1,0:T(8,128)S(1)} %get-tuple-element.32.own_ref), channel_id=1, source_target_pairs={{0,16},{4,20},{8,24},{12,28},{16,0},{20,4},{24,8},{28,12},{1,17},{... | collective-permute-start | bytes 208904 | tf_op jit(solution)/shard_map/ppermute | solution.py:346
  37.2 0.0 collective-permute-done.6.next_ref
  37.3 1.4 %input_grad.4.rest_0_ = bf16[128,2048]{1,0:T(8,128)(2,1)} custom-call(bf16[128,256]{1,0:T(8,128)(2,1)S(1)} %pad_add_fusion.ms_ref, bf16[2048,256]{1,0:T(8,128)(2,1)S(1)} %get-tuple-element.21.table_ref, f32[8,2048]{1,0:T(8,128)S(1)} %get-tuple-element.22.wide_ref, bf16[128,2048]{1,0:T(8,128)(2,1)S(1)} %copy-done.1, ...), custom_call_target="tpu_custom_call", output_to_operand_aliasing={{}: (7, {})} | custom-call | flops 1 | bytes 1 | tf_op jit(solution)/shard_map/input_grad/pallas_call | solution.py:468
  38.6 0.0 collective-permute-done.5.next_ref
  38.6 1.4 %input_grad.5.held_ref = bf16[128,2048]{1,0:T(8,128)(2,1)} custom-call(bf16[128,256]{1,0:T(8,128)(2,1)S(1)} %pad_add_fusion.ms_ref, bf16[2048,256]{1,0:T(8,128)(2,1)S(1)} %get-tuple-element.21.table_ref, f32[8,2048]{1,0:T(8,128)S(1)} %get-tuple-element.22.wide_ref, bf16[128,2048]{1,0:T(8,128)(2,1)S(1)} %copy-done.1, ...), custom_call_target="tpu_custom_call", output_to_operand_aliasing={{}: (7, {})} | custom-call | flops 1 | bytes 1 | tf_op jit(solution)/shard_map/input_grad/pallas_call | solution.py:468
  40.0 0.0 collective-permute-done.4.other_ref
  40.0 0.6 %finish_sums.1 = (f32[128,128]{1,0:T(8,128)}, f32[7,128]{1,0:T(8,128)}, bf16[128,2048]{1,0:T(8,128)(2,1)}) custom-call(f32[136,128]{1,0:T(8,128)S(1)} %get-tuple-element.32.own_ref, f32[136,128]{1,0:T(8,128)S(1)} %collective-permute-done.4.other_ref, bf16[128,2048]{1,0:T(8,128)(2,1)} %input_grad.5.held_ref), custom_call_target="tpu_custom_call", output_to_operand_aliasing={{2}: (2, {})} | custom-call | flops 1 | bytes 1 | tf_op jit(solution)/shard_map/finish_sums/pallas_call | solution.py:324
  (2 shorter events, 0.0 us)
Async XLA Ops:
  0.6 16.3 %collective-permute-start = (bf16[128,2048]{1,0:T(8,128)(2,1)}, bf16[128,2048]{1,0:T(8,128)(2,1)S(1)}, u32[]{:S(2)}, u32[]{:S(2)}) collective-permute-start(bf16[128,2048]{1,0:T(8,128)(2,1)} %x_ref.9), channel_id=1, source_target_pairs={{0,4},{4,8},{8,12},{12,16},{16,20},{20,24},{24,28},{1,5},{5,9},{9,... | collective-permute-start | bytes 1572872 | tf_op jit(solution)/shard_map/ppermute | solution.py:346
  6.2 1.0 %copy-start = (bf16[128,2048]{1,0:T(8,128)(2,1)S(1)}, bf16[128,2048]{1,0:T(8,128)(2,1)}, u32[]{:S(2)}) copy-start(bf16[128,2048]{1,0:T(8,128)(2,1)} %x_ref.9) | copy-start | bytes 1572868
  7.2 1.0 %copy-start.2 = (bf16[128,2048]{1,0:T(8,128)(2,1)S(1)}, bf16[128,2048]{1,0:T(8,128)(2,1)}, u32[]{:S(2)}) copy-start(bf16[128,2048]{1,0:T(8,128)(2,1)} %u_ref.3) | copy-start | bytes 1572868
  8.3 0.8 %copy-start.4 = (bf16[128,128]{1,0:T(8,128)(2,1)S(1)}, bf16[128,128]{1,0:T(8,128)(2,1)}, u32[]{:S(2)}) copy-start(bf16[128,128]{1,0:T(8,128)(2,1)} %m_ref.1) | copy-start | bytes 98308
  9.0 7.9 %copy-start.1 = (bf16[128,2048]{1,0:T(8,128)(2,1)S(1)}, bf16[128,2048]{1,0:T(8,128)(2,1)}, u32[]{:S(2)}) copy-start(bf16[128,2048]{1,0:T(8,128)(2,1)} %x_ref.9) | copy-start | bytes 1572868
  9.0 7.9 %copy-start.3 = (bf16[128,2048]{1,0:T(8,128)(2,1)S(1)}, bf16[128,2048]{1,0:T(8,128)(2,1)}, u32[]{:S(2)}) copy-start(bf16[128,2048]{1,0:T(8,128)(2,1)} %u_ref.3) | copy-start | bytes 1572868
  14.5 17.2 %collective-permute-start.3 = (bf16[144,1024]{1,0:T(8,128)(2,1)S(1)}, bf16[144,1024]{1,0:T(8,128)(2,1)S(1)}, u32[]{:S(2)}, u32[]{:S(2)}) collective-permute-start(bf16[144,1024]{1,0:T(8,128)(2,1)S(1)} %get-tuple-element.31.cot_ref), channel_id=1, source_target_pairs={{4,0},{8,4},{12,8},{16,12},{20,16},{24,20},{28,24},{5,1},{9,5},{13... | collective-permute-start | bytes 884744 | tf_op jit(solution)/shard_map/ppermute | solution.py:346
  17.0 7.5 %copy-start.6 = (bf16[128,7]{0,1:T(8,128)(2,1)S(1)}, bf16[128,7]{0,1:T(8,128)(2,1)}, u32[]{:S(2)}) copy-start(bf16[128,7]{0,1:T(8,128)(2,1)} %param.7) | copy-start | bytes 5380
  22.1 4.7 %collective-permute-start.1 = (f32[136,128]{1,0:T(8,128)S(1)}, f32[136,128]{1,0:T(8,128)S(1)}, u32[]{:S(2)}, u32[]{:S(2)}) collective-permute-start(f32[136,128]{1,0:T(8,128)S(1)} %get-tuple-element.27.own_ref), channel_id=1, source_target_pairs={{0,4},{4,0},{8,12},{12,8},{16,20},{20,16},{24,28},{28,24},{1,5},{5... | collective-permute-start | bytes 208904 | tf_op jit(solution)/shard_map/ppermute | solution.py:346
  24.6 12.6 %collective-permute-start.6 = (bf16[144,512]{1,0:T(8,128)(2,1)S(1)}, bf16[144,512]{1,0:T(8,128)(2,1)S(1)}, u32[]{:S(2)}, u32[]{:S(2)}) collective-permute-start(bf16[144,512]{1,0:T(8,128)(2,1)S(1)} %get-tuple-element.34.cot_ref), channel_id=1, source_target_pairs={{4,0},{8,4},{12,8},{16,12},{20,16},{24,20},{28,24},{5,1},{9,5},{13... | collective-permute-start | bytes 442376 | tf_op jit(solution)/shard_map/ppermute | solution.py:346
  26.8 4.8 %copy-start.5 = (bf16[128,128]{1,0:T(8,128)(2,1)S(1)}, bf16[128,128]{1,0:T(8,128)(2,1)}, u32[]{:S(2)}) copy-start(bf16[128,128]{1,0:T(8,128)(2,1)} %m_ref.1) | copy-start | bytes 98308
  26.8 7.1 %collective-permute-start.2 = (f32[136,128]{1,0:T(8,128)S(1)}, f32[136,128]{1,0:T(8,128)S(1)}, u32[]{:S(2)}, u32[]{:S(2)}) collective-permute-start(f32[136,128]{1,0:T(8,128)S(1)} %get-tuple-element.29.own_ref), channel_id=1, source_target_pairs={{0,8},{4,12},{8,0},{12,4},{16,24},{20,28},{24,16},{28,20},{1,9},{5... | collective-permute-start | bytes 208904 | tf_op jit(solution)/shard_map/ppermute | solution.py:346
  30.3 8.3 %collective-permute-start.5 = (bf16[144,512]{1,0:T(8,128)(2,1)S(1)}, bf16[144,512]{1,0:T(8,128)(2,1)S(1)}, u32[]{:S(2)}, u32[]{:S(2)}) collective-permute-start(bf16[144,512]{1,0:T(8,128)(2,1)S(1)} %get-tuple-element.33.cot_ref), channel_id=1, source_target_pairs={{4,0},{8,4},{12,8},{16,12},{20,16},{24,20},{28,24},{5,1},{9,5},{13... | collective-permute-start | bytes 442376 | tf_op jit(solution)/shard_map/ppermute | solution.py:346
  34.0 6.0 %collective-permute-start.4 = (f32[136,128]{1,0:T(8,128)S(1)}, f32[136,128]{1,0:T(8,128)S(1)}, u32[]{:S(2)}, u32[]{:S(2)}) collective-permute-start(f32[136,128]{1,0:T(8,128)S(1)} %get-tuple-element.32.own_ref), channel_id=1, source_target_pairs={{0,16},{4,20},{8,24},{12,28},{16,0},{20,4},{24,8},{28,12},{1,17},{... | collective-permute-start | bytes 208904 | tf_op jit(solution)/shard_map/ppermute | solution.py:346

commit v4 on v3

v4 whole, which is shorter than its diff:
```python
import functools

import jax
import jax.numpy as jnp
from jax import lax
from jax.experimental import pallas as pl
from jax.experimental.pallas import tpu as pltpu
from jax.sharding import PartitionSpec as P

GROUP = 16
ROWS = 16
EDGE = 8
LANES = 128
PIECES = (8, 5, 3)
ISSUE = (0, 1, 2)
EARLY = 1
F32 = jnp.float32
BF16 = jnp.bfloat16
LONG = pl.CostEstimate(flops=1, bytes_accessed=16 << 20, transcendentals=0)
SMALL = pl.CostEstimate(flops=1, bytes_accessed=1, transcendentals=0)


def iota(shape, dim):
    return lax.broadcasted_iota(jnp.int32, shape, dim)


def split3(values):
    high = values.astype(BF16)
    rest = values - high.astype(F32)
    middle = rest.astype(BF16)
    low = (rest - middle.astype(F32)).astype(BF16)
    return jnp.concatenate([high, middle, low], axis=0)


def exact_dot(values, table):
    rows = values.shape[0]
    out = jnp.dot(split3(values), table, preferred_element_type=F32)
    return out[:rows] + out[rows : 2 * rows] + out[2 * rows :]


def delayed(values, distance):
    return values if distance == 0 else pltpu.roll(values, distance, 0)


def toeplitz(base):
    lanes = base.shape[1]
    blocks = [
        pltpu.roll(
            jnp.broadcast_to(base[g : g + 1], (ROWS, lanes)), 0, 1, stride=1, stride_axis=0
        )
        for g in range(base.shape[0])
    ]
    return jnp.concatenate(blocks, 0).astype(BF16)


def own_group(product, lane_group):
    total = product[:ROWS]
    for g in range(1, product.shape[0] // ROWS):
        total = jnp.where(lane_group == g, product[g * ROWS : (g + 1) * ROWS], total)
    return total


def stacked(first, second, start, stop):
    extent = first.shape[0]
    if stop <= extent:
        return first[start:stop]
    if start >= extent:
        return second[start - extent : stop - extent]
    return jnp.concatenate([first[start:], second[: stop - extent]], 0)


def masked(cots, lane_group):
    return jnp.concatenate(
        [
            jnp.where(lane_group == g, cots, jnp.zeros_like(cots))
            for g in range(LANES // GROUP)
        ],
        0,
    )


def contracted(alone, part):
    return lax.dot_general(
        alone, part, (((1,), (1,)), ((), ())), preferred_element_type=F32
    )


def diagonal_sums(pairs, lanes):
    if pairs.shape[1] < lanes:
        pad = jnp.zeros((pairs.shape[0], lanes - pairs.shape[1]), F32)
        pairs = jnp.concatenate([pairs, pad], 1)
    return [
        jnp.sum(
            pltpu.roll(pairs[g * ROWS : (g + 1) * ROWS], 0, 1, stride=1, stride_axis=0),
            0,
            keepdims=True,
        )
        for g in range(LANES // GROUP)
    ]


def medium_sums(diagonals, med, lanes):
    flip_back = iota((lanes, med), 0) == med + ROWS - 1 - iota((lanes, med), 1)
    return exact_dot(jnp.concatenate(diagonals, 0), flip_back.astype(BF16))


def turning(extent):
    return (iota((extent, extent), 0) ^ (ROWS - 1) == iota((extent, extent), 1)).astype(BF16)


def gated(wide, near, taps):
    gate = wide[0:1] * near[ROWS:]
    for j in range(1, taps):
        gate = gate + wide[j : j + 1] * delayed(near, j)[ROWS:]
    return gate


def lane_groups():
    return iota((ROWS, 2 * LANES), 1) % LANES // GROUP


def own_kernel(taps, pieces, strip, ms_ref, st_ref, x_ref, u_ref, *outs):
    *send_refs, cot_ref, turned_ref, conv_ref, medium_ref, table_ref, back_ref, wide_ref = outs
    rows, width = x_ref.shape
    groups, med = medium_ref.shape
    window = med + ROWS
    lanes = med + 128
    tile = LANES // GROUP

    flip = (iota((med, lanes), 0) == med - iota((med, lanes), 1)).astype(BF16)
    spread = iota((groups, width), 0) == iota((groups, width), 1) // GROUP
    wide_ref[...] = jnp.dot(st_ref[...], spread.astype(BF16), preferred_element_type=F32)
    upturn = turning(rows)
    lane_group = lane_groups()

    def one_strip(step, carry):
        mine = pl.ds(pl.multiple_of(step * (strip // GROUP), tile), strip // GROUP)
        back = ms_ref[mine, :]
        base = jnp.dot(back[:, :med], flip, preferred_element_type=F32)
        back = back.astype(F32)
        diagonals = []
        for block in range(strip // LANES):
            at = pl.ds(pl.multiple_of(step * strip + block * LANES, LANES), LANES)
            x = x_ref[:, at]
            near = jnp.concatenate([jnp.zeros((ROWS, LANES), F32), x.astype(F32)], 0)
            cot = u_ref[:, at].astype(F32) * gated(wide_ref[:, at], near, taps)
            cot = cot.astype(BF16)
            cot_ref[:, at] = cot
            turned = jnp.dot(upturn, cot, preferred_element_type=F32).astype(BF16)
            turned_ref[:, at] = turned
            table = toeplitz(base[block * tile : (block + 1) * tile])
            table_ref[at, :] = table
            back_ref[at, :] = toeplitz(back[block * tile : (block + 1) * tile])

            pairs = jnp.zeros((LANES, window), F32)
            for a in range(0, rows // ROWS, 2):
                lo, mid, hi = (ROWS * k for k in (a, a + 1, a + 2))
                empty = jnp.zeros((med - lo, LANES), BF16)
                part = jnp.concatenate(
                    [
                        jnp.concatenate([empty, x[:mid]], 0),
                        jnp.concatenate([empty, x[ROWS:hi]], 0),
                    ],
                    1,
                )
                conv = own_group(
                    jnp.dot(table[:, :window], part, preferred_element_type=F32), lane_group
                )
                conv_ref[lo:mid, at] = conv[:, :LANES]
                conv_ref[mid:hi, at] = conv[:, LANES:]
                if a:
                    both = jnp.concatenate([turned[lo:mid], turned[mid:hi]], 1)
                    pairs = pairs + contracted(masked(both, lane_group), part)
            diagonals += diagonal_sums(pairs, lanes)
        medium_ref[mine, :] = medium_sums(diagonals, med, lanes)
        return carry

    lax.fori_loop(0, width // strip, one_strip, 0)
    for send_ref, (start, stop) in zip(send_refs, pieces):
        for at in range(start, stop, LANES):
            block = slice(at, at + LANES)
            parts = [cot_ref[:, block], x_ref[:ROWS, block], u_ref[:ROWS, block]]
            cot, x, u = (part.astype(F32) for part in parts)
            send_ref[:, at - start : at - start + LANES] = jnp.concatenate(
                [cot[EDGE:], x[:EDGE], u[:EDGE]], 0
            ).astype(BF16)


def halo_kernel(taps, factor, cols, table_ref, wide_ref, prev_ref, x_ref, u_ref, turned_ref,
                conv_ref, medium_ref, *rest):
    gate_cot_ref, sums_ref = rest[len(rest) // 2 - 1 :][:2]
    rows, width = x_ref.shape
    med = prev_ref.shape[0]
    window = med + ROWS
    lanes = med + 128
    tile = LANES // GROUP
    groups = cols // GROUP
    total_groups = sums_ref.shape[0] - 8
    upturn = turning(ROWS)
    lane_group = lane_groups()

    def one_step(step, total):
        diagonals, short = [], []
        for block in range(cols // LANES):
            start = step * cols + block * LANES
            at = slice(start, start + LANES)
            prev, x, u = prev_ref[:, at], x_ref[:, at], u_ref[:, at]
            near = jnp.concatenate([prev[med - ROWS :], x], 0).astype(F32)
            table = table_ref[at, :med]
            head = gated(wide_ref[:, at], near[: 2 * ROWS], taps) * u[:ROWS].astype(F32)
            head = head.astype(BF16)
            gate_cot_ref[:ROWS, at] = head
            head = jnp.dot(upturn, head, preferred_element_type=F32).astype(BF16)

            pairs = None
            gate_cots = []
            for a in range(0, rows // ROWS, 2):
                lo, mid, hi = (ROWS * k for k in (a, a + 1, a + 2))
                part = jnp.concatenate(
                    [stacked(prev, x, lo, med), stacked(prev, x, mid, med + ROWS)], 1
                )
                conv = own_group(
                    jnp.dot(table[:, : med - lo], part, preferred_element_type=F32),
                    lane_group,
                )
                if a == 0:
                    part = jnp.concatenate([part, jnp.concatenate([x[:ROWS], x[ROWS:hi]], 1)], 0)
                    both = jnp.concatenate([head, turned_ref[mid:hi, at]], 1)
                else:
                    both = jnp.concatenate([turned_ref[lo:mid, at], turned_ref[mid:hi, at]], 1)
                more = contracted(masked(both, lane_group), part)
                if more.shape[1] < window:
                    more = jnp.concatenate(
                        [more, jnp.zeros((LANES, window - more.shape[1]), F32)], 1
                    )
                pairs = more if pairs is None else pairs + more
                for k in range(2):
                    here = slice(lo + k * ROWS, mid + k * ROWS)
                    whole = conv_ref[here, at] + conv[:, k * LANES : (k + 1) * LANES]
                    gate_cots.append((u[here].astype(F32) * whole).astype(BF16))
            gate_cot = jnp.concatenate(gate_cots, 0)
            gate_cot_ref[ROWS:, at] = gate_cot
            diagonals += diagonal_sums(pairs, lanes)
            gate_cot = gate_cot.astype(F32)
            sums = [
                jnp.sum(gate_cot * delayed(near, j)[ROWS:], 0, keepdims=True)
                for j in range(taps)
            ]
            short.append(jnp.concatenate(sums + [jnp.zeros((8 - taps, LANES), F32)], 0))

        mine = slice(step * groups, (step + 1) * groups)
        medium = medium_ref[mine, :] + medium_sums(diagonals, med, lanes)
        sums_ref[mine, :] = medium * factor
        gather = iota((cols, med), 1) == step * groups + iota((cols, med), 0) // GROUP
        return total + exact_dot(jnp.concatenate(short, 1), gather.astype(BF16))

    total = jnp.zeros((8, med), F32)
    for step in range(width // cols):
        total = one_step(step, total)
    sums_ref[total_groups:, :] = total * factor


def back_kernel(taps, pieces, table_ref, back_ref, wide_ref, x_ref, gate_cot_ref, cot_ref, *rest):
    count = len(pieces)
    next_refs = rest[:count]
    out_ref, made, sems = rest[-3:]
    rows = x_ref.shape[0]
    window = table_ref.shape[1] - 128 + ROWS
    lane_group = lane_groups()
    first = pieces[0][0]
    blocks = [
        (start, next_ref, at)
        for (start, stop), next_ref in zip(pieces, next_refs)
        for at in range(start, stop, LANES)
    ]
    rest_of = jnp.zeros((ROWS - EDGE, LANES), F32)
    copies = []
    for index, (start, next_ref, begin) in enumerate(blocks):
        at = slice(begin, begin + LANES)
        there = slice(begin - first, begin - first + LANES)
        forward = table_ref[at, :window]
        table = back_ref[at, : window + 2 * ROWS]
        x = x_ref[:, at]
        later = next_ref[:, begin - start : begin - start + LANES].astype(F32)
        x_next, u_next = later[rows - EDGE : rows], later[rows:]
        near = jnp.concatenate([x[rows - ROWS :].astype(F32), x_next], 0)
        head = (u_next * gated(wide_ref[:, at], near, taps)).astype(BF16)
        part = jnp.concatenate(
            [x[rows + ROWS - window :], jnp.concatenate([x_next, rest_of], 0).astype(BF16)], 0
        )
        conv = own_group(
            jnp.dot(forward, part, preferred_element_type=F32), lane_group[:, :LANES]
        )
        gate_after = jnp.concatenate([u_next * conv[:EDGE], rest_of], 0).astype(BF16)
        cot = jnp.concatenate([gate_cot_ref[:ROWS, at], cot_ref[ROWS:, at]], 0)
        after = jnp.concatenate([head.astype(F32), later[: rows - EDGE]], 0).astype(BF16)
        gate_cot = gate_cot_ref[ROWS:, at]
        for a in range(0, rows // ROWS, 2):
            sides = [
                jnp.concatenate(
                    [
                        stacked(cot, after, k, k + window),
                        stacked(gate_cot, gate_after, k, k + 2 * ROWS),
                    ],
                    0,
                )
                for k in (a * ROWS, (a + 1) * ROWS)
            ]
            product = jnp.dot(
                table, jnp.concatenate(sides, 1), preferred_element_type=F32
            )
            out = own_group(product, lane_group).astype(BF16)
            made[a * ROWS : (a + 1) * ROWS, there] = out[:, :LANES]
            made[(a + 1) * ROWS : (a + 2) * ROWS, there] = out[:, LANES:]
        if index % 2 or index == len(blocks) - 1:
            since = blocks[index - index % 2][2]
            copy = pltpu.make_async_copy(
                made.at[:, since - first : begin + LANES - first],
                out_ref.at[:, since : begin + LANES],
                sems.at[index // 2],
            )
            copy.start()
            copies.append(copy)
    for copy in copies:
        copy.wait()


def add_kernel(own_ref, other_ref, *rest):
    out_ref = rest[len(rest) // 2]
    out_ref[...] = own_ref[...] + other_ref[...]


def add_after(own, other, *held):
    whole = pl.BlockSpec(own.shape, lambda: (0, 0))
    anywhere = [pl.BlockSpec(memory_space=pl.ANY)] * len(held)
    return pl.pallas_call(
        add_kernel,
        in_specs=[whole] * 2 + anywhere,
        out_specs=[whole] + anywhere,
        out_shape=[jax.ShapeDtypeStruct(a.shape, a.dtype) for a in (own, *held)],
        input_output_aliases={2 + k: 1 + k for k in range(len(held))},
        compiler_params=pltpu.CompilerParams(vmem_limit_bytes=16 << 20),
        cost_estimate=LONG,
        name="add_sums",
    )(own, other, *held)


def finish_kernel(groups, taps, own_ref, other_ref, held_ref, medium_ref, short_ref, held_out_ref):
    total = own_ref[...] + other_ref[...]
    medium_ref[...] = total[:groups]
    short_ref[...] = total[groups : groups + taps, :groups]


def finish(own, other, held, groups, taps):
    lanes = own.shape[1]
    return pl.pallas_call(
        functools.partial(finish_kernel, groups, taps),
        in_specs=[pl.BlockSpec(own.shape, lambda: (0, 0))] * 2
        + [pl.BlockSpec(memory_space=pl.ANY)],
        out_specs=[
            pl.BlockSpec((groups, lanes), lambda: (0, 0)),
            pl.BlockSpec((taps, groups), lambda: (0, 0)),
            pl.BlockSpec(memory_space=pl.ANY),
        ],
        out_shape=[
            jax.ShapeDtypeStruct((groups, lanes), own.dtype),
            jax.ShapeDtypeStruct((taps, groups), own.dtype),
            jax.ShapeDtypeStruct(held.shape, held.dtype),
        ],
        input_output_aliases={2: 2},
        compiler_params=pltpu.CompilerParams(vmem_limit_bytes=16 << 20),
        cost_estimate=LONG,
        name="finish_sums",
    )(own, other, held)


def permuted(block, pairs):
    return lax.ppermute(block, "ctx", pairs)


def local(inputs, upstream, medium_filter, short_filter):
    rows, width = inputs.shape
    groups, med = medium_filter.shape
    taps = short_filter.shape[1]
    devices = lax.axis_size("ctx")
    assert rows == med and med % 128 == 0 and groups <= med
    assert taps <= 8 and width % LANES == 0
    strip = min(width, 8 * LANES)
    lanes = med + 128
    factor = float(GROUP * rows * devices) ** -0.5
    forward = [(i, i + 1) for i in range(devices - 1)]
    backward = [(i + 1, i) for i in range(devices - 1)]

    def params(mebibytes=40):
        return pltpu.CompilerParams(vmem_limit_bytes=mebibytes << 20)

    short_rows = jnp.pad(short_filter.T, ((0, 8 - taps), (0, 0)))
    previous = permuted(inputs, forward)
    resident = pl.BlockSpec(memory_space=pltpu.VMEM)
    sizes = PIECES if width == LANES * sum(PIECES) else (width // LANES,)
    ends = [LANES * sum(sizes[: k + 1]) for k in range(len(sizes))]
    pieces = [(end - LANES * size, end) for end, size in zip(ends, sizes)]
    both = jnp.pad(medium_filter, ((0, 0), (0, lanes - med))) + jnp.pad(
        short_filter, ((0, 0), (med + ROWS, lanes - med - ROWS - taps))
    )
    *sends, cot, turned, conv, medium, table, back, wide = pl.pallas_call(
        functools.partial(own_kernel, taps, pieces, min(width, 4 * LANES)),
        in_specs=[resident] * 4,
        out_specs=[resident] * (len(pieces) + 7),
        out_shape=[
            jax.ShapeDtypeStruct((rows + EDGE, stop - start), BF16) for start, stop in pieces
        ]
        + [
            jax.ShapeDtypeStruct((rows, width), BF16),
            jax.ShapeDtypeStruct((rows, width), BF16),
            jax.ShapeDtypeStruct((rows, width), F32),
            jax.ShapeDtypeStruct((groups, med), F32),
            jax.ShapeDtypeStruct((groups * ROWS, lanes), BF16),
            jax.ShapeDtypeStruct((groups * ROWS, lanes), BF16),
            jax.ShapeDtypeStruct((8, width), F32),
        ],
        compiler_params=params(),
        cost_estimate=SMALL,
        name="own_block",
    )(both, short_rows, inputs, upstream)
    following = [permuted(sends[0], backward)]

    halo_in = [table, wide, previous, inputs, upstream, turned, conv, medium]
    waiting = [k for k in range(len(pieces)) if ISSUE[k] == 1]
    held = [sends[k] for k in waiting]
    gate_cot, sums, *held = pl.pallas_call(
        functools.partial(halo_kernel, taps, factor, strip),
        in_specs=[resident] * len(halo_in) + [pl.BlockSpec(memory_space=pl.ANY)] * len(held),
        out_specs=[resident] * 2 + [pl.BlockSpec(memory_space=pl.ANY)] * len(held),
        out_shape=[
            jax.ShapeDtypeStruct((rows + ROWS, width), BF16),
            jax.ShapeDtypeStruct((groups + 8, med), F32),
        ]
        + [jax.ShapeDtypeStruct(h.shape, h.dtype) for h in held],
        input_output_aliases={8 + k: 2 + k for k in range(len(held))},
        compiler_params=params(),
        cost_estimate=SMALL,
        name="halo_sums",
    )(*halo_in, *held)
    for k, value in zip(waiting, held):
        sends[k] = value

    def input_grad(which, gradient):
        mine = [pieces[k] for k in which]
        extent = mine[-1][1] - mine[0][0]
        operands = [table, back, wide, inputs, gate_cot, cot]
        operands += [following[k] for k in which]
        in_specs = [resident] * len(operands)
        aliases = {}
        if gradient is not None:
            aliases[len(operands)] = 0
            in_specs.append(pl.BlockSpec(memory_space=pl.ANY))
            operands.append(gradient)
        return pl.pallas_call(
            functools.partial(back_kernel, taps, mine),
            in_specs=in_specs,
            out_specs=pl.BlockSpec(memory_space=pl.ANY),
            out_shape=jax.ShapeDtypeStruct((rows, width), BF16),
            input_output_aliases=aliases,
            scratch_shapes=[
                pltpu.VMEM((rows, extent), BF16),
                pltpu.SemaphoreType.DMA((-(-extent // (2 * LANES)),)),
            ],
            compiler_params=params(),
            cost_estimate=SMALL,
            name="input_grad",
        )(*operands)

    gradient = None
    if devices & (devices - 1):
        stages = 1
        sums = lax.psum(sums, "ctx")
    else:
        stages = max(1, (devices - 1).bit_length())
    others = jnp.zeros_like(sums)
    for stage in range(stages):
        if devices & (devices - 1) == 0:
            others = permuted(sums, [(i, i ^ (1 << ((0, 1, 2)[stage] if stages == 3 else stage))) for i in range(devices)])
        if len(following) < len(pieces) and ISSUE[len(following)] == stage + 1:
            following.append(permuted(sends[len(following)], backward))
        last = stage == stages - 1
        if len(pieces) > 1 and stage == EARLY and not last:
            gradient = input_grad([0], None)
        if last:
            break
        waiting = [k for k in range(len(pieces)) if ISSUE[k] == stage + 2]
        held = [sends[k] for k in waiting] + ([] if gradient is None else [gradient])
        sums, *held = add_after(sums, others, *held)
        if gradient is not None:
            gradient = held.pop()
        for k, value in zip(waiting, held):
            sends[k] = value
    for k in range(len(following), len(pieces)):
        following.append(permuted(sends[k], backward))
    rest = range(len(pieces)) if gradient is None else range(1, len(pieces))
    gradient = input_grad(list(rest), gradient)
    medium, short, gradient = finish(sums, others, gradient, groups, taps)
    return gradient, medium, short.T


def solution(mesh):
    return jax.shard_map(
        local,
        mesh=mesh,
        in_specs=(P("ctx", "fsdp"), P("ctx", "fsdp"), P("fsdp", None), P("fsdp", None)),
        out_specs=(P("ctx", "fsdp"), P("fsdp", None), P("fsdp", None)),
        check_vma=False,
    )
```

time: 41.1 us -> 39.6 us (0.964)
  Pallas kernels: 16.1 us -> 13.4 us
  waiting for transfers between devices: 2.04 us -> 3.35 us
  local copies, waits for them, and re-layouts: 3.68 us -> 2.97 us
  starting transfers between devices: 18 us -> 18.7 us
    pallas_call x7 -> x6, Pallas kernels: 15.5 us -> 12.8 us  [the longest x1 5.18 us: local(): pl.pallas_call(functools.partial(own_kernel, taps, pieces, min(width, 4 *...]
    ppermute x7, waiting for transfers between devices: 2.04 us -> 3.35 us  [permuted(): return lax.ppermute(block, 'ctx', pairs)]
    ppermute x7, starting transfers between devices: 18 us -> 18.7 us  [permuted(): return lax.ppermute(block, 'ctx', pairs)]
    pad x1, local copies, waits for them, and re-layouts: 0.69 us -> 0.01 us  [local(): short_rows = jnp.pad(short_filter.T, ((0, 8 - taps), (0, 0)))]
    unnamed x15 -> x13, local copies, waits for them, and re-layouts: 2.99 us -> 2.97 us
  transfers between devices with their start and end apart: 7 -> 7, of which waited for: 2 -> 3; matrix products, arithmetic and copies ran while one was open for 2% -> 2% of each run, Pallas kernels for 38% -> 32%
where the time goes in v4:
time: 39.6 us; the launch traced here: 39.3 us
  starting transfers between devices  18.7 us (47%)
  Pallas kernels  13.4 us (34%)
  waiting for transfers between devices  3.35 us (8%)
  local copies, waits for them, and re-layouts  2.97 us (8%)
  between operations  0.76 us (2%)
    ppermute x7, starting transfers between devices, permuted(): return lax.ppermute(block, 'ctx', pairs)  18.7 us
    pallas_call x1, Pallas kernels, local(): pl.pallas_call(functools.partial(own_kernel, taps, pieces, min(width, 4 *...  5.18 us
    pallas_call x1, Pallas kernels, local(): pl.pallas_call(functools.partial(halo_kernel, taps, factor, strip), in_sp...  3.85 us
    pallas_call x2, Pallas kernels, input_grad(): pl.pallas_call(functools.partial(back_kernel, taps, mine), in_specs=in_sp...  3.7 us
    ppermute x7, waiting for transfers between devices, permuted(): return lax.ppermute(block, 'ctx', pairs)  3.35 us
    unnamed x13, local copies, waits for them, and re-layouts  2.97 us
  transfers between devices with their start and end apart: 7, of which 3 were waited for; matrix products, arithmetic and copies ran while one was open for 2% of the time, Pallas kernels for 32%

profile of v4, /device:TPU:0, one launch (start us, length us, event | category | flops | bytes accessed | tf_op | source)
XLA Modules:
  0.0 39.3 jit_solution(12319941265670678556)
XLA Ops:
  0.6 0.0 copy-start.4
  0.6 4.9 %collective-permute-start = (bf16[128,2048]{1,0:T(8,128)(2,1)}, bf16[128,2048]{1,0:T(8,128)(2,1)S(1)}, u32[]{:S(2)}, u32[]{:S(2)}) collective-permute-start(bf16[128,2048]{1,0:T(8,128)(2,1)} %x_ref.7), channel_id=1, source_target_pairs={{0,4},{4,8},{8,12},{12,16},{16,20},{20,24},{24,28},{1,5},{5,9},{9,... | collective-permute-start | bytes 1572872 | tf_op jit(solution)/shard_map/ppermute | solution.py:378
  5.5 0.0 copy-start.5
  5.5 0.9 %copy.12 = bf16[128,7]{1,0:T(8,128)(2,1)S(1)} copy(bf16[128,7]{0,1:T(8,128)(2,1)} %param.7) | data formatting | bytes 3584 | tf_op args[3]
  6.4 0.0 copy-done.5
  6.4 0.0 copy-done.4
  6.4 0.1 pad_add_fusion.ms_ref
  6.5 0.0 copy-start
  6.5 1.0 %copy-done = bf16[128,2048]{1,0:T(8,128)(2,1)S(1)} copy-done((bf16[128,2048]{1,0:T(8,128)(2,1)S(1)}, bf16[128,2048]{1,0:T(8,128)(2,1)}, u32[]{:S(2)}) %copy-start) | copy-done | bytes 524312
  7.6 0.0 copy-start.2
  7.6 1.0 %copy-done.2 = bf16[128,2048]{1,0:T(8,128)(2,1)S(1)} copy-done((bf16[128,2048]{1,0:T(8,128)(2,1)S(1)}, bf16[128,2048]{1,0:T(8,128)(2,1)}, u32[]{:S(2)}) %copy-start.2) | copy-done | bytes 524312
  8.6 0.0 copy-start.1
  8.6 0.0 copy-start.3
  8.6 5.2 %own_block.1 = (bf16[136,1024]{1,0:T(8,128)(2,1)S(1)}, bf16[136,640]{1,0:T(8,128)(2,1)S(1)}, bf16[136,384]{1,0:T(8,128)(2,1)S(1)}, bf16[128,2048]{1,0:T(8,128)(2...) custom-call(bf16[128,256]{1,0:T(8,128)(2,1)S(1)} %pad_add_fusion.ms_, ...), custom_call_target="tpu_custom_call" | custom-call | flops 1 | bytes 1 | tf_op jit(solution)/shard_map/own_block/pallas_call | solution.py:406
  13.8 1.3 %collective-permute-start.3 = (bf16[136,1024]{1,0:T(8,128)(2,1)S(1)}, bf16[136,1024]{1,0:T(8,128)(2,1)S(1)}, u32[]{:S(2)}, u32[]{:S(2)}) collective-permute-start(bf16[136,1024]{1,0:T(8,128)(2,1)S(1)} %get-tuple-element.35), channel_id=1, source_target_pairs={{4,0},{8,4},{12,8},{16,12},{20,16},{24,20},{28,24},{5,1},{9,5},{13... | collective-permute-start | bytes 835592 | tf_op jit(solution)/shard_map/ppermute | solution.py:378
  15.1 1.9 %collective-permute-done.prev_ref = bf16[128,2048]{1,0:T(8,128)(2,1)S(1)} collective-permute-done((bf16[128,2048]{1,0:T(8,128)(2,1)}, bf16[128,2048]{1,0:T(8,128)(2,1)S(1)}, u32[]{:S(2)}, u32[]{:S(2)}) %collective-permute-start) | collective-permute-done | bytes 524320 | tf_op jit(solution)/shard_map/ppermute | solution.py:378
  17.0 0.0 copy-done.1
  17.0 0.0 copy-done.3
  17.0 3.9 %halo_sums.1 = (bf16[144,2048]{1,0:T(8,128)(2,1)S(1)}, f32[136,128]{1,0:T(8,128)S(1)}, bf16[136,640]{1,0:T(8,128)(2,1)S(1)}) custom-call(bf16[2048,256]{1,0:T(8,128)(2,1)S(1)} %get-tuple-element.23.table_ref, f32[8,2048]{1,0:T(8,128)S(1)} %get-tuple-element.24.wide_ref, ...), custom_call_target="tpu_custom_call", output_to_operand_aliasing={{2}: (8, {})} | custom-call | flops 1 | bytes 1 | tf_op jit(solution)/shard_map/halo_sums/pallas_call | solution.py:431
  20.8 2.4 %collective-permute-start.1 = (f32[136,128]{1,0:T(8,128)S(1)}, f32[136,128]{1,0:T(8,128)S(1)}, u32[]{:S(2)}, u32[]{:S(2)}) collective-permute-start(f32[136,128]{1,0:T(8,128)S(1)} %get-tuple-element.29.own_ref), channel_id=1, source_target_pairs={{0,4},{4,0},{8,12},{12,8},{16,20},{20,16},{24,28},{28,24},{1,5},{5... | collective-permute-start | bytes 208904 | tf_op jit(solution)/shard_map/ppermute | solution.py:378
  23.3 1.3 %collective-permute-start.5 = (bf16[136,640]{1,0:T(8,128)(2,1)S(1)}, bf16[136,640]{1,0:T(8,128)(2,1)S(1)}, u32[]{:S(2)}, u32[]{:S(2)}) collective-permute-start(bf16[136,640]{1,0:T(8,128)(2,1)S(1)} %get-tuple-element.37), channel_id=1, source_target_pairs={{4,0},{8,4},{12,8},{16,12},{20,16},{24,20},{28,24},{5,1},{9,5},{13... | collective-permute-start | bytes 522248 | tf_op jit(solution)/shard_map/ppermute | solution.py:378
  24.6 1.0 %collective-permute-done.1.other_ref = f32[136,128]{1,0:T(8,128)S(1)} collective-permute-done((f32[136,128]{1,0:T(8,128)S(1)}, f32[136,128]{1,0:T(8,128)S(1)}, u32[]{:S(2)}, u32[]{:S(2)}) %collective-permute-start.1) | collective-permute-done | bytes 69664 | tf_op jit(solution)/shard_map/ppermute | solution.py:378
  25.6 3.8 %collective-permute-start.2 = (f32[136,128]{1,0:T(8,128)S(1)}, f32[136,128]{1,0:T(8,128)S(1)}, u32[]{:S(2)}, u32[]{:S(2)}) collective-permute-start(f32[136,128]{1,0:T(8,128)S(1)} %get-tuple-element.31.own_ref), channel_id=1, source_target_pairs={{0,8},{4,12},{8,0},{12,4},{16,24},{20,28},{24,16},{28,20},{1,9},{5... | collective-permute-start | bytes 208904 | tf_op jit(solution)/shard_map/ppermute | solution.py:378
  29.4 1.3 %collective-permute-start.6 = (bf16[136,384]{1,0:T(8,128)(2,1)S(1)}, bf16[136,384]{1,0:T(8,128)(2,1)S(1)}, u32[]{:S(2)}, u32[]{:S(2)}) collective-permute-start(bf16[136,384]{1,0:T(8,128)(2,1)S(1)} %get-tuple-element.38), channel_id=1, source_target_pairs={{4,0},{8,4},{12,8},{16,12},{20,16},{24,20},{28,24},{5,1},{9,5},{13... | collective-permute-start | bytes 313352 | tf_op jit(solution)/shard_map/ppermute | solution.py:378
  30.7 0.0 collective-permute-done.3.rest_0_
  30.7 1.9 %input_grad.2.rest_0_ = bf16[128,2048]{1,0:T(8,128)(2,1)} custom-call(bf16[2048,256]{1,0:T(8,128)(2,1)S(1)} %get-tuple-element.23.table_ref, bf16[2048,256]{1,0:T(8,128)(2,1)S(1)} %get-tuple-element.32.back_ref, f32[8,2048]{1,0:T(8,128)S(1)} %get-tuple-element.24.wide_ref, bf16[128,2048]{1,0:T(8,128)(2,1)S(1)} %copy-done.1, ...), custom_call_target="tpu_custom_call" | custom-call | flops 1 | bytes 1 | tf_op jit(solution)/shard_map/input_grad/pallas_call | solution.py:459
  32.6 0.0 collective-permute-done.2.other_ref
  32.6 3.7 %collective-permute-start.4 = (f32[136,128]{1,0:T(8,128)S(1)}, f32[136,128]{1,0:T(8,128)S(1)}, u32[]{:S(2)}, u32[]{:S(2)}) collective-permute-start(f32[136,128]{1,0:T(8,128)S(1)} %get-tuple-element.36.own_ref), channel_id=1, source_target_pairs={{0,16},{4,20},{8,24},{12,28},{16,0},{20,4},{24,8},{28,12},{1,17},{... | collective-permute-start | bytes 208904 | tf_op jit(solution)/shard_map/ppermute | solution.py:378
  36.3 0.0 collective-permute-done.6.rest_1_
  36.3 0.0 collective-permute-done.5.rest_0_
  36.3 1.8 %input_grad.3.held_ref = bf16[128,2048]{1,0:T(8,128)(2,1)} custom-call(bf16[2048,256]{1,0:T(8,128)(2,1)S(1)} %get-tuple-element.23.table_ref, bf16[2048,256]{1,0:T(8,128)(2,1)S(1)} %get-tuple-element.32.back_ref, f32[8,2048]{1,0:T(8,128)S(1)} %get-tuple-element.24.wide_ref, bf16[128,2048]{1,0:T(8,128)(2,1)S(1)} %copy-done.1, ...), custom_call_target="tpu_custom_call", output_to_operand_aliasing={{}: (8, {})} | custom-call | flops 1 | bytes 1 | tf_op jit(solution)/shard_map/input_grad/pallas_call | solution.py:459
  38.2 0.5 %collective-permute-done.4.other_ref = f32[136,128]{1,0:T(8,128)S(1)} collective-permute-done((f32[136,128]{1,0:T(8,128)S(1)}, f32[136,128]{1,0:T(8,128)S(1)}, u32[]{:S(2)}, u32[]{:S(2)}) %collective-permute-start.4) | collective-permute-done | bytes 69664 | tf_op jit(solution)/shard_map/ppermute | solution.py:378
  38.6 0.6 %finish_sums.1 = (f32[128,128]{1,0:T(8,128)}, f32[7,128]{1,0:T(8,128)}, bf16[128,2048]{1,0:T(8,128)(2,1)}) custom-call(f32[136,128]{1,0:T(8,128)S(1)} %get-tuple-element.36.own_ref, f32[136,128]{1,0:T(8,128)S(1)} %collective-permute-done.4.other_ref, bf16[128,2048]{1,0:T(8,128)(2,1)} %input_grad.3.held_ref), custom_call_target="tpu_custom_call", output_to_operand_aliasing={{2}: (2, {})} | custom-call | flops 1 | bytes 16777216 | tf_op jit(solution)/shard_map/finish_sums/pallas_call | solution.py:356
  (3 shorter events, 0.0 us)
Async XLA Ops:
  0.6 5.8 %copy-start.4 = (bf16[128,128]{1,0:T(8,128)(2,1)S(1)}, bf16[128,128]{1,0:T(8,128)(2,1)}, u32[]{:S(2)}) copy-start(bf16[128,128]{1,0:T(8,128)(2,1)} %param.6) | copy-start | bytes 98308
  0.6 16.3 %collective-permute-start = (bf16[128,2048]{1,0:T(8,128)(2,1)}, bf16[128,2048]{1,0:T(8,128)(2,1)S(1)}, u32[]{:S(2)}, u32[]{:S(2)}) collective-permute-start(bf16[128,2048]{1,0:T(8,128)(2,1)} %x_ref.7), channel_id=1, source_target_pairs={{0,4},{4,8},{8,12},{12,16},{16,20},{20,24},{24,28},{1,5},{5,9},{9,... | collective-permute-start | bytes 1572872 | tf_op jit(solution)/shard_map/ppermute | solution.py:378
  5.5 0.9 %copy-start.5 = (bf16[128,7]{0,1:T(8,128)(2,1)S(1)}, bf16[128,7]{0,1:T(8,128)(2,1)}, u32[]{:S(2)}) copy-start(bf16[128,7]{0,1:T(8,128)(2,1)} %param.7) | copy-start | bytes 5380
  6.5 1.0 %copy-start = (bf16[128,2048]{1,0:T(8,128)(2,1)S(1)}, bf16[128,2048]{1,0:T(8,128)(2,1)}, u32[]{:S(2)}) copy-start(bf16[128,2048]{1,0:T(8,128)(2,1)} %x_ref.7) | copy-start | bytes 1572868
  7.6 1.0 %copy-start.2 = (bf16[128,2048]{1,0:T(8,128)(2,1)S(1)}, bf16[128,2048]{1,0:T(8,128)(2,1)}, u32[]{:S(2)}) copy-start(bf16[128,2048]{1,0:T(8,128)(2,1)} %u_ref.3) | copy-start | bytes 1572868
  8.6 8.4 %copy-start.1 = (bf16[128,2048]{1,0:T(8,128)(2,1)S(1)}, bf16[128,2048]{1,0:T(8,128)(2,1)}, u32[]{:S(2)}) copy-start(bf16[128,2048]{1,0:T(8,128)(2,1)} %x_ref.7) | copy-start | bytes 1572868
  8.6 8.4 %copy-start.3 = (bf16[128,2048]{1,0:T(8,128)(2,1)S(1)}, bf16[128,2048]{1,0:T(8,128)(2,1)}, u32[]{:S(2)}) copy-start(bf16[128,2048]{1,0:T(8,128)(2,1)} %u_ref.3) | copy-start | bytes 1572868
  13.8 16.9 %collective-permute-start.3 = (bf16[136,1024]{1,0:T(8,128)(2,1)S(1)}, bf16[136,1024]{1,0:T(8,128)(2,1)S(1)}, u32[]{:S(2)}, u32[]{:S(2)}) collective-permute-start(bf16[136,1024]{1,0:T(8,128)(2,1)S(1)} %get-tuple-element.35), channel_id=1, source_target_pairs={{4,0},{8,4},{12,8},{16,12},{20,16},{24,20},{28,24},{5,1},{9,5},{13... | collective-permute-start | bytes 835592 | tf_op jit(solution)/shard_map/ppermute | solution.py:378
  20.8 4.7 %collective-permute-start.1 = (f32[136,128]{1,0:T(8,128)S(1)}, f32[136,128]{1,0:T(8,128)S(1)}, u32[]{:S(2)}, u32[]{:S(2)}) collective-permute-start(f32[136,128]{1,0:T(8,128)S(1)} %get-tuple-element.29.own_ref), channel_id=1, source_target_pairs={{0,4},{4,0},{8,12},{12,8},{16,20},{20,16},{24,28},{28,24},{1,5},{5... | collective-permute-start | bytes 208904 | tf_op jit(solution)/shard_map/ppermute | solution.py:378
  23.3 13.0 %collective-permute-start.5 = (bf16[136,640]{1,0:T(8,128)(2,1)S(1)}, bf16[136,640]{1,0:T(8,128)(2,1)S(1)}, u32[]{:S(2)}, u32[]{:S(2)}) collective-permute-start(bf16[136,640]{1,0:T(8,128)(2,1)S(1)} %get-tuple-element.37), channel_id=1, source_target_pairs={{4,0},{8,4},{12,8},{16,12},{20,16},{24,20},{28,24},{5,1},{9,5},{13... | collective-permute-start | bytes 522248 | tf_op jit(solution)/shard_map/ppermute | solution.py:378
  25.6 7.0 %collective-permute-start.2 = (f32[136,128]{1,0:T(8,128)S(1)}, f32[136,128]{1,0:T(8,128)S(1)}, u32[]{:S(2)}, u32[]{:S(2)}) collective-permute-start(f32[136,128]{1,0:T(8,128)S(1)} %get-tuple-element.31.own_ref), channel_id=1, source_target_pairs={{0,8},{4,12},{8,0},{12,4},{16,24},{20,28},{24,16},{28,20},{1,9},{5... | collective-permute-start | bytes 208904 | tf_op jit(solution)/shard_map/ppermute | solution.py:378
  29.4 6.9 %collective-permute-start.6 = (bf16[136,384]{1,0:T(8,128)(2,1)S(1)}, bf16[136,384]{1,0:T(8,128)(2,1)S(1)}, u32[]{:S(2)}, u32[]{:S(2)}) collective-permute-start(bf16[136,384]{1,0:T(8,128)(2,1)S(1)} %get-tuple-element.38), channel_id=1, source_target_pairs={{4,0},{8,4},{12,8},{16,12},{20,16},{24,20},{28,24},{5,1},{9,5},{13... | collective-permute-start | bytes 313352 | tf_op jit(solution)/shard_map/ppermute | solution.py:378
  32.6 6.1 %collective-permute-start.4 = (f32[136,128]{1,0:T(8,128)S(1)}, f32[136,128]{1,0:T(8,128)S(1)}, u32[]{:S(2)}, u32[]{:S(2)}) collective-permute-start(f32[136,128]{1,0:T(8,128)S(1)} %get-tuple-element.36.own_ref), channel_id=1, source_target_pairs={{0,16},{4,20},{8,24},{12,28},{16,0},{20,4},{24,8},{28,12},{1,17},{... | collective-permute-start | bytes 208904 | tf_op jit(solution)/shard_map/ppermute | solution.py:378

commit v5 on v4

--- a/solution.py
+++ b/solution.py
@@ -11,9 +11,6 @@
 ROWS = 16
 EDGE = 8
 LANES = 128
-PIECES = (8, 5, 3)
-ISSUE = (0, 1, 2)
-EARLY = 1
 F32 = jnp.float32
 BF16 = jnp.bfloat16
 LONG = pl.CostEstimate(flops=1, bytes_accessed=16 << 20, transcendentals=0)
@@ -186,77 +183,71 @@
             ).astype(BF16)
 
 
-def halo_kernel(taps, factor, cols, table_ref, wide_ref, prev_ref, x_ref, u_ref, turned_ref,
+def halo_kernel(taps, factor, table_ref, wide_ref, prev_ref, x_ref, u_ref, turned_ref,
                 conv_ref, medium_ref, *rest):
     gate_cot_ref, sums_ref = rest[len(rest) // 2 - 1 :][:2]
     rows, width = x_ref.shape
     med = prev_ref.shape[0]
     window = med + ROWS
     lanes = med + 128
-    tile = LANES // GROUP
-    groups = cols // GROUP
     total_groups = sums_ref.shape[0] - 8
     upturn = turning(ROWS)
     lane_group = lane_groups()
 
-    def one_step(step, total):
-        diagonals, short = [], []
-        for block in range(cols // LANES):
-            start = step * cols + block * LANES
-            at = slice(start, start + LANES)
-            prev, x, u = prev_ref[:, at], x_ref[:, at], u_ref[:, at]
-            near = jnp.concatenate([prev[med - ROWS :], x], 0).astype(F32)
-            table = table_ref[at, :med]
-            head = gated(wide_ref[:, at], near[: 2 * ROWS], taps) * u[:ROWS].astype(F32)
-            head = head.astype(BF16)
-            gate_cot_ref[:ROWS, at] = head
-            head = jnp.dot(upturn, head, preferred_element_type=F32).astype(BF16)
-
-            pairs = None
-            gate_cots = []
-            for a in range(0, rows // ROWS, 2):
-                lo, mid, hi = (ROWS * k for k in (a, a + 1, a + 2))
-                part = jnp.concatenate(
-                    [stacked(prev, x, lo, med), stacked(prev, x, mid, med + ROWS)], 1
+    diagonals, short = [], []
+    for start in range(0, width, LANES):
+        at = slice(start, start + LANES)
+        prev, x, u = prev_ref[:, at], x_ref[:, at], u_ref[:, at]
+        near = jnp.concatenate([prev[med - ROWS :], x], 0).astype(F32)
+        table = table_ref[at, :med]
+        head = gated(wide_ref[:, at], near[: 2 * ROWS], taps) * u[:ROWS].astype(F32)
+        head = head.astype(BF16)
+        gate_cot_ref[:ROWS, at] = head
+        head = jnp.dot(upturn, head, preferred_element_type=F32).astype(BF16)
+
+        pairs = None
+        gate_cots = []
+        for a in range(0, rows // ROWS, 2):
+            lo, mid, hi = (ROWS * k for k in (a, a + 1, a + 2))
+            part = jnp.concatenate(
+                [stacked(prev, x, lo, med), stacked(prev, x, mid, med + ROWS)], 1
+            )
+            conv = own_group(
+                jnp.dot(table[:, : med - lo], part, preferred_element_type=F32),
+                lane_group,
+            )
+            if a == 0:
+                part = jnp.concatenate([part, jnp.concatenate([x[:ROWS], x[ROWS:hi]], 1)], 0)
+                both = jnp.concatenate([head, turned_ref[mid:hi, at]], 1)
+            else:
+                both = jnp.concatenate([turned_ref[lo:mid, at], turned_ref[mid:hi, at]], 1)
+            more = contracted(masked(both, lane_group), part)
+            if more.shape[1] < window:
+                more = jnp.concatenate(
+                    [more, jnp.zeros((LANES, window - more.shape[1]), F32)], 1
                 )
-                conv = own_group(
-                    jnp.dot(table[:, : med - lo], part, preferred_element_type=F32),
-                    lane_group,
-                )
-                if a == 0:
-                    part = jnp.concatenate([part, jnp.concatenate([x[:ROWS], x[ROWS:hi]], 1)], 0)
-                    both = jnp.concatenate([head, turned_ref[mid:hi, at]], 1)
-                else:
-                    both = jnp.concatenate([turned_ref[lo:mid, at], turned_ref[mid:hi, at]], 1)
-                more = contracted(masked(both, lane_group), part)
-                if more.shape[1] < window:
-                    more = jnp.concatenate(
-                        [more, jnp.zeros((LANES, window - more.shape[1]), F32)], 1
-                    )
-                pairs = more if pairs is None else pairs + more
-                for k in range(2):
-                    here = slice(lo + k * ROWS, mid + k * ROWS)
-                    whole = conv_ref[here, at] + conv[:, k * LANES : (k + 1) * LANES]
-                    gate_cots.append((u[here].astype(F32) * whole).astype(BF16))
-            gate_cot = jnp.concatenate(gate_cots, 0)
-            gate_cot_ref[ROWS:, at] = gate_cot
-            diagonals += diagonal_sums(pairs, lanes)
-            gate_cot = gate_cot.astype(F32)
-            sums = [
-                jnp.sum(gate_cot * delayed(near, j)[ROWS:], 0, keepdims=True)
-                for j in range(taps)
-            ]
-            short.append(jnp.concatenate(sums + [jnp.zeros((8 - taps, LANES), F32)], 0))
-
-        mine = slice(step * groups, (step + 1) * groups)
-        medium = medium_ref[mine, :] + medium_sums(diagonals, med, lanes)
-        sums_ref[mine, :] = medium * factor
-        gather = iota((cols, med), 1) == step * groups + iota((cols, med), 0) // GROUP
-        return total + exact_dot(jnp.concatenate(short, 1), gather.astype(BF16))
-
-    total = jnp.zeros((8, med), F32)
-    for step in range(width // cols):
-        total = one_step(step, total)
+            pairs = more if pairs is None else pairs + more
+            for k in range(2):
+                here = slice(lo + k * ROWS, mid + k * ROWS)
+                whole = conv_ref[here, at] + conv[:, k * LANES : (k + 1) * LANES]
+                gate_cots.append((u[here].astype(F32) * whole).astype(BF16))
+        gate_cot = jnp.concatenate(gate_cots, 0)
+        gate_cot_ref[ROWS:, at] = gate_cot
+        diagonals += diagonal_sums(pairs, lanes)
+        gate_cot = gate_cot.astype(F32)
+        sums = [
+            jnp.sum(gate_cot * delayed(near, j)[ROWS:], 0, keepdims=True)
+            for j in range(taps)
+        ]
+        short.append(jnp.concatenate(sums + [jnp.zeros((8 - taps, LANES), F32)], 0))
+
+    sums_ref[:total_groups, :] = (medium_ref[...] + medium_sums(diagonals, med, lanes)) * factor
+    gather = (iota((LANES, med), 1) == iota((LANES, med), 0) // GROUP).astype(BF16)
+    gathered = exact_dot(jnp.concatenate(short, 0), gather)
+    total = gathered[:8]
+    for block in range(1, width // LANES):
+        part = gathered[8 * block : 8 * (block + 1)]
+        total = total + pltpu.roll(part, block * (LANES // GROUP), 1)
     sums_ref[total_groups:, :] = total * factor
 
 
@@ -385,19 +376,19 @@
     devices = lax.axis_size("ctx")
     assert rows == med and med % 128 == 0 and groups <= med
     assert taps <= 8 and width % LANES == 0
-    strip = min(width, 8 * LANES)
     lanes = med + 128
     factor = float(GROUP * rows * devices) ** -0.5
     forward = [(i, i + 1) for i in range(devices - 1)]
     backward = [(i + 1, i) for i in range(devices - 1)]
 
-    def params(mebibytes=40):
-        return pltpu.CompilerParams(vmem_limit_bytes=mebibytes << 20)
+    def params():
+        return pltpu.CompilerParams(vmem_limit_bytes=40 << 20)
 
     short_rows = jnp.pad(short_filter.T, ((0, 8 - taps), (0, 0)))
     previous = permuted(inputs, forward)
     resident = pl.BlockSpec(memory_space=pltpu.VMEM)
-    sizes = PIECES if width == LANES * sum(PIECES) else (width // LANES,)
+    count = width // LANES
+    sizes = (count // 2, 5 * count // 16, 3 * count // 16) if count % 16 == 0 else (count,)
     ends = [LANES * sum(sizes[: k + 1]) for k in range(len(sizes))]
     pieces = [(end - LANES * size, end) for end, size in zip(ends, sizes)]
     both = jnp.pad(medium_filter, ((0, 0), (0, lanes - med))) + jnp.pad(
@@ -426,10 +417,10 @@
     following = [permuted(sends[0], backward)]
 
     halo_in = [table, wide, previous, inputs, upstream, turned, conv, medium]
-    waiting = [k for k in range(len(pieces)) if ISSUE[k] == 1]
+    waiting = [k for k in range(len(pieces)) if k == 1]
     held = [sends[k] for k in waiting]
     gate_cot, sums, *held = pl.pallas_call(
-        functools.partial(halo_kernel, taps, factor, strip),
+        functools.partial(halo_kernel, taps, factor),
         in_specs=[resident] * len(halo_in) + [pl.BlockSpec(memory_space=pl.ANY)] * len(held),
         out_specs=[resident] * 2 + [pl.BlockSpec(memory_space=pl.ANY)] * len(held),
         out_shape=[
@@ -480,15 +471,15 @@
     others = jnp.zeros_like(sums)
     for stage in range(stages):
         if devices & (devices - 1) == 0:
-            others = permuted(sums, [(i, i ^ (1 << ((0, 1, 2)[stage] if stages == 3 else stage))) for i in range(devices)])
-        if len(following) < len(pieces) and ISSUE[len(following)] == stage + 1:
-            following.append(permuted(sends[len(following)], backward))
+            others = permuted(sums, [(i, i ^ (1 << stage)) for i in range(devices)])
+        if stage + 1 < len(pieces):
+            following.append(permuted(sends[stage + 1], backward))
         last = stage == stages - 1
-        if len(pieces) > 1 and stage == EARLY and not last:
+        if len(pieces) > 1 and stage == 1 and not last:
             gradient = input_grad([0], None)
         if last:
             break
-        waiting = [k for k in range(len(pieces)) if ISSUE[k] == stage + 2]
+        waiting = [k for k in range(len(pieces)) if k == stage + 2]
         held = [sends[k] for k in waiting] + ([] if gradient is None else [gradient])
         sums, *held = add_after(sums, others, *held)
         if gradient is not None:

time: 39.6 us -> 39.8 us (level)
  no operation moved by 1% of the time
where the time goes in v5:
time: 39.8 us; the launch traced here: 39.4 us
  starting transfers between devices  19 us (48%)
  Pallas kernels  13.2 us (33%)
  waiting for transfers between devices  3.31 us (8%)
  local copies, waits for them, and re-layouts  2.97 us (7%)
  between operations  0.76 us (2%)
    ppermute x7, starting transfers between devices, permuted(): return lax.ppermute(block, 'ctx', pairs)  19 us
    pallas_call x1, Pallas kernels, local(): pl.pallas_call(functools.partial(own_kernel, taps, pieces, min(width, 4 *...  5.18 us
    pallas_call x2, Pallas kernels, input_grad(): pl.pallas_call(functools.partial(back_kernel, taps, mine), in_specs=in_sp...  3.71 us
    pallas_call x1, Pallas kernels, local(): pl.pallas_call(functools.partial(halo_kernel, taps, factor), in_specs=[re...  3.69 us
    ppermute x7, waiting for transfers between devices, permuted(): return lax.ppermute(block, 'ctx', pairs)  3.31 us
    unnamed x13, local copies, waits for them, and re-layouts  2.97 us
  transfers between devices with their start and end apart: 7, of which 3 were waited for; matrix products, arithmetic and copies ran while one was open for 2% of the time, Pallas kernels for 32%

profile of v5, /device:TPU:0, one launch (start us, length us, event | category | flops | bytes accessed | tf_op | source)
XLA Modules:
  0.0 39.4 jit_solution(3675304304706271460)
XLA Ops:
  0.6 0.0 copy-start.4
  0.6 4.9 %collective-permute-start = (bf16[128,2048]{1,0:T(8,128)(2,1)}, bf16[128,2048]{1,0:T(8,128)(2,1)S(1)}, u32[]{:S(2)}, u32[]{:S(2)}) collective-permute-start(bf16[128,2048]{1,0:T(8,128)(2,1)} %x_ref.7), channel_id=1, source_target_pairs={{0,4},{4,8},{8,12},{12,16},{16,20},{20,24},{24,28},{1,5},{5,9},{9,... | collective-permute-start | bytes 1572872 | tf_op jit(solution)/shard_map/ppermute | solution.py:369
  5.5 0.0 copy-start.5
  5.5 0.9 %copy.12 = bf16[128,7]{1,0:T(8,128)(2,1)S(1)} copy(bf16[128,7]{0,1:T(8,128)(2,1)} %param.7) | data formatting | bytes 3584 | tf_op args[3]
  6.4 0.0 copy-done.5
  6.4 0.0 copy-done.4
  6.4 0.1 pad_add_fusion.ms_ref
  6.5 0.0 copy-start
  6.5 1.0 %copy-done = bf16[128,2048]{1,0:T(8,128)(2,1)S(1)} copy-done((bf16[128,2048]{1,0:T(8,128)(2,1)S(1)}, bf16[128,2048]{1,0:T(8,128)(2,1)}, u32[]{:S(2)}) %copy-start) | copy-done | bytes 524312
  7.6 0.0 copy-start.2
  7.6 1.0 %copy-done.2 = bf16[128,2048]{1,0:T(8,128)(2,1)S(1)} copy-done((bf16[128,2048]{1,0:T(8,128)(2,1)S(1)}, bf16[128,2048]{1,0:T(8,128)(2,1)}, u32[]{:S(2)}) %copy-start.2) | copy-done | bytes 524312
  8.6 0.0 copy-start.1
  8.6 0.0 copy-start.3
  8.6 5.2 %own_block.1 = (bf16[136,1024]{1,0:T(8,128)(2,1)S(1)}, bf16[136,640]{1,0:T(8,128)(2,1)S(1)}, bf16[136,384]{1,0:T(8,128)(2,1)S(1)}, bf16[128,2048]{1,0:T(8,128)(2...) custom-call(bf16[128,256]{1,0:T(8,128)(2,1)S(1)} %pad_add_fusion.ms_, ...), custom_call_target="tpu_custom_call" | custom-call | flops 1 | bytes 1 | tf_op jit(solution)/shard_map/own_block/pallas_call | solution.py:397
  13.8 1.3 %collective-permute-start.3 = (bf16[136,1024]{1,0:T(8,128)(2,1)S(1)}, bf16[136,1024]{1,0:T(8,128)(2,1)S(1)}, u32[]{:S(2)}, u32[]{:S(2)}) collective-permute-start(bf16[136,1024]{1,0:T(8,128)(2,1)S(1)} %get-tuple-element.35), channel_id=1, source_target_pairs={{4,0},{8,4},{12,8},{16,12},{20,16},{24,20},{28,24},{5,1},{9,5},{13... | collective-permute-start | bytes 835592 | tf_op jit(solution)/shard_map/ppermute | solution.py:369
  15.1 1.9 %collective-permute-done.prev_ref = bf16[128,2048]{1,0:T(8,128)(2,1)S(1)} collective-permute-done((bf16[128,2048]{1,0:T(8,128)(2,1)}, bf16[128,2048]{1,0:T(8,128)(2,1)S(1)}, u32[]{:S(2)}, u32[]{:S(2)}) %collective-permute-start) | collective-permute-done | bytes 524320 | tf_op jit(solution)/shard_map/ppermute | solution.py:369
  17.0 0.0 copy-done.1
  17.0 0.0 copy-done.3
  17.0 3.7 %halo_sums.1 = (bf16[144,2048]{1,0:T(8,128)(2,1)S(1)}, f32[136,128]{1,0:T(8,128)S(1)}, bf16[136,640]{1,0:T(8,128)(2,1)S(1)}) custom-call(bf16[2048,256]{1,0:T(8,128)(2,1)S(1)} %get-tuple-element.23.table_ref, f32[8,2048]{1,0:T(8,128)S(1)} %get-tuple-element.24.wide_ref, ...), custom_call_target="tpu_custom_call", output_to_operand_aliasing={{2}: (8, {})} | custom-call | flops 1 | bytes 1 | tf_op jit(solution)/shard_map/halo_sums/pallas_call | solution.py:422
  20.7 2.4 %collective-permute-start.1 = (f32[136,128]{1,0:T(8,128)S(1)}, f32[136,128]{1,0:T(8,128)S(1)}, u32[]{:S(2)}, u32[]{:S(2)}) collective-permute-start(f32[136,128]{1,0:T(8,128)S(1)} %get-tuple-element.29.own_ref), channel_id=1, source_target_pairs={{0,4},{4,0},{8,12},{12,8},{16,20},{20,16},{24,28},{28,24},{1,5},{5... | collective-permute-start | bytes 208904 | tf_op jit(solution)/shard_map/ppermute | solution.py:369
  23.1 1.3 %collective-permute-start.5 = (bf16[136,640]{1,0:T(8,128)(2,1)S(1)}, bf16[136,640]{1,0:T(8,128)(2,1)S(1)}, u32[]{:S(2)}, u32[]{:S(2)}) collective-permute-start(bf16[136,640]{1,0:T(8,128)(2,1)S(1)} %get-tuple-element.37), channel_id=1, source_target_pairs={{4,0},{8,4},{12,8},{16,12},{20,16},{24,20},{28,24},{5,1},{9,5},{13... | collective-permute-start | bytes 522248 | tf_op jit(solution)/shard_map/ppermute | solution.py:369
  24.4 1.0 %collective-permute-done.1.other_ref = f32[136,128]{1,0:T(8,128)S(1)} collective-permute-done((f32[136,128]{1,0:T(8,128)S(1)}, f32[136,128]{1,0:T(8,128)S(1)}, u32[]{:S(2)}, u32[]{:S(2)}) %collective-permute-start.1) | collective-permute-done | bytes 69664 | tf_op jit(solution)/shard_map/ppermute | solution.py:369
  25.4 3.8 %collective-permute-start.2 = (f32[136,128]{1,0:T(8,128)S(1)}, f32[136,128]{1,0:T(8,128)S(1)}, u32[]{:S(2)}, u32[]{:S(2)}) collective-permute-start(f32[136,128]{1,0:T(8,128)S(1)} %get-tuple-element.31.own_ref), channel_id=1, source_target_pairs={{0,8},{4,12},{8,0},{12,4},{16,24},{20,28},{24,16},{28,20},{1,9},{5... | collective-permute-start | bytes 208904 | tf_op jit(solution)/shard_map/ppermute | solution.py:369
  29.2 1.3 %collective-permute-start.6 = (bf16[136,384]{1,0:T(8,128)(2,1)S(1)}, bf16[136,384]{1,0:T(8,128)(2,1)S(1)}, u32[]{:S(2)}, u32[]{:S(2)}) collective-permute-start(bf16[136,384]{1,0:T(8,128)(2,1)S(1)} %get-tuple-element.38), channel_id=1, source_target_pairs={{4,0},{8,4},{12,8},{16,12},{20,16},{24,20},{28,24},{5,1},{9,5},{13... | collective-permute-start | bytes 313352 | tf_op jit(solution)/shard_map/ppermute | solution.py:369
  30.5 0.0 collective-permute-done.3.rest_0_
  30.5 1.9 %input_grad.2.rest_0_ = bf16[128,2048]{1,0:T(8,128)(2,1)} custom-call(bf16[2048,256]{1,0:T(8,128)(2,1)S(1)} %get-tuple-element.23.table_ref, bf16[2048,256]{1,0:T(8,128)(2,1)S(1)} %get-tuple-element.32.back_ref, f32[8,2048]{1,0:T(8,128)S(1)} %get-tuple-element.24.wide_ref, bf16[128,2048]{1,0:T(8,128)(2,1)S(1)} %copy-done.1, ...), custom_call_target="tpu_custom_call" | custom-call | flops 1 | bytes 1 | tf_op jit(solution)/shard_map/input_grad/pallas_call | solution.py:450
  32.4 0.0 collective-permute-done.2.other_ref
  32.4 4.0 %collective-permute-start.4 = (f32[136,128]{1,0:T(8,128)S(1)}, f32[136,128]{1,0:T(8,128)S(1)}, u32[]{:S(2)}, u32[]{:S(2)}) collective-permute-start(f32[136,128]{1,0:T(8,128)S(1)} %get-tuple-element.36.own_ref), channel_id=1, source_target_pairs={{0,16},{4,20},{8,24},{12,28},{16,0},{20,4},{24,8},{28,12},{1,17},{... | collective-permute-start | bytes 208904 | tf_op jit(solution)/shard_map/ppermute | solution.py:369
  36.5 0.0 collective-permute-done.6.rest_1_
  36.5 0.0 collective-permute-done.5.rest_0_
  36.5 1.9 %input_grad.3.held_ref = bf16[128,2048]{1,0:T(8,128)(2,1)} custom-call(bf16[2048,256]{1,0:T(8,128)(2,1)S(1)} %get-tuple-element.23.table_ref, bf16[2048,256]{1,0:T(8,128)(2,1)S(1)} %get-tuple-element.32.back_ref, f32[8,2048]{1,0:T(8,128)S(1)} %get-tuple-element.24.wide_ref, bf16[128,2048]{1,0:T(8,128)(2,1)S(1)} %copy-done.1, ...), custom_call_target="tpu_custom_call", output_to_operand_aliasing={{}: (8, {})} | custom-call | flops 1 | bytes 1 | tf_op jit(solution)/shard_map/input_grad/pallas_call | solution.py:450
  38.3 0.4 %collective-permute-done.4.other_ref = f32[136,128]{1,0:T(8,128)S(1)} collective-permute-done((f32[136,128]{1,0:T(8,128)S(1)}, f32[136,128]{1,0:T(8,128)S(1)}, u32[]{:S(2)}, u32[]{:S(2)}) %collective-permute-start.4) | collective-permute-done | bytes 69664 | tf_op jit(solution)/shard_map/ppermute | solution.py:369
  38.8 0.6 %finish_sums.1 = (f32[128,128]{1,0:T(8,128)}, f32[7,128]{1,0:T(8,128)}, bf16[128,2048]{1,0:T(8,128)(2,1)}) custom-call(f32[136,128]{1,0:T(8,128)S(1)} %get-tuple-element.36.own_ref, f32[136,128]{1,0:T(8,128)S(1)} %collective-permute-done.4.other_ref, bf16[128,2048]{1,0:T(8,128)(2,1)} %input_grad.3.held_ref), custom_call_target="tpu_custom_call", output_to_operand_aliasing={{2}: (2, {})} | custom-call | flops 1 | bytes 16777216 | tf_op jit(solution)/shard_map/finish_sums/pallas_call | solution.py:347
  (3 shorter events, 0.0 us)
Async XLA Ops:
  0.6 5.8 %copy-start.4 = (bf16[128,128]{1,0:T(8,128)(2,1)S(1)}, bf16[128,128]{1,0:T(8,128)(2,1)}, u32[]{:S(2)}) copy-start(bf16[128,128]{1,0:T(8,128)(2,1)} %param.6) | copy-start | bytes 98308
  0.6 16.3 %collective-permute-start = (bf16[128,2048]{1,0:T(8,128)(2,1)}, bf16[128,2048]{1,0:T(8,128)(2,1)S(1)}, u32[]{:S(2)}, u32[]{:S(2)}) collective-permute-start(bf16[128,2048]{1,0:T(8,128)(2,1)} %x_ref.7), channel_id=1, source_target_pairs={{0,4},{4,8},{8,12},{12,16},{16,20},{20,24},{24,28},{1,5},{5,9},{9,... | collective-permute-start | bytes 1572872 | tf_op jit(solution)/shard_map/ppermute | solution.py:369
  5.5 0.9 %copy-start.5 = (bf16[128,7]{0,1:T(8,128)(2,1)S(1)}, bf16[128,7]{0,1:T(8,128)(2,1)}, u32[]{:S(2)}) copy-start(bf16[128,7]{0,1:T(8,128)(2,1)} %param.7) | copy-start | bytes 5380
  6.5 1.0 %copy-start = (bf16[128,2048]{1,0:T(8,128)(2,1)S(1)}, bf16[128,2048]{1,0:T(8,128)(2,1)}, u32[]{:S(2)}) copy-start(bf16[128,2048]{1,0:T(8,128)(2,1)} %x_ref.7) | copy-start | bytes 1572868
  7.6 1.0 %copy-start.2 = (bf16[128,2048]{1,0:T(8,128)(2,1)S(1)}, bf16[128,2048]{1,0:T(8,128)(2,1)}, u32[]{:S(2)}) copy-start(bf16[128,2048]{1,0:T(8,128)(2,1)} %u_ref.3) | copy-start | bytes 1572868
  8.6 8.4 %copy-start.1 = (bf16[128,2048]{1,0:T(8,128)(2,1)S(1)}, bf16[128,2048]{1,0:T(8,128)(2,1)}, u32[]{:S(2)}) copy-start(bf16[128,2048]{1,0:T(8,128)(2,1)} %x_ref.7) | copy-start | bytes 1572868
  8.6 8.4 %copy-start.3 = (bf16[128,2048]{1,0:T(8,128)(2,1)S(1)}, bf16[128,2048]{1,0:T(8,128)(2,1)}, u32[]{:S(2)}) copy-start(bf16[128,2048]{1,0:T(8,128)(2,1)} %u_ref.3) | copy-start | bytes 1572868
  13.8 16.7 %collective-permute-start.3 = (bf16[136,1024]{1,0:T(8,128)(2,1)S(1)}, bf16[136,1024]{1,0:T(8,128)(2,1)S(1)}, u32[]{:S(2)}, u32[]{:S(2)}) collective-permute-start(bf16[136,1024]{1,0:T(8,128)(2,1)S(1)} %get-tuple-element.35), channel_id=1, source_target_pairs={{4,0},{8,4},{12,8},{16,12},{20,16},{24,20},{28,24},{5,1},{9,5},{13... | collective-permute-start | bytes 835592 | tf_op jit(solution)/shard_map/ppermute | solution.py:369
  20.7 4.7 %collective-permute-start.1 = (f32[136,128]{1,0:T(8,128)S(1)}, f32[136,128]{1,0:T(8,128)S(1)}, u32[]{:S(2)}, u32[]{:S(2)}) collective-permute-start(f32[136,128]{1,0:T(8,128)S(1)} %get-tuple-element.29.own_ref), channel_id=1, source_target_pairs={{0,4},{4,0},{8,12},{12,8},{16,20},{20,16},{24,28},{28,24},{1,5},{5... | collective-permute-start | bytes 208904 | tf_op jit(solution)/shard_map/ppermute | solution.py:369
  23.1 13.3 %collective-permute-start.5 = (bf16[136,640]{1,0:T(8,128)(2,1)S(1)}, bf16[136,640]{1,0:T(8,128)(2,1)S(1)}, u32[]{:S(2)}, u32[]{:S(2)}) collective-permute-start(bf16[136,640]{1,0:T(8,128)(2,1)S(1)} %get-tuple-element.37), channel_id=1, source_target_pairs={{4,0},{8,4},{12,8},{16,12},{20,16},{24,20},{28,24},{5,1},{9,5},{13... | collective-permute-start | bytes 522248 | tf_op jit(solution)/shard_map/ppermute | solution.py:369
  25.4 7.0 %collective-permute-start.2 = (f32[136,128]{1,0:T(8,128)S(1)}, f32[136,128]{1,0:T(8,128)S(1)}, u32[]{:S(2)}, u32[]{:S(2)}) collective-permute-start(f32[136,128]{1,0:T(8,128)S(1)} %get-tuple-element.31.own_ref), channel_id=1, source_target_pairs={{0,8},{4,12},{8,0},{12,4},{16,24},{20,28},{24,16},{28,20},{1,9},{5... | collective-permute-start | bytes 208904 | tf_op jit(solution)/shard_map/ppermute | solution.py:369
  29.2 7.2 %collective-permute-start.6 = (bf16[136,384]{1,0:T(8,128)(2,1)S(1)}, bf16[136,384]{1,0:T(8,128)(2,1)S(1)}, u32[]{:S(2)}, u32[]{:S(2)}) collective-permute-start(bf16[136,384]{1,0:T(8,128)(2,1)S(1)} %get-tuple-element.38), channel_id=1, source_target_pairs={{4,0},{8,4},{12,8},{16,12},{20,16},{24,20},{28,24},{5,1},{9,5},{13... | collective-permute-start | bytes 313352 | tf_op jit(solution)/shard_map/ppermute | solution.py:369
  32.4 6.3 %collective-permute-start.4 = (f32[136,128]{1,0:T(8,128)S(1)}, f32[136,128]{1,0:T(8,128)S(1)}, u32[]{:S(2)}, u32[]{:S(2)}) collective-permute-start(f32[136,128]{1,0:T(8,128)S(1)} %get-tuple-element.36.own_ref), channel_id=1, source_target_pairs={{0,16},{4,20},{8,24},{12,28},{16,0},{20,4},{24,8},{28,12},{1,17},{... | collective-permute-start | bytes 208904 | tf_op jit(solution)/shard_map/ppermute | solution.py:369

commit v6 on v5

--- a/solution.py
+++ b/solution.py
@@ -388,14 +388,14 @@
     previous = permuted(inputs, forward)
     resident = pl.BlockSpec(memory_space=pltpu.VMEM)
     count = width // LANES
-    sizes = (count // 2, 5 * count // 16, 3 * count // 16) if count % 16 == 0 else (count,)
+    sizes = (count // 2, count // 4, count // 4) if count % 16 == 0 else (count,)
     ends = [LANES * sum(sizes[: k + 1]) for k in range(len(sizes))]
     pieces = [(end - LANES * size, end) for end, size in zip(ends, sizes)]
     both = jnp.pad(medium_filter, ((0, 0), (0, lanes - med))) + jnp.pad(
         short_filter, ((0, 0), (med + ROWS, lanes - med - ROWS - taps))
     )
     *sends, cot, turned, conv, medium, table, back, wide = pl.pallas_call(
-        functools.partial(own_kernel, taps, pieces, min(width, 4 * LANES)),
+        functools.partial(own_kernel, taps, pieces, min(width, 8 * LANES)),
         in_specs=[resident] * 4,
         out_specs=[resident] * (len(pieces) + 7),
         out_shape=[

time: 39.8 us -> 39.3 us (0.987)
  waiting for transfers between devices: 3.31 us -> 4.32 us
  Pallas kernels: 13.2 us -> 12.5 us
  starting transfers between devices: 19 us -> 18.3 us
    ppermute x7, waiting for transfers between devices: 3.31 us -> 4.32 us  [permuted(): return lax.ppermute(block, 'ctx', pairs)]
    pallas_call x1, Pallas kernels: 5.18 us -> 4.42 us  [local(): pl.pallas_call(functools.partial(own_kernel, taps, pieces, min(width, 8 *...]
    ppermute x7, starting transfers between devices: 19 us -> 18.3 us  [permuted(): return lax.ppermute(block, 'ctx', pairs)]
  transfers between devices with their start and end apart: 7 -> 7, of which waited for: 3 -> 4; matrix products, arithmetic and copies ran while one was open for 2% -> 2% of each run, Pallas kernels for 32% -> 30%
where the time goes in v6:
time: 39.3 us; the launch traced here: 38.9 us
  starting transfers between devices  18.3 us (47%)
  Pallas kernels  12.5 us (32%)
  waiting for transfers between devices  4.32 us (11%)
  local copies, waits for them, and re-layouts  2.97 us (8%)
  between operations  0.76 us (2%)
    ppermute x7, starting transfers between devices, permuted(): return lax.ppermute(block, 'ctx', pairs)  18.3 us
    pallas_call x1, Pallas kernels, local(): pl.pallas_call(functools.partial(own_kernel, taps, pieces, min(width, 8 *...  4.42 us
    ppermute x7, waiting for transfers between devices, permuted(): return lax.ppermute(block, 'ctx', pairs)  4.32 us
    pallas_call x2, Pallas kernels, input_grad(): pl.pallas_call(functools.partial(back_kernel, taps, mine), in_specs=in_sp...  3.7 us
    pallas_call x1, Pallas kernels, local(): pl.pallas_call(functools.partial(halo_kernel, taps, factor), in_specs=[re...  3.7 us
    unnamed x13, local copies, waits for them, and re-layouts  2.97 us
  transfers between devices with their start and end apart: 7, of which 4 were waited for; matrix products, arithmetic and copies ran while one was open for 2% of the time, Pallas kernels for 30%

profile of v6, /device:TPU:0, one launch (start us, length us, event | category | flops | bytes accessed | tf_op | source)
XLA Modules:
  0.0 38.9 jit_solution(13172529733277836194)
XLA Ops:
  0.6 0.0 copy-start.4
  0.6 4.9 %collective-permute-start = (bf16[128,2048]{1,0:T(8,128)(2,1)}, bf16[128,2048]{1,0:T(8,128)(2,1)S(1)}, u32[]{:S(2)}, u32[]{:S(2)}) collective-permute-start(bf16[128,2048]{1,0:T(8,128)(2,1)} %x_ref.7), channel_id=1, source_target_pairs={{0,4},{4,8},{8,12},{12,16},{16,20},{20,24},{24,28},{1,5},{5,9},{9,... | collective-permute-start | bytes 1572872 | tf_op jit(solution)/shard_map/ppermute | solution.py:369
  5.5 0.0 copy-start.5
  5.5 0.9 %copy.12 = bf16[128,7]{1,0:T(8,128)(2,1)S(1)} copy(bf16[128,7]{0,1:T(8,128)(2,1)} %param.7) | data formatting | bytes 3584 | tf_op args[3]
  6.4 0.0 copy-done.5
  6.4 0.0 copy-done.4
  6.4 0.1 pad_add_fusion.ms_ref
  6.5 0.0 copy-start
  6.5 1.0 %copy-done = bf16[128,2048]{1,0:T(8,128)(2,1)S(1)} copy-done((bf16[128,2048]{1,0:T(8,128)(2,1)S(1)}, bf16[128,2048]{1,0:T(8,128)(2,1)}, u32[]{:S(2)}) %copy-start) | copy-done | bytes 524312
  7.6 0.0 copy-start.2
  7.6 1.0 %copy-done.2 = bf16[128,2048]{1,0:T(8,128)(2,1)S(1)} copy-done((bf16[128,2048]{1,0:T(8,128)(2,1)S(1)}, bf16[128,2048]{1,0:T(8,128)(2,1)}, u32[]{:S(2)}) %copy-start.2) | copy-done | bytes 524312
  8.6 0.0 copy-start.1
  8.6 0.0 copy-start.3
  8.6 4.4 %own_block.1 = (bf16[136,1024]{1,0:T(8,128)(2,1)S(1)}, bf16[136,512]{1,0:T(8,128)(2,1)S(1)}, bf16[136,512]{1,0:T(8,128)(2,1)S(1)}, bf16[128,2048]{1,0:T(8,128)(2...) custom-call(bf16[128,256]{1,0:T(8,128)(2,1)S(1)} %pad_add_fusion.ms_, ...), custom_call_target="tpu_custom_call" | custom-call | flops 1 | bytes 1 | tf_op jit(solution)/shard_map/own_block/pallas_call | solution.py:397
  13.0 1.3 %collective-permute-start.3 = (bf16[136,1024]{1,0:T(8,128)(2,1)S(1)}, bf16[136,1024]{1,0:T(8,128)(2,1)S(1)}, u32[]{:S(2)}, u32[]{:S(2)}) collective-permute-start(bf16[136,1024]{1,0:T(8,128)(2,1)S(1)} %get-tuple-element.35), channel_id=1, source_target_pairs={{4,0},{8,4},{12,8},{16,12},{20,16},{24,20},{28,24},{5,1},{9,5},{13... | collective-permute-start | bytes 835592 | tf_op jit(solution)/shard_map/ppermute | solution.py:369
  14.3 2.6 %collective-permute-done.prev_ref = bf16[128,2048]{1,0:T(8,128)(2,1)S(1)} collective-permute-done((bf16[128,2048]{1,0:T(8,128)(2,1)}, bf16[128,2048]{1,0:T(8,128)(2,1)S(1)}, u32[]{:S(2)}, u32[]{:S(2)}) %collective-permute-start) | collective-permute-done | bytes 524320 | tf_op jit(solution)/shard_map/ppermute | solution.py:369
  17.0 0.0 copy-done.1
  17.0 0.0 copy-done.3
  17.0 3.7 %halo_sums.1 = (bf16[144,2048]{1,0:T(8,128)(2,1)S(1)}, f32[136,128]{1,0:T(8,128)S(1)}, bf16[136,512]{1,0:T(8,128)(2,1)S(1)}) custom-call(bf16[2048,256]{1,0:T(8,128)(2,1)S(1)} %get-tuple-element.23.table_ref, f32[8,2048]{1,0:T(8,128)S(1)} %get-tuple-element.24.wide_ref, ...), custom_call_target="tpu_custom_call", output_to_operand_aliasing={{2}: (8, {})} | custom-call | flops 1 | bytes 1 | tf_op jit(solution)/shard_map/halo_sums/pallas_call | solution.py:422
  20.7 2.4 %collective-permute-start.1 = (f32[136,128]{1,0:T(8,128)S(1)}, f32[136,128]{1,0:T(8,128)S(1)}, u32[]{:S(2)}, u32[]{:S(2)}) collective-permute-start(f32[136,128]{1,0:T(8,128)S(1)} %get-tuple-element.29.own_ref), channel_id=1, source_target_pairs={{0,4},{4,0},{8,12},{12,8},{16,20},{20,16},{24,28},{28,24},{1,5},{5... | collective-permute-start | bytes 208904 | tf_op jit(solution)/shard_map/ppermute | solution.py:369
  23.1 1.3 %collective-permute-start.5 = (bf16[136,512]{1,0:T(8,128)(2,1)S(1)}, bf16[136,512]{1,0:T(8,128)(2,1)S(1)}, u32[]{:S(2)}, u32[]{:S(2)}) collective-permute-start(bf16[136,512]{1,0:T(8,128)(2,1)S(1)} %get-tuple-element.37), channel_id=1, source_target_pairs={{4,0},{8,4},{12,8},{16,12},{20,16},{24,20},{28,24},{5,1},{9,5},{13... | collective-permute-start | bytes 417800 | tf_op jit(solution)/shard_map/ppermute | solution.py:369
  24.4 1.0 %collective-permute-done.1.other_ref = f32[136,128]{1,0:T(8,128)S(1)} collective-permute-done((f32[136,128]{1,0:T(8,128)S(1)}, f32[136,128]{1,0:T(8,128)S(1)}, u32[]{:S(2)}, u32[]{:S(2)}) %collective-permute-start.1) | collective-permute-done | bytes 69664 | tf_op jit(solution)/shard_map/ppermute | solution.py:369
  25.4 3.8 %collective-permute-start.2 = (f32[136,128]{1,0:T(8,128)S(1)}, f32[136,128]{1,0:T(8,128)S(1)}, u32[]{:S(2)}, u32[]{:S(2)}) collective-permute-start(f32[136,128]{1,0:T(8,128)S(1)} %get-tuple-element.31.own_ref), channel_id=1, source_target_pairs={{0,8},{4,12},{8,0},{12,4},{16,24},{20,28},{24,16},{28,20},{1,9},{5... | collective-permute-start | bytes 208904 | tf_op jit(solution)/shard_map/ppermute | solution.py:369
  29.3 1.3 %collective-permute-start.6 = (bf16[136,512]{1,0:T(8,128)(2,1)S(1)}, bf16[136,512]{1,0:T(8,128)(2,1)S(1)}, u32[]{:S(2)}, u32[]{:S(2)}) collective-permute-start(bf16[136,512]{1,0:T(8,128)(2,1)S(1)} %get-tuple-element.38), channel_id=1, source_target_pairs={{4,0},{8,4},{12,8},{16,12},{20,16},{24,20},{28,24},{5,1},{9,5},{13... | collective-permute-start | bytes 417800 | tf_op jit(solution)/shard_map/ppermute | solution.py:369
  30.5 0.0 collective-permute-done.3.rest_0_
  30.6 1.9 %input_grad.2.rest_0_ = bf16[128,2048]{1,0:T(8,128)(2,1)} custom-call(bf16[2048,256]{1,0:T(8,128)(2,1)S(1)} %get-tuple-element.23.table_ref, bf16[2048,256]{1,0:T(8,128)(2,1)S(1)} %get-tuple-element.32.back_ref, f32[8,2048]{1,0:T(8,128)S(1)} %get-tuple-element.24.wide_ref, bf16[128,2048]{1,0:T(8,128)(2,1)S(1)} %copy-done.1, ...), custom_call_target="tpu_custom_call" | custom-call | flops 1 | bytes 1 | tf_op jit(solution)/shard_map/input_grad/pallas_call | solution.py:450
  32.4 0.0 collective-permute-done.2.other_ref
  32.4 3.3 %collective-permute-start.4 = (f32[136,128]{1,0:T(8,128)S(1)}, f32[136,128]{1,0:T(8,128)S(1)}, u32[]{:S(2)}, u32[]{:S(2)}) collective-permute-start(f32[136,128]{1,0:T(8,128)S(1)} %get-tuple-element.36.own_ref), channel_id=1, source_target_pairs={{0,16},{4,20},{8,24},{12,28},{16,0},{20,4},{24,8},{28,12},{1,17},{... | collective-permute-start | bytes 208904 | tf_op jit(solution)/shard_map/ppermute | solution.py:369
  35.7 0.0 collective-permute-done.5.rest_0_
  35.7 0.5 %collective-permute-done.6.rest_1_ = bf16[136,512]{1,0:T(8,128)(2,1)S(1)} collective-permute-done((bf16[136,512]{1,0:T(8,128)(2,1)S(1)}, bf16[136,512]{1,0:T(8,128)(2,1)S(1)}, u32[]{:S(2)}, u32[]{:S(2)}) %collective-permute-start.6) | collective-permute-done | bytes 139296 | tf_op jit(solution)/shard_map/ppermute | solution.py:369
  36.2 1.8 %input_grad.3.held_ref = bf16[128,2048]{1,0:T(8,128)(2,1)} custom-call(bf16[2048,256]{1,0:T(8,128)(2,1)S(1)} %get-tuple-element.23.table_ref, bf16[2048,256]{1,0:T(8,128)(2,1)S(1)} %get-tuple-element.32.back_ref, f32[8,2048]{1,0:T(8,128)S(1)} %get-tuple-element.24.wide_ref, bf16[128,2048]{1,0:T(8,128)(2,1)S(1)} %copy-done.1, ...), custom_call_target="tpu_custom_call", output_to_operand_aliasing={{}: (8, {})} | custom-call | flops 1 | bytes 1 | tf_op jit(solution)/shard_map/input_grad/pallas_call | solution.py:450
  38.0 0.2 collective-permute-done.4.other_ref
  38.3 0.6 %finish_sums.1 = (f32[128,128]{1,0:T(8,128)}, f32[7,128]{1,0:T(8,128)}, bf16[128,2048]{1,0:T(8,128)(2,1)}) custom-call(f32[136,128]{1,0:T(8,128)S(1)} %get-tuple-element.36.own_ref, f32[136,128]{1,0:T(8,128)S(1)} %collective-permute-done.4.other_ref, bf16[128,2048]{1,0:T(8,128)(2,1)} %input_grad.3.held_ref), custom_call_target="tpu_custom_call", output_to_operand_aliasing={{2}: (2, {})} | custom-call | flops 1 | bytes 16777216 | tf_op jit(solution)/shard_map/finish_sums/pallas_call | solution.py:347
  (3 shorter events, 0.0 us)
Async XLA Ops:
  0.6 5.8 %copy-start.4 = (bf16[128,128]{1,0:T(8,128)(2,1)S(1)}, bf16[128,128]{1,0:T(8,128)(2,1)}, u32[]{:S(2)}) copy-start(bf16[128,128]{1,0:T(8,128)(2,1)} %param.6) | copy-start | bytes 98308
  0.6 16.3 %collective-permute-start = (bf16[128,2048]{1,0:T(8,128)(2,1)}, bf16[128,2048]{1,0:T(8,128)(2,1)S(1)}, u32[]{:S(2)}, u32[]{:S(2)}) collective-permute-start(bf16[128,2048]{1,0:T(8,128)(2,1)} %x_ref.7), channel_id=1, source_target_pairs={{0,4},{4,8},{8,12},{12,16},{16,20},{20,24},{24,28},{1,5},{5,9},{9,... | collective-permute-start | bytes 1572872 | tf_op jit(solution)/shard_map/ppermute | solution.py:369
  5.5 0.9 %copy-start.5 = (bf16[128,7]{0,1:T(8,128)(2,1)S(1)}, bf16[128,7]{0,1:T(8,128)(2,1)}, u32[]{:S(2)}) copy-start(bf16[128,7]{0,1:T(8,128)(2,1)} %param.7) | copy-start | bytes 5380
  6.5 1.0 %copy-start = (bf16[128,2048]{1,0:T(8,128)(2,1)S(1)}, bf16[128,2048]{1,0:T(8,128)(2,1)}, u32[]{:S(2)}) copy-start(bf16[128,2048]{1,0:T(8,128)(2,1)} %x_ref.7) | copy-start | bytes 1572868
  7.6 1.0 %copy-start.2 = (bf16[128,2048]{1,0:T(8,128)(2,1)S(1)}, bf16[128,2048]{1,0:T(8,128)(2,1)}, u32[]{:S(2)}) copy-start(bf16[128,2048]{1,0:T(8,128)(2,1)} %u_ref.3) | copy-start | bytes 1572868
  8.6 8.4 %copy-start.1 = (bf16[128,2048]{1,0:T(8,128)(2,1)S(1)}, bf16[128,2048]{1,0:T(8,128)(2,1)}, u32[]{:S(2)}) copy-start(bf16[128,2048]{1,0:T(8,128)(2,1)} %x_ref.7) | copy-start | bytes 1572868
  8.6 8.4 %copy-start.3 = (bf16[128,2048]{1,0:T(8,128)(2,1)S(1)}, bf16[128,2048]{1,0:T(8,128)(2,1)}, u32[]{:S(2)}) copy-start(bf16[128,2048]{1,0:T(8,128)(2,1)} %u_ref.3) | copy-start | bytes 1572868
  13.0 17.5 %collective-permute-start.3 = (bf16[136,1024]{1,0:T(8,128)(2,1)S(1)}, bf16[136,1024]{1,0:T(8,128)(2,1)S(1)}, u32[]{:S(2)}, u32[]{:S(2)}) collective-permute-start(bf16[136,1024]{1,0:T(8,128)(2,1)S(1)} %get-tuple-element.35), channel_id=1, source_target_pairs={{4,0},{8,4},{12,8},{16,12},{20,16},{24,20},{28,24},{5,1},{9,5},{13... | collective-permute-start | bytes 835592 | tf_op jit(solution)/shard_map/ppermute | solution.py:369
  20.7 4.7 %collective-permute-start.1 = (f32[136,128]{1,0:T(8,128)S(1)}, f32[136,128]{1,0:T(8,128)S(1)}, u32[]{:S(2)}, u32[]{:S(2)}) collective-permute-start(f32[136,128]{1,0:T(8,128)S(1)} %get-tuple-element.29.own_ref), channel_id=1, source_target_pairs={{0,4},{4,0},{8,12},{12,8},{16,20},{20,16},{24,28},{28,24},{1,5},{5... | collective-permute-start | bytes 208904 | tf_op jit(solution)/shard_map/ppermute | solution.py:369
  23.1 12.6 %collective-permute-start.5 = (bf16[136,512]{1,0:T(8,128)(2,1)S(1)}, bf16[136,512]{1,0:T(8,128)(2,1)S(1)}, u32[]{:S(2)}, u32[]{:S(2)}) collective-permute-start(bf16[136,512]{1,0:T(8,128)(2,1)S(1)} %get-tuple-element.37), channel_id=1, source_target_pairs={{4,0},{8,4},{12,8},{16,12},{20,16},{24,20},{28,24},{5,1},{9,5},{13... | collective-permute-start | bytes 417800 | tf_op jit(solution)/shard_map/ppermute | solution.py:369
  25.4 7.0 %collective-permute-start.2 = (f32[136,128]{1,0:T(8,128)S(1)}, f32[136,128]{1,0:T(8,128)S(1)}, u32[]{:S(2)}, u32[]{:S(2)}) collective-permute-start(f32[136,128]{1,0:T(8,128)S(1)} %get-tuple-element.31.own_ref), channel_id=1, source_target_pairs={{0,8},{4,12},{8,0},{12,4},{16,24},{20,28},{24,16},{28,20},{1,9},{5... | collective-permute-start | bytes 208904 | tf_op jit(solution)/shard_map/ppermute | solution.py:369
  29.3 6.9 %collective-permute-start.6 = (bf16[136,512]{1,0:T(8,128)(2,1)S(1)}, bf16[136,512]{1,0:T(8,128)(2,1)S(1)}, u32[]{:S(2)}, u32[]{:S(2)}) collective-permute-start(bf16[136,512]{1,0:T(8,128)(2,1)S(1)} %get-tuple-element.38), channel_id=1, source_target_pairs={{4,0},{8,4},{12,8},{16,12},{20,16},{24,20},{28,24},{5,1},{9,5},{13... | collective-permute-start | bytes 417800 | tf_op jit(solution)/shard_map/ppermute | solution.py:369
  32.4 5.8 %collective-permute-start.4 = (f32[136,128]{1,0:T(8,128)S(1)}, f32[136,128]{1,0:T(8,128)S(1)}, u32[]{:S(2)}, u32[]{:S(2)}) collective-permute-start(f32[136,128]{1,0:T(8,128)S(1)} %get-tuple-element.36.own_ref), channel_id=1, source_target_pairs={{0,16},{4,20},{8,24},{12,28},{16,0},{20,4},{24,8},{28,12},{1,17},{... | collective-permute-start | bytes 208904 | tf_op jit(solution)/shard_map/ppermute | solution.py:369

commit v7 on v6

--- a/solution.py
+++ b/solution.py
@@ -475,7 +475,7 @@
         if stage + 1 < len(pieces):
             following.append(permuted(sends[stage + 1], backward))
         last = stage == stages - 1
-        if len(pieces) > 1 and stage == 1 and not last:
+        if len(pieces) > 1 and stage == 0 and not last:
             gradient = input_grad([0], None)
         if last:
             break

time: 39.3 us -> 40 us (1.018)
  waiting for transfers between devices: 4.32 us -> 5.27 us
    ppermute x7, waiting for transfers between devices: 4.32 us -> 5.27 us  [permuted(): return lax.ppermute(block, 'ctx', pairs)]
where the time goes in v7:
time: 40 us; the launch traced here: 39.6 us
  starting transfers between devices  18.1 us (45%)
  Pallas kernels  12.5 us (31%)
  waiting for transfers between devices  5.27 us (13%)
  local copies, waits for them, and re-layouts  2.97 us (7%)
  between operations  0.76 us (2%)
    ppermute x7, starting transfers between devices, permuted(): return lax.ppermute(block, 'ctx', pairs)  18.1 us
    ppermute x7, waiting for transfers between devices, permuted(): return lax.ppermute(block, 'ctx', pairs)  5.27 us
    pallas_call x1, Pallas kernels, local(): pl.pallas_call(functools.partial(own_kernel, taps, pieces, min(width, 8 *...  4.42 us
    pallas_call x2, Pallas kernels, input_grad(): pl.pallas_call(functools.partial(back_kernel, taps, mine), in_specs=in_sp...  3.7 us
    pallas_call x1, Pallas kernels, local(): pl.pallas_call(functools.partial(halo_kernel, taps, factor), in_specs=[re...  3.7 us
    unnamed x13, local copies, waits for them, and re-layouts  2.97 us
  transfers between devices with their start and end apart: 7, of which 4 were waited for; matrix products, arithmetic and copies ran while one was open for 2% of the time, Pallas kernels for 30%

profile of v7, /device:TPU:0, one launch (start us, length us, event | category | flops | bytes accessed | tf_op | source)
XLA Modules:
  0.0 39.6 jit_solution(4371870040495207726)
XLA Ops:
  0.6 0.0 copy-start.4
  0.6 4.9 %collective-permute-start = (bf16[128,2048]{1,0:T(8,128)(2,1)}, bf16[128,2048]{1,0:T(8,128)(2,1)S(1)}, u32[]{:S(2)}, u32[]{:S(2)}) collective-permute-start(bf16[128,2048]{1,0:T(8,128)(2,1)} %x_ref.7), channel_id=1, source_target_pairs={{0,4},{4,8},{8,12},{12,16},{16,20},{20,24},{24,28},{1,5},{5,9},{9,... | collective-permute-start | bytes 1572872 | tf_op jit(solution)/shard_map/ppermute | solution.py:369
  5.5 0.0 copy-start.5
  5.5 0.9 %copy.13 = bf16[128,7]{1,0:T(8,128)(2,1)S(1)} copy(bf16[128,7]{0,1:T(8,128)(2,1)} %param.7) | data formatting | bytes 3584 | tf_op args[3]
  6.4 0.0 copy-done.5
  6.4 0.0 copy-done.4
  6.4 0.1 pad_add_fusion.ms_ref
  6.5 0.0 copy-start
  6.5 1.0 %copy-done = bf16[128,2048]{1,0:T(8,128)(2,1)S(1)} copy-done((bf16[128,2048]{1,0:T(8,128)(2,1)S(1)}, bf16[128,2048]{1,0:T(8,128)(2,1)}, u32[]{:S(2)}) %copy-start) | copy-done | bytes 524312
  7.6 0.0 copy-start.2
  7.6 1.0 %copy-done.2 = bf16[128,2048]{1,0:T(8,128)(2,1)S(1)} copy-done((bf16[128,2048]{1,0:T(8,128)(2,1)S(1)}, bf16[128,2048]{1,0:T(8,128)(2,1)}, u32[]{:S(2)}) %copy-start.2) | copy-done | bytes 524312
  8.6 0.0 copy-start.1
  8.6 0.0 copy-start.3
  8.6 4.4 %own_block.1 = (bf16[136,1024]{1,0:T(8,128)(2,1)S(1)}, bf16[136,512]{1,0:T(8,128)(2,1)S(1)}, bf16[136,512]{1,0:T(8,128)(2,1)S(1)}, bf16[128,2048]{1,0:T(8,128)(2...) custom-call(bf16[128,256]{1,0:T(8,128)(2,1)S(1)} %pad_add_fusion.ms_, ...), custom_call_target="tpu_custom_call" | custom-call | flops 1 | bytes 1 | tf_op jit(solution)/shard_map/own_block/pallas_call | solution.py:397
  13.0 1.3 %collective-permute-start.2 = (bf16[136,1024]{1,0:T(8,128)(2,1)S(1)}, bf16[136,1024]{1,0:T(8,128)(2,1)S(1)}, u32[]{:S(2)}, u32[]{:S(2)}) collective-permute-start(bf16[136,1024]{1,0:T(8,128)(2,1)S(1)} %get-tuple-element.35), channel_id=1, source_target_pairs={{4,0},{8,4},{12,8},{16,12},{20,16},{24,20},{28,24},{5,1},{9,5},{13... | collective-permute-start | bytes 835592 | tf_op jit(solution)/shard_map/ppermute | solution.py:369
  14.3 2.6 %collective-permute-done.prev_ref = bf16[128,2048]{1,0:T(8,128)(2,1)S(1)} collective-permute-done((bf16[128,2048]{1,0:T(8,128)(2,1)}, bf16[128,2048]{1,0:T(8,128)(2,1)S(1)}, u32[]{:S(2)}, u32[]{:S(2)}) %collective-permute-start) | collective-permute-done | bytes 524320 | tf_op jit(solution)/shard_map/ppermute | solution.py:369
  17.0 0.0 copy-done.1
  17.0 0.0 copy-done.3
  17.0 3.7 %halo_sums.1 = (bf16[144,2048]{1,0:T(8,128)(2,1)S(1)}, f32[136,128]{1,0:T(8,128)S(1)}, bf16[136,512]{1,0:T(8,128)(2,1)S(1)}) custom-call(bf16[2048,256]{1,0:T(8,128)(2,1)S(1)} %get-tuple-element.24.table_ref, f32[8,2048]{1,0:T(8,128)S(1)} %get-tuple-element.25.wide_ref, ...), custom_call_target="tpu_custom_call", output_to_operand_aliasing={{2}: (8, {})} | custom-call | flops 1 | bytes 1 | tf_op jit(solution)/shard_map/halo_sums/pallas_call | solution.py:422
  20.7 2.4 %collective-permute-start.1 = (f32[136,128]{1,0:T(8,128)S(1)}, f32[136,128]{1,0:T(8,128)S(1)}, u32[]{:S(2)}, u32[]{:S(2)}) collective-permute-start(f32[136,128]{1,0:T(8,128)S(1)} %get-tuple-element.30.own_ref), channel_id=1, source_target_pairs={{0,4},{4,0},{8,12},{12,8},{16,20},{20,16},{24,28},{28,24},{1,5},{5... | collective-permute-start | bytes 208904 | tf_op jit(solution)/shard_map/ppermute | solution.py:369
  23.1 1.3 %collective-permute-start.5 = (bf16[136,512]{1,0:T(8,128)(2,1)S(1)}, bf16[136,512]{1,0:T(8,128)(2,1)S(1)}, u32[]{:S(2)}, u32[]{:S(2)}) collective-permute-start(bf16[136,512]{1,0:T(8,128)(2,1)S(1)} %get-tuple-element.39), channel_id=1, source_target_pairs={{4,0},{8,4},{12,8},{16,12},{20,16},{24,20},{28,24},{5,1},{9,5},{13... | collective-permute-start | bytes 417800 | tf_op jit(solution)/shard_map/ppermute | solution.py:369
  24.4 0.0 collective-permute-done.2.rest_0_
  24.4 1.9 %input_grad.2.rest_1_ = bf16[128,2048]{1,0:T(8,128)(2,1)} custom-call(bf16[2048,256]{1,0:T(8,128)(2,1)S(1)} %get-tuple-element.24.table_ref, bf16[2048,256]{1,0:T(8,128)(2,1)S(1)} %get-tuple-element.32.back_ref, f32[8,2048]{1,0:T(8,128)S(1)} %get-tuple-element.25.wide_ref, bf16[128,2048]{1,0:T(8,128)(2,1)S(1)} %copy-done.1, ...), custom_call_target="tpu_custom_call" | custom-call | flops 1 | bytes 1 | tf_op jit(solution)/shard_map/input_grad/pallas_call | solution.py:450
  26.3 0.0 collective-permute-done.1.other_ref
  26.3 2.9 %collective-permute-start.3 = (f32[136,128]{1,0:T(8,128)S(1)}, f32[136,128]{1,0:T(8,128)S(1)}, u32[]{:S(2)}, u32[]{:S(2)}) collective-permute-start(f32[136,128]{1,0:T(8,128)S(1)} %get-tuple-element.36.own_ref), channel_id=1, source_target_pairs={{0,8},{4,12},{8,0},{12,4},{16,24},{20,28},{24,16},{28,20},{1,9},{5... | collective-permute-start | bytes 208904 | tf_op jit(solution)/shard_map/ppermute | solution.py:369
  29.3 1.3 %collective-permute-start.6 = (bf16[136,512]{1,0:T(8,128)(2,1)S(1)}, bf16[136,512]{1,0:T(8,128)(2,1)S(1)}, u32[]{:S(2)}, u32[]{:S(2)}) collective-permute-start(bf16[136,512]{1,0:T(8,128)(2,1)S(1)} %get-tuple-element.40), channel_id=1, source_target_pairs={{4,0},{8,4},{12,8},{16,12},{20,16},{24,20},{28,24},{5,1},{9,5},{13... | collective-permute-start | bytes 417800 | tf_op jit(solution)/shard_map/ppermute | solution.py:369
  30.5 1.0 %collective-permute-done.3.other_ref = f32[136,128]{1,0:T(8,128)S(1)} collective-permute-done((f32[136,128]{1,0:T(8,128)S(1)}, f32[136,128]{1,0:T(8,128)S(1)}, u32[]{:S(2)}, u32[]{:S(2)}) %collective-permute-start.3) | collective-permute-done | bytes 69664 | tf_op jit(solution)/shard_map/ppermute | solution.py:369
  31.6 4.0 %collective-permute-start.4 = (f32[136,128]{1,0:T(8,128)S(1)}, f32[136,128]{1,0:T(8,128)S(1)}, u32[]{:S(2)}, u32[]{:S(2)}) collective-permute-start(f32[136,128]{1,0:T(8,128)S(1)} %get-tuple-element.38.own_ref), channel_id=1, source_target_pairs={{0,16},{4,20},{8,24},{12,28},{16,0},{20,4},{24,8},{28,12},{1,17},{... | collective-permute-start | bytes 208904 | tf_op jit(solution)/shard_map/ppermute | solution.py:369
  35.5 0.0 collective-permute-done.5.rest_0_
  35.5 0.7 %collective-permute-done.6.rest_1_ = bf16[136,512]{1,0:T(8,128)(2,1)S(1)} collective-permute-done((bf16[136,512]{1,0:T(8,128)(2,1)S(1)}, bf16[136,512]{1,0:T(8,128)(2,1)S(1)}, u32[]{:S(2)}, u32[]{:S(2)}) %collective-permute-start.6) | collective-permute-done | bytes 139296 | tf_op jit(solution)/shard_map/ppermute | solution.py:369
  36.2 1.8 %input_grad.3.held_ref = bf16[128,2048]{1,0:T(8,128)(2,1)} custom-call(bf16[2048,256]{1,0:T(8,128)(2,1)S(1)} %get-tuple-element.24.table_ref, bf16[2048,256]{1,0:T(8,128)(2,1)S(1)} %get-tuple-element.32.back_ref, f32[8,2048]{1,0:T(8,128)S(1)} %get-tuple-element.25.wide_ref, bf16[128,2048]{1,0:T(8,128)(2,1)S(1)} %copy-done.1, ...), custom_call_target="tpu_custom_call", output_to_operand_aliasing={{}: (8, {})} | custom-call | flops 1 | bytes 1 | tf_op jit(solution)/shard_map/input_grad/pallas_call | solution.py:450
  38.0 1.0 %collective-permute-done.4.other_ref = f32[136,128]{1,0:T(8,128)S(1)} collective-permute-done((f32[136,128]{1,0:T(8,128)S(1)}, f32[136,128]{1,0:T(8,128)S(1)}, u32[]{:S(2)}, u32[]{:S(2)}) %collective-permute-start.4) | collective-permute-done | bytes 69664 | tf_op jit(solution)/shard_map/ppermute | solution.py:369
  39.0 0.6 %finish_sums.1 = (f32[128,128]{1,0:T(8,128)}, f32[7,128]{1,0:T(8,128)}, bf16[128,2048]{1,0:T(8,128)(2,1)}) custom-call(f32[136,128]{1,0:T(8,128)S(1)} %get-tuple-element.38.own_ref, f32[136,128]{1,0:T(8,128)S(1)} %collective-permute-done.4.other_ref, bf16[128,2048]{1,0:T(8,128)(2,1)} %input_grad.3.held_ref), custom_call_target="tpu_custom_call", output_to_operand_aliasing={{2}: (2, {})} | custom-call | flops 1 | bytes 16777216 | tf_op jit(solution)/shard_map/finish_sums/pallas_call | solution.py:347
  (3 shorter events, 0.0 us)
Async XLA Ops:
  0.6 5.8 %copy-start.4 = (bf16[128,128]{1,0:T(8,128)(2,1)S(1)}, bf16[128,128]{1,0:T(8,128)(2,1)}, u32[]{:S(2)}) copy-start(bf16[128,128]{1,0:T(8,128)(2,1)} %param.6) | copy-start | bytes 98308
  0.6 16.3 %collective-permute-start = (bf16[128,2048]{1,0:T(8,128)(2,1)}, bf16[128,2048]{1,0:T(8,128)(2,1)S(1)}, u32[]{:S(2)}, u32[]{:S(2)}) collective-permute-start(bf16[128,2048]{1,0:T(8,128)(2,1)} %x_ref.7), channel_id=1, source_target_pairs={{0,4},{4,8},{8,12},{12,16},{16,20},{20,24},{24,28},{1,5},{5,9},{9,... | collective-permute-start | bytes 1572872 | tf_op jit(solution)/shard_map/ppermute | solution.py:369
  5.5 0.9 %copy-start.5 = (bf16[128,7]{0,1:T(8,128)(2,1)S(1)}, bf16[128,7]{0,1:T(8,128)(2,1)}, u32[]{:S(2)}) copy-start(bf16[128,7]{0,1:T(8,128)(2,1)} %param.7) | copy-start | bytes 5380
  6.5 1.0 %copy-start = (bf16[128,2048]{1,0:T(8,128)(2,1)S(1)}, bf16[128,2048]{1,0:T(8,128)(2,1)}, u32[]{:S(2)}) copy-start(bf16[128,2048]{1,0:T(8,128)(2,1)} %x_ref.7) | copy-start | bytes 1572868
  7.6 1.0 %copy-start.2 = (bf16[128,2048]{1,0:T(8,128)(2,1)S(1)}, bf16[128,2048]{1,0:T(8,128)(2,1)}, u32[]{:S(2)}) copy-start(bf16[128,2048]{1,0:T(8,128)(2,1)} %u_ref.3) | copy-start | bytes 1572868
  8.6 8.4 %copy-start.1 = (bf16[128,2048]{1,0:T(8,128)(2,1)S(1)}, bf16[128,2048]{1,0:T(8,128)(2,1)}, u32[]{:S(2)}) copy-start(bf16[128,2048]{1,0:T(8,128)(2,1)} %x_ref.7) | copy-start | bytes 1572868
  8.6 8.4 %copy-start.3 = (bf16[128,2048]{1,0:T(8,128)(2,1)S(1)}, bf16[128,2048]{1,0:T(8,128)(2,1)}, u32[]{:S(2)}) copy-start(bf16[128,2048]{1,0:T(8,128)(2,1)} %u_ref.3) | copy-start | bytes 1572868
  13.0 11.4 %collective-permute-start.2 = (bf16[136,1024]{1,0:T(8,128)(2,1)S(1)}, bf16[136,1024]{1,0:T(8,128)(2,1)S(1)}, u32[]{:S(2)}, u32[]{:S(2)}) collective-permute-start(bf16[136,1024]{1,0:T(8,128)(2,1)S(1)} %get-tuple-element.35), channel_id=1, source_target_pairs={{4,0},{8,4},{12,8},{16,12},{20,16},{24,20},{28,24},{5,1},{9,5},{13... | collective-permute-start | bytes 835592 | tf_op jit(solution)/shard_map/ppermute | solution.py:369
  20.7 5.6 %collective-permute-start.1 = (f32[136,128]{1,0:T(8,128)S(1)}, f32[136,128]{1,0:T(8,128)S(1)}, u32[]{:S(2)}, u32[]{:S(2)}) collective-permute-start(f32[136,128]{1,0:T(8,128)S(1)} %get-tuple-element.30.own_ref), channel_id=1, source_target_pairs={{0,4},{4,0},{8,12},{12,8},{16,20},{20,16},{24,28},{28,24},{1,5},{5... | collective-permute-start | bytes 208904 | tf_op jit(solution)/shard_map/ppermute | solution.py:369
  23.1 12.4 %collective-permute-start.5 = (bf16[136,512]{1,0:T(8,128)(2,1)S(1)}, bf16[136,512]{1,0:T(8,128)(2,1)S(1)}, u32[]{:S(2)}, u32[]{:S(2)}) collective-permute-start(bf16[136,512]{1,0:T(8,128)(2,1)S(1)} %get-tuple-element.39), channel_id=1, source_target_pairs={{4,0},{8,4},{12,8},{16,12},{20,16},{24,20},{28,24},{5,1},{9,5},{13... | collective-permute-start | bytes 417800 | tf_op jit(solution)/shard_map/ppermute | solution.py:369
  26.3 5.2 %collective-permute-start.3 = (f32[136,128]{1,0:T(8,128)S(1)}, f32[136,128]{1,0:T(8,128)S(1)}, u32[]{:S(2)}, u32[]{:S(2)}) collective-permute-start(f32[136,128]{1,0:T(8,128)S(1)} %get-tuple-element.36.own_ref), channel_id=1, source_target_pairs={{0,8},{4,12},{8,0},{12,4},{16,24},{20,28},{24,16},{28,20},{1,9},{5... | collective-permute-start | bytes 208904 | tf_op jit(solution)/shard_map/ppermute | solution.py:369
  29.3 6.9 %collective-permute-start.6 = (bf16[136,512]{1,0:T(8,128)(2,1)S(1)}, bf16[136,512]{1,0:T(8,128)(2,1)S(1)}, u32[]{:S(2)}, u32[]{:S(2)}) collective-permute-start(bf16[136,512]{1,0:T(8,128)(2,1)S(1)} %get-tuple-element.40), channel_id=1, source_target_pairs={{4,0},{8,4},{12,8},{16,12},{20,16},{24,20},{28,24},{5,1},{9,5},{13... | collective-permute-start | bytes 417800 | tf_op jit(solution)/shard_map/ppermute | solution.py:369
  31.6 7.5 %collective-permute-start.4 = (f32[136,128]{1,0:T(8,128)S(1)}, f32[136,128]{1,0:T(8,128)S(1)}, u32[]{:S(2)}, u32[]{:S(2)}) collective-permute-start(f32[136,128]{1,0:T(8,128)S(1)} %get-tuple-element.38.own_ref), channel_id=1, source_target_pairs={{0,16},{4,20},{8,24},{12,28},{16,0},{20,4},{24,8},{28,12},{1,17},{... | collective-permute-start | bytes 208904 | tf_op jit(solution)/shard_map/ppermute | solution.py:369
